TPU v7x, 512 devices: a whole 4x8x8 slice. The times are simulated.
512 devices in a mesh: dp: 32 (over x, z_lo, core), tensor: 16 (over z_hi, y).
Axes of the slice: x: 4, y: 8, z: 8 (z_hi: 2, z_lo: 4; z = z_hi * 4 + z_lo), core: 2. Of those that a mesh axis runs over, the one named last changes fastest.
Arguments:
- x_inner: bfloat16 [32, 256, 16384], P('dp', None, 'tensor'), may hold values from -6 to 6
- proj_dt: bfloat16 [32, 256, 512], P('dp', 'tensor'), may hold values from -6 to 6
- proj_bc: bfloat16 [32, 256, 32], P('dp', 'tensor'), may hold values from -6 to 6
- grad_y: bfloat16 [32, 256, 16384], P('dp', None, 'tensor'), may hold values from -6 to 6
- w_xdt: bfloat16 [512, 16384], P(None, 'tensor'), may hold values from -0.046875 to 0.046875
- w_xbc: bfloat16 [32, 16384], P(None, 'tensor'), may hold values from -0.046875 to 0.046875
- w_dt: bfloat16 [512, 16384], P(None, 'tensor'), may hold values from -0.25 to 0.25
- dt_bias: float32 [16384], P('tensor'), may hold values from -6 to -2.5
- a_log: float32 [16, 16384], P(None, 'tensor'), may hold values from -0.7 to 2.8
- d_skip: float32 [16384], P('tensor'), may hold values from 0.5 to 1.5
- dt_gain: float32 [512], replicated, may hold values from 0.25 to 1.75
- bc_gain: float32 [32], replicated, may hold values from 0.25 to 1.75
Outputs:
- grad_x: bfloat16 [32, 256, 16384], P('dp', None, 'tensor')
- grad_w_xdt: float32 [512, 16384], P('dp', 'tensor')
- grad_w_dt: float32 [512, 16384], P('dp', 'tensor')
- grad_w_xbc: float32 [32, 16384], P(None, 'tensor')
- grad_a_log: float32 [16, 16384], P(None, 'tensor')
- grad_dt_bias: float32 [16384], P('tensor')
- grad_d_skip: float32 [16384], P('tensor')
- grad_dt_gain: float32 [512], replicated
- grad_bc_gain: float32 [32], replicated
All inputs are finite; a program needn't handle non-finite values.
Results may differ from a plain program's by a relative error of at most 0.0059.
Values may be sent and summed in bfloat16 or wider, within the bound.
No kernel may reach another device: no remote copies, remote signals or barrier semaphores. Data moves between devices by JAX's collectives and lax.ppermute only.
A program may use at most 128 MiB of HBM per device.

v0:
```python
import math

import jax
import jax.numpy as jnp
from jax import lax
from jax.sharding import PartitionSpec as P

norm_eps = 1e-06
state_floor = 0.25
contract_rows = (((0,), (0,)), ((), ()))
contract_cols = (((1,), (1,)), ((), ()))


def unit_rows(dt_part, bc_part):
    dt_square = jnp.mean(dt_part * dt_part, axis=-1, keepdims=True)
    dt_unit = dt_part * lax.rsqrt(dt_square + norm_eps)
    split_at = bc_part.shape[-1] // 2
    b_part = bc_part[..., :split_at]
    c_part = bc_part[..., split_at:]
    b_square = jnp.mean(b_part * b_part, axis=-1, keepdims=True)
    c_square = jnp.mean(c_part * c_part, axis=-1, keepdims=True)
    b_unit = b_part * lax.rsqrt(jnp.maximum(b_square, state_floor))
    c_unit = c_part * lax.rsqrt(jnp.maximum(c_square, state_floor))
    return (dt_unit, jnp.concatenate([b_unit, c_unit], axis=-1))


def join_blocks(earlier, later):
    return (earlier[0] * later[0], later[0] * earlier[1] + later[1])


def block_scan(dt_rows, b_rows, c_rows, x_rows, a_mat):
    block_width = 16
    tokens = dt_rows.shape[0]
    blocks = tokens // block_width
    width = dt_rows.shape[1]
    dt_blocks = dt_rows.reshape(blocks, block_width, width)
    x_blocks = x_rows.reshape(blocks, block_width, width)
    b_blocks = b_rows.reshape(blocks, block_width, b_rows.shape[1])
    c_blocks = c_rows.reshape(blocks, block_width, c_rows.shape[1])
    sources = []
    decays = []
    for offset in range(block_width):
        dt_now = dt_blocks[:, offset]
        decays.append(jnp.exp(dt_now[:, None, :] * a_mat[None]))
        sources.append((dt_now * x_blocks[:, offset])[:, None, :] * b_blocks[:, offset][:, :, None])
    end_state = jnp.zeros((blocks,) + a_mat.shape, jnp.float32)
    for offset in range(block_width):
        end_state = decays[offset] * end_state + sources[offset]
    total_decay = jnp.exp(jnp.sum(dt_blocks, axis=1)[:, None, :] * a_mat[None])
    through_decay, through_state = lax.associative_scan(join_blocks, (total_decay, end_state))
    carry_state = jnp.concatenate(
        [jnp.zeros((1,) + a_mat.shape, jnp.float32), through_state[:-1]], axis=0
    )
    results = []
    for offset in range(block_width):
        carry_state = decays[offset] * carry_state + sources[offset]
        results.append(jnp.sum(c_blocks[:, offset][:, :, None] * carry_state, axis=1))
    return jnp.stack(results, axis=1).reshape(tokens, width)


def body(
    x_inner, proj_dt, proj_bc, grad_y, w_xdt, w_xbc, w_dt, dt_bias, a_log, d_skip, dt_gain, bc_gain
):
    x_rows = x_inner[0]
    gy_rows = grad_y[0]
    own_dt = proj_dt[0]
    own_bc = proj_bc[0]
    own_count = own_dt.shape[0]
    tokens = x_rows.shape[0]
    channels = x_rows.shape[1]
    data_count = lax.axis_size("dp")
    grad_scale = 1.0 / math.sqrt(data_count * tokens)
    full_dt, full_bc = (
        lax.all_gather(own_dt, "tensor", axis=0, tiled=True),
        lax.all_gather(own_bc, "tensor", axis=0, tiled=True),
    )
    (dt_unit, bc_unit), full_back = jax.vjp(
        unit_rows, full_dt.astype(jnp.float32), full_bc.astype(jnp.float32)
    )
    dt_low = (dt_unit * dt_gain).astype(jnp.bfloat16)
    bc_normed = bc_unit * bc_gain
    split_at = bc_normed.shape[1] // 2
    pre_act = jnp.dot(dt_low, w_dt, preferred_element_type=jnp.float32) + dt_bias
    dt_rows = jax.nn.softplus(pre_act)
    a_mat = -jnp.exp(a_log)
    x_float = x_rows.astype(jnp.float32)
    gy_float = gy_rows.astype(jnp.float32)
    b_rows = bc_normed[:, :split_at]
    c_rows = bc_normed[:, split_at:]
    group_width = math.gcd(channels, 256)
    group_count = channels // group_width

    def to_groups(matrix):
        return matrix.reshape(matrix.shape[0], group_count, group_width).transpose(1, 0, 2)

    def from_groups(stacked):
        return stacked.transpose(1, 0, 2).reshape(stacked.shape[1], channels)

    def group_grads(items):
        dt_group, x_group, gy_group, a_group = items
        group_out, group_back = jax.vjp(block_scan, dt_group, b_rows, c_rows, x_group, a_group)
        return group_back(gy_group)

    dt_parts, b_parts, c_parts, x_parts, a_parts = lax.map(
        group_grads, (to_groups(dt_rows), to_groups(x_float), to_groups(gy_float), to_groups(a_mat))
    )
    dt_grad = from_groups(dt_parts)
    x_grad = from_groups(x_parts)
    a_grad = from_groups(a_parts)
    b_grad = jnp.sum(b_parts, axis=0)
    c_grad = jnp.sum(c_parts, axis=0)
    pre_float = dt_grad * jax.nn.sigmoid(pre_act)
    pre_grad = pre_float.astype(jnp.bfloat16)
    columns_taken = dt_low
    grad_w_dt = lax.psum_scatter(
        grad_scale
        * lax.dot_general(
            columns_taken, pre_grad, contract_rows, preferred_element_type=jnp.float32
        ),
        "dp",
        scatter_dimension=0,
        tiled=True,
    )
    dt_normed_part = lax.dot_general(
        pre_grad, w_dt, contract_cols, preferred_element_type=jnp.float32
    )
    bc_normed_part = jnp.concatenate([b_grad, c_grad], axis=1)
    dt_normed_grad, bc_normed_grad = lax.psum((dt_normed_part, bc_normed_part), "tensor")
    proj_dt_grad, proj_bc_grad = full_back((dt_normed_grad * dt_gain, bc_normed_grad * bc_gain))
    proj_dt_low = proj_dt_grad.astype(jnp.bfloat16)
    proj_bc_low = proj_bc_grad.astype(jnp.bfloat16)
    own_start = lax.axis_index("tensor") * own_count
    owned_dt_grad = lax.dynamic_slice_in_dim(dt_normed_grad, own_start, own_count, 0)
    owned_bc_grad = lax.dynamic_slice_in_dim(bc_normed_grad, own_start, own_count, 0)
    owned_dt_unit = lax.dynamic_slice_in_dim(dt_unit, own_start, own_count, 0)
    owned_bc_unit = lax.dynamic_slice_in_dim(bc_unit, own_start, own_count, 0)
    dt_gain_part = jnp.sum(owned_dt_grad * owned_dt_unit, axis=0)
    bc_gain_part = jnp.sum(owned_bc_grad * owned_bc_unit, axis=0)
    summed = x_grad + d_skip * gy_float
    summed = summed + jnp.dot(proj_dt_low, w_xdt, preferred_element_type=jnp.float32)
    summed = summed + jnp.dot(proj_bc_low, w_xbc, preferred_element_type=jnp.float32)
    grad_x = summed.astype(jnp.bfloat16)[None]
    columns_taken = proj_dt_low
    grad_w_xdt = lax.psum_scatter(
        grad_scale
        * lax.dot_general(columns_taken, x_rows, contract_rows, preferred_element_type=jnp.float32),
        "dp",
        scatter_dimension=0,
        tiled=True,
    )
    xbc_part = grad_scale * lax.dot_general(
        proj_bc_low, x_rows, contract_rows, preferred_element_type=jnp.float32
    )
    alog_part = grad_scale * a_grad * a_mat
    bias_part = grad_scale * jnp.sum(pre_float, axis=0)
    skip_part = grad_scale * jnp.sum(gy_float * x_float, axis=0)
    grad_w_xbc, grad_a_log, grad_dt_bias, grad_d_skip = lax.psum(
        (xbc_part, alog_part, bias_part, skip_part), "dp"
    )
    grad_dt_gain, grad_bc_gain = lax.psum(
        (grad_scale * dt_gain_part, grad_scale * bc_gain_part), ("dp", "tensor")
    )
    return (
        grad_x,
        grad_w_xdt,
        grad_w_dt,
        grad_w_xbc,
        grad_a_log,
        grad_dt_bias,
        grad_d_skip,
        grad_dt_gain,
        grad_bc_gain,
    )


def solution(mesh):
    return jax.shard_map(
        body,
        mesh=mesh,
        in_specs=(
            P("dp", None, "tensor"),
            P("dp", "tensor", None),
            P("dp", "tensor", None),
            P("dp", None, "tensor"),
            P(None, "tensor"),
            P(None, "tensor"),
            P(None, "tensor"),
            P("tensor"),
            P(None, "tensor"),
            P("tensor"),
            P(),
            P(),
        ),
        out_specs=(
            P("dp", None, "tensor"),
            P("dp", "tensor"),
            P("dp", "tensor"),
            P(None, "tensor"),
            P(None, "tensor"),
            P("tensor"),
            P("tensor"),
            P(),
            P(),
        ),
        check_vma=False,
    )
```

profile of v0, /device:TPU:1, one launch (start us, length us, event | category | flops | bytes accessed | tf_op | source)
XLA Modules:
  0.0 1411.5 jit_solution(16463149494984167069)
XLA Ops:
  7.3 51.5 %all-gather.1 = bf16[1,256,32]{2,1,0:T(8,128)(2,1)S(1)} all-gather(bf16[1,16,32]{2,1,0:T(8,128)(2,1)} %param.16), channel_id=3, replica_groups=mesh['dp'=32,'tensor'=16] {'tensor'}, dimensions={1}, use_global_device_ids=true | all-gather | bytes 17408 | tf_op jit(solution)/shard_map/all_gather | solution.py:75
  60.6 41.2 %all-gather = bf16[1,256,512]{2,1,0:T(8,128)(2,1)S(1)} all-gather(bf16[1,16,512]{2,1,0:T(8,128)(2,1)} %param.15), channel_id=2, replica_groups=mesh['dp'=32,'tensor'=16] {'tensor'}, dimensions={1}, use_global_device_ids=true | all-gather | bytes 278528 | tf_op jit(solution)/shard_map/all_gather | solution.py:74
  114.0 510.7 %while.18 = (s32[]{:T(128)}, f32[4,256,256]{2,1,0:T(8,128)}, f32[4,256,16]{1,2,0:T(8,128)}, f32[4,256,16]{1,2,0:T(8,128)}, f32[4,256,256]{2,1,0:T(8,128)}, /*ind...) while((s32[]{:T(128)}, f32[4,256,256]{2,1,0:T(8,128)}, ...), condition=%wide.region_87.88_spmd, body=%wide.region_3.87_spmd.sunk | while | flops 75317248 | bytes 78499272 | solution.py:104
  178.5 3.3 pad.714
  186.4 2.7 pad.717
  191.0 4.8 pad.723
  196.1 3.1 pad.725
  199.3 2.9 pad.720
  220.7 3.0 multiply_reduce_fusion.114
  306.2 3.3 pad.714
  314.1 2.7 pad.717
  318.7 4.8 pad.723
  323.7 3.1 pad.725
  326.9 2.9 pad.720
  348.4 3.0 multiply_reduce_fusion.114
  433.8 3.3 pad.714
  446.4 4.8 pad.723
  451.4 3.1 pad.725
  454.6 2.9 pad.720
  476.0 3.0 multiply_reduce_fusion.114
  561.5 3.3 pad.714
  574.1 4.8 pad.723
  579.1 3.1 pad.725
  582.3 2.9 pad.720
  603.7 3.0 multiply_reduce_fusion.114
  628.2 80.2 %psum.57 = f32[256,32]{1,0:T(8,128)S(1)} all-reduce(f32[256,32]{1,0:T(8,128)S(1)} %copy.327), channel_id=1, replica_groups=mesh['dp'=32,'tensor'=16] {'tensor'}, use_global_device_ids=true, to_apply=%region_92.93 | all-reduce | flops 8192 | bytes 65536 | tf_op jit(solution)/shard_map/psum | solution.py:128
  712.9 109.6 %all-reduce.109.cloned.1.call-done = f32[256,512]{1,0:T(8,128)} async-done(((f32[256,512]{1,0:T(8,128)}), f32[256,512]{1,0:T(8,128)}) %all-reduce.109.cloned.1.call-update) | async-done | bytes 524304 | tf_op jit(solution)/shard_map/psum | solution.py:128
  830.0 79.5 %all-reduce.104 = (f32[1024]{0:T(1024)}, f32[1024]{0:T(1024)}) all-reduce(f32[1024]{0:T(1024)S(1)} %broadcast_multiply_fusion.2, f32[1024]{0:T(1024)S(1)} %broadcast_multiply_fusion.1), channel_id=1, replica_groups=mesh['dp'=32,'tensor'=16] {'dp'}, use_global_device_ids=true, to_apply=%region_100.101 | all-reduce | flops 2048 | bytes 16384 | tf_op jit(solution)/shard_map/psum | solution.py:157
  910.3 95.5 %all-reduce.103 = (f32[512]{0:T(512)}, f32[32]{0:T(128)}) all-reduce(f32[512]{0:T(512)S(1)} %broadcast_multiply_fusion.3, f32[32]{0:T(128)S(1)} %broadcast_multiply_fusion.4), channel_id=1, replica_groups=mesh['dp'=32,'tensor'=16] {'dp','tensor'}, use_global_device_ids=true, to_apply=%region_104.105 | all-reduce | flops 544 | bytes 4352 | tf_op jit(solution)/shard_map/psum | solution.py:160
  1008.5 93.6 %all-reduce.111.cloned.1.call-done = (f32[32,1024]{1,0:T(8,128)}, f32[16,1024]{1,0:T(8,128)}) async-done(((f32[32,1024]{1,0:T(8,128)}, f32[16,1024]{1,0:T(8,128)}), (f32[32,1024]{1,0:T(8,128)}, f32[16,1024]{1,0:T(8,128)})) %all-reduce.111.cloned.1.call-update) | async-done | bytes 196624 | tf_op jit(solution)/shard_map/psum | solution.py:157
  1102.2 149.6 %reduce-scatter.5.cloned.1.call-done = f32[16,1024]{1,0:T(8,128)} async-done(((f32[512,1024]{1,0:T(8,128)}), f32[16,1024]{1,0:T(8,128)}) %reduce-scatter.5.cloned.1.call-update) | async-done | bytes 65552 | tf_op jit(solution)/shard_map/reduce_scatter | solution.py:115
  1251.8 150.2 %reduce-scatter.3.cloned.1.call-done = f32[16,1024]{1,0:T(8,128)} async-done(((f32[512,1024]{1,0:T(8,128)}), f32[16,1024]{1,0:T(8,128)}) %reduce-scatter.3.cloned.1.call-update) | async-done | bytes 65552 | tf_op jit(solution)/shard_map/reduce_scatter | solution.py:144
  (2647 shorter events, 458.1 us)
Async XLA Ops:
  7.2 103.9 %copy-start = (bf16[512,1024]{1,0:T(8,128)(2,1)S(1)}, bf16[512,1024]{1,0:T(8,128)(2,1)}, u32[]{:S(2)}) copy-start(bf16[512,1024]{1,0:T(8,128)(2,1)} %param.20) | copy-start | bytes 3145732
  7.2 97.8 %copy-start.34 = (bf16[1,256,1024]{2,1,0:T(8,128)(2,1)S(1)}, bf16[1,256,1024]{2,1,0:T(8,128)(2,1)}, u32[]{:S(2)}) copy-start(bf16[1,256,1024]{2,1,0:T(8,128)(2,1)} %param.14) | copy-start | bytes 1572868
  7.2 815.2 %all-reduce.109.cloned.1.call-start = ((), (), s32[]{:S(2)}) async-start(), calls=%async_computation.2 | async-start | bytes 1048576 | tf_op jit(solution)/shard_map/psum | solution.py:128
  58.8 43.7 %copy-start.9 = (f32[256,32]{1,0:T(8,128)}, f32[256,32]{1,0:T(8,128)S(1)}, u32[]{:S(2)}) copy-start(f32[256,32]{1,0:T(8,128)S(1)} %bitcast_convert_fusion) | copy-start | bytes 98308
  59.1 43.6 %copy-start.246 = (f32[256]{0:T(256)}, f32[256]{0:T(256)S(1)}, u32[]{:S(2)}) copy-start(f32[256]{0:T(256)S(1)} %maximum_rsqrt_fusion.1) | copy-start | bytes 3076
  59.1 43.6 %copy-start.248 = (f32[256]{0:T(256)}, f32[256]{0:T(256)S(1)}, u32[]{:S(2)}) copy-start(f32[256]{0:T(256)S(1)} %maximum_rsqrt_fusion) | copy-start | bytes 3076
  116.9 20.0 %copy-start.138 = (f32[16,1,256]{2,1,0:T(1,128)}, f32[16,1,256]{2,1,0:T(1,128)S(1)}, u32[]{:S(2)}) copy-start(f32[16,1,256]{2,1,0:T(1,128)S(1)} %get-tuple-element.958) | copy-start | bytes 49156 | tf_op jit(solution)/shard_map/while
  116.9 20.0 %copy-start.156 = (f32[16,1,256]{2,1,0:T(1,128)}, f32[16,1,256]{2,1,0:T(1,128)S(1)}, u32[]{:S(2)}) copy-start(f32[16,1,256]{2,1,0:T(1,128)S(1)} %get-tuple-element.943) | copy-start | bytes 49156 | tf_op jit(solution)/shard_map/while
  129.9 38.0 %copy-start.11 = (f32[16,256]{1,0:T(8,128)}, f32[16,256]{1,0:T(8,128)S(1)}, u32[]{:S(2)}) copy-start(f32[16,256]{1,0:T(8,128)S(1)} %get-tuple-element.889) | copy-start | bytes 49156 | tf_op jit(solution)/shard_map/while
  244.6 20.0 %copy-start.138 = (f32[16,1,256]{2,1,0:T(1,128)}, f32[16,1,256]{2,1,0:T(1,128)S(1)}, u32[]{:S(2)}) copy-start(f32[16,1,256]{2,1,0:T(1,128)S(1)} %get-tuple-element.958) | copy-start | bytes 49156 | tf_op jit(solution)/shard_map/while
  244.6 20.0 %copy-start.156 = (f32[16,1,256]{2,1,0:T(1,128)}, f32[16,1,256]{2,1,0:T(1,128)S(1)}, u32[]{:S(2)}) copy-start(f32[16,1,256]{2,1,0:T(1,128)S(1)} %get-tuple-element.943) | copy-start | bytes 49156 | tf_op jit(solution)/shard_map/while
  257.5 38.0 %copy-start.11 = (f32[16,256]{1,0:T(8,128)}, f32[16,256]{1,0:T(8,128)S(1)}, u32[]{:S(2)}) copy-start(f32[16,256]{1,0:T(8,128)S(1)} %get-tuple-element.889) | copy-start | bytes 49156 | tf_op jit(solution)/shard_map/while
  385.2 38.0 %copy-start.11 = (f32[16,256]{1,0:T(8,128)}, f32[16,256]{1,0:T(8,128)S(1)}, u32[]{:S(2)}) copy-start(f32[16,256]{1,0:T(8,128)S(1)} %get-tuple-element.889) | copy-start | bytes 49156 | tf_op jit(solution)/shard_map/while
  512.9 38.0 %copy-start.11 = (f32[16,256]{1,0:T(8,128)}, f32[16,256]{1,0:T(8,128)S(1)}, u32[]{:S(2)}) copy-start(f32[16,256]{1,0:T(8,128)S(1)} %get-tuple-element.889) | copy-start | bytes 49156 | tf_op jit(solution)/shard_map/while
  626.5 81.9 %copy-start.257 = (f32[32]{0:T(128)S(1)}, f32[32]{0:T(128)}, u32[]{:S(2)}) copy-start(f32[32]{0:T(128)} %param.25) | copy-start | bytes 388
  626.6 81.9 %copy-start.10 = (f32[256,32]{1,0:T(8,128)S(1)}, f32[256,32]{1,0:T(8,128)}, u32[]{:S(2)}) copy-start(f32[256,32]{1,0:T(8,128)} %copy-done.9) | copy-start | bytes 98308
  626.6 82.2 %copy-start.253 = (f32[256]{0:T(256)S(1)}, f32[256]{0:T(256)}, u32[]{:S(2)}) copy-start(f32[256]{0:T(256)} %copy-done.252) | copy-start | bytes 3076
  626.6 82.2 %copy-start.255 = (f32[256]{0:T(256)S(1)}, f32[256]{0:T(256)}, u32[]{:S(2)}) copy-start(f32[256]{0:T(256)} %copy-done.254) | copy-start | bytes 3076
  626.6 82.2 %copy-start.247 = (f32[256]{0:T(256)S(1)}, f32[256]{0:T(256)}, u32[]{:S(2)}) copy-start(f32[256]{0:T(256)} %copy-done.246) | copy-start | bytes 3076
  626.6 82.2 %copy-start.249 = (f32[256]{0:T(256)S(1)}, f32[256]{0:T(256)}, u32[]{:S(2)}) copy-start(f32[256]{0:T(256)} %copy-done.248) | copy-start | bytes 3076
  627.9 81.3 %copy-start.231 = (f32[16,1024]{1,0:T(8,128)S(1)}, f32[16,1024]{1,0:T(8,128)}, u32[]{:S(2)}) copy-start(f32[16,1024]{1,0:T(8,128)} %param.22) | copy-start | bytes 196612
  627.9 82.0 %copy-start.35 = (bf16[1,256,1024]{2,1,0:T(8,128)(2,1)S(1)}, bf16[1,256,1024]{2,1,0:T(8,128)(2,1)}, u32[]{:S(2)}) copy-start(bf16[1,256,1024]{2,1,0:T(8,128)(2,1)} %param.14) | copy-start | bytes 1572868
  627.9 82.9 %copy-start.60 = (bf16[1,256,512]{2,1,0:T(8,128)(2,1)S(1)}, bf16[1,256,512]{2,1,0:T(8,128)(2,1)}, u32[]{:S(2)}) copy-start(bf16[1,256,512]{2,1,0:T(8,128)(2,1)} %copy-done.59) | copy-start | bytes 786436
  627.9 82.9 %copy-start.242 = (f32[512]{0:T(512)S(1)}, f32[512]{0:T(512)}, u32[]{:S(2)}) copy-start(f32[512]{0:T(512)} %param.24) | copy-start | bytes 6148
  627.9 82.9 %copy-start.245 = (f32[256]{0:T(256)S(1)}, f32[256]{0:T(256)}, u32[]{:S(2)}) copy-start(f32[256]{0:T(256)} %copy-done.244) | copy-start | bytes 3076
  627.9 474.2 %all-reduce.111.cloned.1.call-start = ((), (), s32[]{:S(2)}) async-start(), calls=%async_computation.5 | async-start | bytes 393216 | tf_op jit(solution)/shard_map/psum | solution.py:157
  710.8 541.0 %reduce-scatter.5.cloned.1.call-start = ((), (), s32[]{:S(2)}) async-start(), calls=%async_computation.4 | async-start | bytes 2162688 | tf_op jit(solution)/shard_map/reduce_scatter | solution.py:115
  712.8 110.9 %copy-start.251 = (f32[256]{0:T(256)S(1)}, f32[256]{0:T(256)}, u32[]{:S(2)}) copy-start(f32[256]{0:T(256)} %copy-done.250) | copy-start | bytes 3076
  712.8 689.2 %reduce-scatter.3.cloned.1.call-start = ((), (), s32[]{:S(2)}) async-start(), calls=%async_computation.3 | async-start | bytes 2162688 | tf_op jit(solution)/shard_map/reduce_scatter | solution.py:144
  827.5 178.2 %copy-start.256 = (f32[1024]{0:T(1024)S(1)}, f32[1024]{0:T(1024)}, u32[]{:S(2)}) copy-start(f32[1024]{0:T(1024)} %param.23) | copy-start | bytes 12292
  830.0 177.5 %copy-start.227 = (bf16[256,32]{1,0:T(8,128)(2,1)S(1)}, bf16[256,32]{1,0:T(8,128)(2,1)}, u32[]{:S(2)}) copy-start(bf16[256,32]{1,0:T(8,128)(2,1)} %copy-done.226) | copy-start | bytes 49156
  830.0 177.5 %copy-start.240 = (bf16[32,1024]{1,0:T(8,128)(2,1)S(1)}, bf16[32,1024]{1,0:T(8,128)(2,1)}, u32[]{:S(2)}) copy-start(bf16[32,1024]{1,0:T(8,128)(2,1)} %param.19) | copy-start | bytes 196612
  (906 other events, 6376.7 us)
Sparse Core Ops, SparseCore 0:
  628.0 194.3 all-reduce.108
  826.3 275.8 all-reduce.110
  1105.5 146.1 reduce-scatter.4
  1255.2 146.6 reduce-scatter.2
where the time goes:
time: 1430 us; the launch traced here: 1410 us
  waiting for transfers between devices  503 us (35%)
  blocking collectives  348 us (24%)
  local copies, waits for them, and re-layouts  296 us (21%)
  other arithmetic  225 us (16%)
  between operations  14.4 us (1%)
    reduce_scatter x1, waiting for transfers between devices, body(): lax.psum_scatter(grad_scale * lax.dot_general(columns_taken, x_rows, cont...  150 us
    reduce_scatter x1, waiting for transfers between devices, body(): lax.psum_scatter(grad_scale * lax.dot_general(columns_taken, pre_grad, co...  150 us
    psum x1, waiting for transfers between devices, body(): lax.psum((dt_normed_part, bc_normed_part), 'tensor')  110 us
    psum x1, blocking collectives, body(): lax.psum((grad_scale * dt_gain_part, grad_scale * bc_gain_part), ('dp', '...  95.5 us
    psum x1, waiting for transfers between devices, body(): lax.psum((xbc_part, alog_part, bias_part, skip_part), 'dp')  93.6 us
    pad x92, local copies, waits for them, and re-layouts, block_scan(): lax.associative_scan(join_blocks, (total_decay, end_state))  93.6 us
    psum x1, blocking collectives, body(): lax.psum((dt_normed_part, bc_normed_part), 'tensor')  80.2 us
    psum x1, blocking collectives, body(): lax.psum((xbc_part, alog_part, bias_part, skip_part), 'dp')  79.5 us
  transfers between devices with their start and end apart: 4, of which 4 were waited for; matrix products, arithmetic and copies ran while one was open for 1% of the time, Pallas kernels for 0%

commit v1 on v0

v1 whole, which is shorter than its diff:
```python
import functools
import math

import jax
import jax.numpy as jnp
from jax import lax
from jax.experimental import pallas as pl
from jax.experimental.pallas import tpu as pltpu
from jax.sharding import PartitionSpec as P

norm_eps = 1e-06
state_floor = 0.25
log2_e = 1.4426950408889634
lane = 128
f32 = jnp.float32
bf16 = jnp.bfloat16
contract_rows = (((0,), (0,)), ((), ()))
contract_cols = (((1,), (1,)), ((), ()))
in_vmem = pl.BlockSpec(memory_space=pltpu.VMEM)


def inverse_norms(proj, rank, state):
    dt_part = proj[:, :rank]
    b_part = proj[:, rank : rank + state]
    c_part = proj[:, rank + state : rank + 2 * state]
    dt_square = jnp.mean(dt_part * dt_part, axis=1, keepdims=True)
    b_square = jnp.mean(b_part * b_part, axis=1, keepdims=True)
    c_square = jnp.mean(c_part * c_part, axis=1, keepdims=True)
    return (
        (dt_part, lax.rsqrt(dt_square + norm_eps)),
        (b_part, lax.rsqrt(jnp.maximum(b_square, state_floor)), b_square),
        (c_part, lax.rsqrt(jnp.maximum(c_square, state_floor)), c_square),
    )


def scan_kernel(
    proj_ref,
    x_ref,
    gy_ref,
    w_ref,
    bias_ref,
    alog_ref,
    skip_ref,
    dt_gain_ref,
    bc_gain_ref,
    normed_ref,
    w_part_ref,
    xg_ref,
    misc_ref,
    dt_s,
    gy_s,
    src_s,
    sig_s,
    a2_s,
    low_s,
    bcb_s,
    u_s,
    b_acc,
    c_acc,
    s1_s,
    s2_s,
    *,
    wide_lanes,
    scale,
):
    tokens, width = x_ref.shape
    state = alog_ref.shape[0]
    rank = w_ref.shape[0]
    dt_norm, b_norm, c_norm = inverse_norms(proj_ref[...].astype(f32), rank, state)
    low_s[...] = (dt_norm[0] * dt_norm[1] * dt_gain_ref[...]).astype(bf16)
    b_rows = b_norm[0] * b_norm[1] * bc_gain_ref[:, :state]
    c_rows = c_norm[0] * c_norm[1] * bc_gain_ref[:, state:]
    bcb_s[:, :state] = jnp.broadcast_to(b_rows[:, :, None], (tokens, state, lane))
    bcb_s[:, state:] = jnp.broadcast_to(c_rows[:, :, None], (tokens, state, lane))
    pre = jnp.dot(low_s[...], w_ref[...], preferred_element_type=f32) + bias_ref[...]
    small = jnp.exp(-jnp.abs(pre))
    dt_rows = jnp.maximum(pre, 0.0) + jnp.log1p(small)
    sig_s[...] = jnp.where(pre >= 0, 1.0, small) / (1.0 + small)
    x_float = x_ref[...].astype(f32)
    gy_float = gy_ref[...].astype(f32)
    dt_s[...] = dt_rows
    gy_s[...] = gy_float
    src_s[...] = dt_rows * x_float
    a_mat = -jnp.exp(alog_ref[...])
    a2_s[...] = a_mat * log2_e
    b_acc[...] = jnp.zeros_like(b_acc)
    c_acc[...] = jnp.zeros_like(c_acc)
    reps = wide_lanes // lane

    def widen(part):
        return jnp.concatenate([part] * reps, axis=1)

    def fold(part):
        total = part[:, :lane]
        for rep in range(1, reps):
            total = total + part[:, rep * lane : (rep + 1) * lane]
        return total

    for group in range(width // wide_lanes):
        cols = slice(group * wide_lanes, (group + 1) * wide_lanes)

        def forward(block, held):
            a2 = a2_s[:, cols]
            for offset in range(8):
                t = block * 8 + offset
                decayed = jnp.exp2(dt_s[pl.ds(t, 1), cols] * a2) * held
                u_s[pl.ds(t, 1), :, cols] = decayed[None]
                c_acc[pl.ds(t, 1)] += fold(decayed * gy_s[pl.ds(t, 1), cols])[None]
                held = decayed + src_s[pl.ds(t, 1), cols] * widen(bcb_s[t, :state])
            return held

        zeros = jnp.zeros((state, wide_lanes), f32)
        lax.fori_loop(0, tokens // 8, forward, zeros)

        def backward(step, carry):
            later, a_total = carry
            block = tokens // 8 - 1 - step
            a2 = a2_s[:, cols]
            for offset in range(7, -1, -1):
                t = block * 8 + offset
                dt_now = dt_s[pl.ds(t, 1), cols]
                adjoint = widen(bcb_s[t, state:]) * gy_s[pl.ds(t, 1), cols] + later
                through = adjoint * u_s[t, :, cols]
                s1_s[pl.ds(t, 1), cols] = jnp.sum(
                    adjoint * widen(bcb_s[t, :state]), axis=0, keepdims=True
                )
                s2_s[pl.ds(t, 1), cols] = jnp.sum(through * a2, axis=0, keepdims=True)
                b_acc[pl.ds(t, 1)] += fold(adjoint * src_s[pl.ds(t, 1), cols])[None]
                a_total = a_total + dt_now * through
                later = jnp.exp2(dt_now * a2) * adjoint
            return later, a_total

        _, a_total = lax.fori_loop(0, tokens // 8, backward, (zeros, zeros))
        misc_ref[:state, cols] = (scale / log2_e) * (a_total * a2_s[:, cols])

    s1 = s1_s[...]
    xg_ref[...] = dt_s[...] * s1 + skip_ref[...] * gy_s[...]
    dt_grad = x_ref[...].astype(f32) * s1 + s2_s[...] * (1.0 / log2_e)
    pre_float = dt_grad * sig_s[...]
    pre_grad = pre_float.astype(bf16)
    misc_ref[state : state + 1, :] = scale * jnp.sum(pre_float, axis=0, keepdims=True)
    misc_ref[state + 1 : state + 2, :] = scale * jnp.sum(
        gy_s[...] * x_ref[...].astype(f32), axis=0, keepdims=True
    )
    normed_ref[:, :rank] = lax.dot_general(
        pre_grad, w_ref[...], contract_cols, preferred_element_type=f32
    ).astype(bf16)
    w_part_ref[...] = (
        scale
        * lax.dot_general(low_s[...], pre_grad, contract_rows, preferred_element_type=f32)
    ).astype(bf16)
    source_sum = jnp.sum(src_s[...] * gy_s[...], axis=1, keepdims=True)
    b_grad = jnp.sum(b_acc[...], axis=2)
    c_grad = jnp.sum(c_acc[...], axis=2) + b_rows * source_sum
    normed_ref[:, rank : rank + state] = b_grad.astype(bf16)
    normed_ref[:, rank + state : rank + 2 * state] = c_grad.astype(bf16)
    normed_ref[:, rank + 2 * state :] = jnp.zeros_like(normed_ref[:, rank + 2 * state :])


def norm_kernel(parts_ref, proj_ref, dt_gain_ref, bc_gain_ref, out_ref, pack_s, *, state):
    rank = dt_gain_ref.shape[1]
    grads = jnp.sum(parts_ref[...].astype(f32), axis=0)
    dt_norm, b_norm, c_norm = inverse_norms(proj_ref[...].astype(f32), rank, state)
    dt_grad = grads[:, :rank]
    dt_unit = dt_norm[0] * dt_norm[1]
    dt_cot = dt_grad * dt_gain_ref[...]
    dt_mean = jnp.mean(dt_cot * dt_unit, axis=1, keepdims=True)
    pack_s[...] = jnp.zeros_like(pack_s)
    pack_s[:, :rank] = dt_norm[1] * (dt_cot - dt_unit * dt_mean)
    gain_rows = []
    dt_gain_part = jnp.sum(dt_grad * dt_unit, axis=0, keepdims=True)
    for piece in range(rank // lane):
        gain_rows.append(dt_gain_part[:, piece * lane : (piece + 1) * lane])
    last = rank + lane
    for index, part in enumerate((b_norm, c_norm)):
        start = rank + index * state
        grad = grads[:, start : start + state]
        unit = part[0] * part[1]
        cot = grad * bc_gain_ref[:, index * state : (index + 1) * state]
        mean = jnp.mean(cot * unit, axis=1, keepdims=True)
        inner = jnp.where(part[2] > state_floor, mean, 0.0)
        inner = jnp.where(part[2] == state_floor, 0.5 * mean, inner)
        pack_s[:, start : start + state] = part[1] * (cot - unit * inner)
        gain_part = jnp.sum(grad * unit, axis=0, keepdims=True)
        pack_s[4:5, last + index * state : last + (index + 1) * state] = gain_part
    for piece, row in enumerate(gain_rows):
        pack_s[piece : piece + 1, last : last + lane] = row
    gains = pack_s[0:8, last : last + lane]
    high = gains.astype(bf16)
    pack_s[8:16, last : last + lane] = gains - high.astype(f32)
    packed = pack_s[...].astype(bf16)
    for peer in range(out_ref.shape[0]):
        out_ref[peer] = packed


def project_kernel(
    low_ref,
    xg_ref,
    x_ref,
    w_xdt_ref,
    w_xbc_ref,
    w_part_ref,
    misc_ref,
    grad_x_ref,
    out_ref,
    all_s,
    *,
    scale,
):
    rank, width = w_xdt_ref.shape
    bc_width = w_xbc_ref.shape[0]
    own = low_ref.shape[0] // 16
    dt_low = low_ref[:, :rank]
    bc_low = low_ref[:, rank : rank + bc_width]
    summed = xg_ref[...] + jnp.dot(dt_low, w_xdt_ref[...], preferred_element_type=f32)
    summed = summed + jnp.dot(bc_low, w_xbc_ref[...], preferred_element_type=f32)
    grad_x_ref[...] = summed.astype(bf16)
    out_ref[:, :width] = (
        scale
        * lax.dot_general(dt_low, x_ref[...], contract_rows, preferred_element_type=f32)
    ).astype(bf16)
    out_ref[:, width : 2 * width] = w_part_ref[...]
    state = bc_width // 2
    all_s[...] = jnp.zeros_like(all_s)
    all_s[: state + 2, :] = misc_ref[: state + 2, :]
    all_s[state + 8 : state + 8 + bc_width, :] = scale * lax.dot_general(
        bc_low, x_ref[...], contract_rows, preferred_element_type=f32
    )
    gains = low_ref[:, rank + lane : rank + 2 * lane].astype(f32)
    total = jnp.zeros((8, lane), f32)
    for peer in range(16):
        first = peer * own
        total = total + (gains[first : first + 8] + gains[first + 8 : first + 16])
    for piece in range(rank // lane + 1):
        row = state + 8 + bc_width
        all_s[row : row + 1, piece * lane : (piece + 1) * lane] = (
            scale * total[piece : piece + 1]
        )
    for piece in range(width // lane):
        out_ref[piece * 64 : (piece + 1) * 64, 2 * width :] = all_s[
            :, piece * lane : (piece + 1) * lane
        ].astype(bf16)


def total_kernel(parts_ref, xdt_ref, dt_ref, own_ref):
    width = xdt_ref.shape[1]
    total = jnp.sum(parts_ref[...].astype(f32), axis=0)
    xdt_ref[...] = total[:, :width]
    dt_ref[...] = total[:, width : 2 * width]
    for peer in range(own_ref.shape[0]):
        own_ref[peer] = total[:, 2 * width :]


def call(kernel, name, outs, scratch, limit_mib, *args):
    return pl.pallas_call(
        kernel,
        out_shape=tuple(jax.ShapeDtypeStruct(shape, dtype) for shape, dtype in outs),
        in_specs=[in_vmem] * len(args),
        out_specs=tuple([in_vmem] * len(outs)),
        scratch_shapes=[pltpu.VMEM(shape, dtype) for shape, dtype in scratch],
        compiler_params=pltpu.CompilerParams(vmem_limit_bytes=limit_mib * 2**20),
        name=name,
    )(*args)


def send_to_all(block, axis):
    return lax.all_to_all(block, axis, 0, 0)


def body(
    x_inner, proj_dt, proj_bc, grad_y, w_xdt, w_xbc, w_dt, dt_bias, a_log, d_skip, dt_gain, bc_gain
):
    x_rows = x_inner[0]
    gy_rows = grad_y[0]
    tokens, width = x_rows.shape
    rank = proj_dt.shape[2]
    bc_width = proj_bc.shape[2]
    state = bc_width // 2
    own = proj_dt.shape[1]
    dp = lax.axis_size("dp")
    tensor = lax.axis_size("tensor")
    scale = 1.0 / math.sqrt(dp * tokens)
    bias_row = dt_bias.reshape(1, width)
    skip_row = d_skip.reshape(1, width)
    dt_gain_row = dt_gain.reshape(1, rank)
    bc_gain_row = bc_gain.reshape(1, bc_width)

    columns = rank + lane
    own_proj = jnp.concatenate(
        [proj_dt[0], proj_bc[0], jnp.zeros((own, lane - bc_width), bf16)], axis=1
    )
    full_proj = send_to_all(
        jnp.broadcast_to(own_proj[None], (tensor, own, columns)), "tensor"
    ).reshape(tokens, columns)

    rows = ((tokens, width), f32)
    normed_part, w_part, xg, misc = call(
        functools.partial(scan_kernel, wide_lanes=min(512, width), scale=scale),
        "scan",
        [
            ((tokens, columns), bf16),
            ((rank, width), bf16),
            ((tokens, width), f32),
            ((state + 8, width), f32),
        ],
        [
            rows,
            rows,
            rows,
            rows,
            ((state, width), f32),
            ((tokens, rank), bf16),
            ((tokens, 2 * state, lane), f32),
            ((tokens, state, width), f32),
            ((tokens, state, lane), f32),
            ((tokens, state, lane), f32),
            rows,
            rows,
        ],
        56,
        full_proj,
        x_rows,
        gy_rows,
        w_dt,
        bias_row,
        a_log,
        skip_row,
        dt_gain_row,
        bc_gain_row,
    )
    normed_parts = send_to_all(normed_part.reshape(tensor, own, columns), "tensor")
    packed_columns = columns + lane
    (own_low,) = call(
        functools.partial(norm_kernel, state=state),
        "norm",
        [((tensor, own, packed_columns), bf16)],
        [((own, packed_columns), f32)],
        16,
        normed_parts,
        own_proj,
        dt_gain_row,
        bc_gain_row,
    )
    low = send_to_all(own_low, "tensor").reshape(tokens, packed_columns)
    grad_x, parts = call(
        functools.partial(project_kernel, scale=scale),
        "project",
        [((tokens, width), bf16), ((rank, 2 * width + lane), bf16)],
        [((64, width), f32)],
        32,
        low,
        xg,
        x_rows,
        w_xdt,
        w_xbc,
        w_part,
        misc,
    )
    per_device = rank // dp
    all_parts = send_to_all(parts.reshape(dp, per_device, 2 * width + lane), "dp")
    grad_w_xdt, grad_w_dt, own_total = call(
        total_kernel,
        "total",
        [
            ((per_device, width), f32),
            ((per_device, width), f32),
            ((dp, per_device, lane), f32),
        ],
        [],
        32,
        all_parts,
    )
    totals = send_to_all(own_total, "dp").reshape(width // lane, 64, lane)
    totals = totals.transpose(1, 0, 2).reshape(64, width)
    gain_row = state + 8 + bc_width
    return (
        grad_x[None],
        grad_w_xdt,
        grad_w_dt,
        totals[state + 8 : state + 8 + bc_width],
        totals[:state],
        totals[state],
        totals[state + 1],
        totals[gain_row, :rank],
        totals[gain_row, rank : rank + bc_width],
    )


def solution(mesh):
    return jax.shard_map(
        body,
        mesh=mesh,
        in_specs=(
            P("dp", None, "tensor"),
            P("dp", "tensor", None),
            P("dp", "tensor", None),
            P("dp", None, "tensor"),
            P(None, "tensor"),
            P(None, "tensor"),
            P(None, "tensor"),
            P("tensor"),
            P(None, "tensor"),
            P("tensor"),
            P(),
            P(),
        ),
        out_specs=(
            P("dp", None, "tensor"),
            P("dp", "tensor"),
            P("dp", "tensor"),
            P(None, "tensor"),
            P(None, "tensor"),
            P("tensor"),
            P("tensor"),
            P(),
            P(),
        ),
        check_vma=False,
    )
```

time: 1430 us -> 178 us (0.12); the launches traced: 1410 us -> 178 us
  waiting for transfers between devices: 503 us -> 0 us
  local copies, waits for them, and re-layouts: 296 us -> 3.15 us
  other arithmetic: 225 us -> 0.74 us
  blocking collectives: 348 us -> 148 us
  Pallas kernels: 0 us -> 25.7 us
    reduce_scatter x2 -> x0, waiting for transfers between devices: 300 us -> none  [the longest x1 150 us: body(): lax.psum_scatter(grad_scale * lax.dot_general(columns_taken, x_rows, cont...]
    psum x3 -> x0, blocking collectives: 255 us -> none  [the longest x1 95.5 us: body(): lax.psum((grad_scale * dt_gain_part, grad_scale * bc_gain_part), ('dp', '...]
    psum x2 -> x0, waiting for transfers between devices: 203 us -> none  [the longest x1 110 us: body(): lax.psum((dt_normed_part, bc_normed_part), 'tensor')]
    all_to_all x0 -> x5, blocking collectives: none -> 148 us  [send_to_all(): return lax.all_to_all(block, axis, 0, 0)]
    reduce_sum x86 -> x0, other arithmetic: 131 us -> none  [the longest x40 71.4 us: block_scan(): (dt_now * x_blocks[:, offset])[:, None, :] * b_blocks[:, offset][:, :, None]]
    slice x173 -> x4, local copies, waits for them, and re-layouts: 114 us -> 2.48 us  [the longest x1 0.66 us: body(): totals[state + 8:state + 8 + bc_width]]
    pad x92 -> x0, local copies, waits for them, and re-layouts: 93.6 us -> none  [block_scan(): lax.associative_scan(join_blocks, (total_decay, end_state))]
    all_gather x2 -> x0, blocking collectives: 92.7 us -> none  [the longest x1 51.5 us: body(): lax.all_gather(own_bc, 'tensor', axis=0, tiled=True)]
  transfers between devices with their start and end apart: 4 -> 0, of which waited for: 4 -> 0; matrix products, arithmetic and copies ran while one was open for 1% -> 0% of each run, Pallas kernels for 0% -> 0%
where the time goes in v1:
time: 178 us
  blocking collectives  148 us (83%)
  Pallas kernels  25.7 us (14%)
  local copies, waits for them, and re-layouts  3.15 us (2%)
    all_to_all x5, blocking collectives, send_to_all(): return lax.all_to_all(block, axis, 0, 0)  148 us
    pallas_call x4, Pallas kernels, call(): pl.pallas_call(kernel, out_shape=tuple((jax.ShapeDtypeStruct(shape, dtype...  25.7 us

profile of v1, /device:TPU:1, one launch (start us, length us, event | category | flops | bytes accessed | tf_op | source)
XLA Modules:
  0.0 177.8 jit_solution(9723014770224710569)
XLA Ops:
  0.6 0.0 copy-start.7
  0.7 0.0 copy-start.6
  0.7 0.1 pad.2.clone
  0.8 0.7 maximum_maximum_fusion.proj_ref
  1.5 30.2 %all_to_all.25 = bf16[16,16,640]{2,1,0:T(8,128)(2,1)} all-to-all(bf16[16,16,640]{2,1,0:T(8,128)(2,1)S(1)} %broadcast_in_dim.13), channel_id=1, replica_groups=mesh['dp'=32,'tensor'=16] {'tensor'}, dimensions={0} | all-to-all | bytes 655360 | tf_op jit(solution)/shard_map/all_to_all | solution.py:267
  31.7 0.0 copy-start
  31.7 0.0 copy-start.1
  31.7 0.0 copy-start.5
  31.7 23.0 %scan.1 = (bf16[256,640]{1,0:T(8,128)(2,1)}, bf16[512,1024]{1,0:T(8,128)(2,1)}, f32[256,1024]{1,0:T(8,128)}, f32[24,1024]{1,0:T(8,128)}) custom-call(bf16[256,640]{1,0:T(8,128)(2,1)} %bitcast.47, bf16[256,1024]{1,0:T(8,128)(2,1)} %bitcast.36, bf16[256,1024]{1,0:T(8,128)(2,1)} %bitcast.48, bf16[512,1024]{1,0:T(8,128)(2,1)} %w_ref.1, f32[1,1024]{1,0:T(1,128)} %bitcast.53, ...), custom_call_target="tpu_custom_call" | custom-call | tf_op jit(solution)/shard_map/scan/pallas_call | solution.py:255
  54.7 0.0 copy-start.2
  54.7 0.0 copy-start.3
  54.7 0.0 copy-start.4
  54.7 18.8 %all_to_all.26.parts_ref = bf16[16,16,640]{2,1,0:T(8,128)(2,1)S(1)} all-to-all(bf16[16,16,640]{2,1,0:T(8,128)(2,1)} %bitcast.49), channel_id=1, replica_groups=mesh['dp'=32,'tensor'=16] {'tensor'}, dimensions={0} | all-to-all | bytes 655360 | tf_op jit(solution)/shard_map/all_to_all | solution.py:267
  73.5 0.0 copy-done.7
  73.5 0.0 copy-done.6
  73.5 0.3 norm.1
  73.8 20.6 %all_to_all.27 = bf16[16,16,768]{2,1,0:T(8,128)(2,1)S(1)} all-to-all(bf16[16,16,768]{2,1,0:T(8,128)(2,1)S(1)} %norm.1), channel_id=1, replica_groups=mesh['dp'=32,'tensor'=16] {'tensor'}, dimensions={0} | all-to-all | bytes 786432 | tf_op jit(solution)/shard_map/all_to_all | solution.py:267
  94.5 0.0 copy-done
  94.5 0.0 copy-done.1
  94.5 0.0 copy-done.5
  94.5 0.0 copy-done.2
  94.5 0.0 copy-done.3
  94.5 0.0 copy-done.4
  94.5 1.4 project.1
  96.0 63.2 %all_to_all.28.parts_ref = bf16[32,16,2176]{2,1,0:T(8,128)(2,1)S(1)} all-to-all(bf16[32,16,2176]{2,1,0:T(8,128)(2,1)S(1)} %bitcast.35), channel_id=1, replica_groups=mesh['dp'=32,'tensor'=16] {'dp'}, dimensions={0} | all-to-all | bytes 4456448 | tf_op jit(solution)/shard_map/all_to_all | solution.py:267
  159.1 0.9 total.1
  160.1 14.8 %all_to_all.29 = f32[32,16,128]{2,1,0:T(8,128)S(1)} all-to-all(f32[32,16,128]{2,1,0:T(8,128)S(1)} %get-tuple-element.26), channel_id=1, replica_groups=mesh['dp'=32,'tensor'=16] {'dp'}, dimensions={0} | all-to-all | bytes 524288 | tf_op jit(solution)/shard_map/all_to_all | solution.py:267
  174.8 0.6 fusion
  175.4 0.6 copy_bitcast_fusion.2
  176.0 0.7 copy_bitcast_fusion.1
  176.7 0.5 slice_bitcast_fusion.2
  177.2 0.6 slice.38
  (3 shorter events, 0.0 us)
Async XLA Ops:
  0.6 72.9 %copy-start.7 = (f32[32]{0:T(128)S(1)}, f32[32]{0:T(128)}, u32[]{:S(2)}) copy-start(f32[32]{0:T(128)} %param.23) | copy-start | bytes 388
  0.7 72.9 %copy-start.6 = (f32[512]{0:T(512)S(1)}, f32[512]{0:T(512)}, u32[]{:S(2)}) copy-start(f32[512]{0:T(512)} %param.22) | copy-start | bytes 6148
  31.7 62.8 %copy-start = (bf16[1,256,1024]{2,1,0:T(8,128)(2,1)S(1)}, bf16[1,256,1024]{2,1,0:T(8,128)(2,1)}, u32[]{:S(2)}) copy-start(bf16[1,256,1024]{2,1,0:T(8,128)(2,1)} %param.12) | copy-start | bytes 1572868
  31.7 62.8 %copy-start.1 = (bf16[512,1024]{1,0:T(8,128)(2,1)S(1)}, bf16[512,1024]{1,0:T(8,128)(2,1)}, u32[]{:S(2)}) copy-start(bf16[512,1024]{1,0:T(8,128)(2,1)} %w_xdt_ref.1) | copy-start | bytes 3145732
  31.7 62.8 %copy-start.5 = (bf16[32,1024]{1,0:T(8,128)(2,1)S(1)}, bf16[32,1024]{1,0:T(8,128)(2,1)}, u32[]{:S(2)}) copy-start(bf16[32,1024]{1,0:T(8,128)(2,1)} %w_xbc_ref.1) | copy-start | bytes 196612
  54.7 39.8 %copy-start.2 = (bf16[512,1024]{1,0:T(8,128)(2,1)S(1)}, bf16[512,1024]{1,0:T(8,128)(2,1)}, u32[]{:S(2)}) copy-start(bf16[512,1024]{1,0:T(8,128)(2,1)} %get-tuple-element.20.w_part_ref) | copy-start | bytes 3145732
  54.7 39.8 %copy-start.3 = (f32[256,1024]{1,0:T(8,128)S(1)}, f32[256,1024]{1,0:T(8,128)}, u32[]{:S(2)}) copy-start(f32[256,1024]{1,0:T(8,128)} %get-tuple-element.19.xg_ref) | copy-start | bytes 3145732
  54.7 39.8 %copy-start.4 = (f32[24,1024]{1,0:T(8,128)S(1)}, f32[24,1024]{1,0:T(8,128)}, u32[]{:S(2)}) copy-start(f32[24,1024]{1,0:T(8,128)} %get-tuple-element.21.misc_ref) | copy-start | bytes 294916

commit v2 on v1

--- a/solution.py
+++ b/solution.py
@@ -194,6 +194,7 @@
 
 
 def project_kernel(
+    core_ref,
     low_ref,
     xg_ref,
     x_ref,
@@ -202,6 +203,8 @@
     w_part_ref,
     misc_ref,
     grad_x_ref,
+    keep_ref,
+    send_ref,
     out_ref,
     all_s,
     *,
@@ -240,22 +243,51 @@
         out_ref[piece * 64 : (piece + 1) * 64, 2 * width :] = all_s[
             :, piece * lane : (piece + 1) * lane
         ].astype(bf16)
+    first_core = core_ref[0] == 0
+    for pair in range(keep_ref.shape[0]):
+        even = out_ref[32 * pair : 32 * pair + 16, :]
+        odd = out_ref[32 * pair + 16 : 32 * pair + 32, :]
+        keep_ref[pair] = jnp.where(first_core, even, odd)
+        send_ref[pair] = jnp.where(first_core, odd, even)
 
 
 def total_kernel(parts_ref, xdt_ref, dt_ref, own_ref):
     width = xdt_ref.shape[1]
-    total = jnp.sum(parts_ref[...].astype(f32), axis=0)
+    total = parts_ref[0].astype(f32)
+    for peer in range(1, parts_ref.shape[0]):
+        total = total + parts_ref[peer].astype(f32)
     xdt_ref[...] = total[:, :width]
     dt_ref[...] = total[:, width : 2 * width]
     for peer in range(own_ref.shape[0]):
         own_ref[peer] = total[:, 2 * width :]
 
 
+def spread_kernel(
+    parts_ref, xbc_ref, alog_ref, bias_ref, skip_ref, dt_gain_ref, bc_gain_ref, all_s, *, order
+):
+    state = alog_ref.shape[0]
+    bc_width = xbc_ref.shape[0]
+    rank = dt_gain_ref.shape[1]
+    for block, (peer, place) in enumerate(order):
+        row, piece = 16 * (block % 4), lane * (block // 4)
+        all_s[row : row + 16, piece : piece + lane] = parts_ref[
+            peer, :, place * lane : (place + 1) * lane
+        ]
+    alog_ref[...] = all_s[:state, :]
+    bias_ref[...] = all_s[state : state + 1, :]
+    skip_ref[...] = all_s[state + 1 : state + 2, :]
+    xbc_ref[...] = all_s[state + 8 : state + 8 + bc_width, :]
+    gain_row = state + 8 + bc_width
+    dt_gain_ref[...] = all_s[gain_row : gain_row + 1, :rank]
+    bc_gain_ref[...] = all_s[gain_row : gain_row + 1, rank : rank + bc_width]
+
+
 def call(kernel, name, outs, scratch, limit_mib, *args):
+    in_smem = pl.BlockSpec(memory_space=pltpu.SMEM)
     return pl.pallas_call(
         kernel,
         out_shape=tuple(jax.ShapeDtypeStruct(shape, dtype) for shape, dtype in outs),
-        in_specs=[in_vmem] * len(args),
+        in_specs=[in_smem if arg.dtype == jnp.int32 else in_vmem for arg in args],
         out_specs=tuple([in_vmem] * len(outs)),
         scratch_shapes=[pltpu.VMEM(shape, dtype) for shape, dtype in scratch],
         compiler_params=pltpu.CompilerParams(vmem_limit_bytes=limit_mib * 2**20),
@@ -263,8 +295,12 @@
     )(*args)
 
 
-def send_to_all(block, axis):
-    return lax.all_to_all(block, axis, 0, 0)
+def send_to_all(block, axis, groups=None):
+    return lax.all_to_all(block, axis, 0, 0, axis_index_groups=groups)
+
+
+def sum_low(parts):
+    return jnp.sum(parts.astype(f32), axis=0).astype(bf16)
 
 
 def body(
@@ -342,12 +378,19 @@
         bc_gain_row,
     )
     low = send_to_all(own_low, "tensor").reshape(tokens, packed_columns)
-    grad_x, parts = call(
+    cores, z_size = 2, 4
+    x_size = dp // (cores * z_size)
+    core = (lax.axis_index("dp") % cores).astype(jnp.int32).reshape(1)
+    per_device = rank // dp
+    row_width = 2 * width + lane
+    half = ((x_size * z_size, per_device, row_width), bf16)
+    grad_x, kept, sent = call(
         functools.partial(project_kernel, scale=scale),
         "project",
-        [((tokens, width), bf16), ((rank, 2 * width + lane), bf16)],
-        [((64, width), f32)],
+        [((tokens, width), bf16), half, half],
+        [((rank, row_width), bf16), ((64, width), f32)],
         32,
+        core,
         low,
         xg,
         x_rows,
@@ -356,33 +399,68 @@
         w_part,
         misc,
     )
-    per_device = rank // dp
-    all_parts = send_to_all(parts.reshape(dp, per_device, 2 * width + lane), "dp")
+    other_core = [(index, index ^ 1) for index in range(dp)]
+    kept = (kept.astype(f32) + lax.ppermute(sent, "dp", other_core).astype(f32)).astype(bf16)
+    z_stride, x_stride = cores, cores * z_size
+    along_x = [[x * x_stride + rest for x in range(x_size)] for rest in range(x_stride)]
+    along_z = [
+        [x * x_stride + z * z_stride + c for z in range(z_size)]
+        for x in range(x_size)
+        for c in range(cores)
+    ]
+    along_xc = [
+        [x * x_stride + z * z_stride + c for x in range(x_size) for c in range(cores)]
+        for z in range(z_size)
+    ]
+    by_x = sum_low(
+        send_to_all(kept.reshape(x_size, z_size, per_device, row_width), "dp", along_x)
+    )
+    by_z = by_x[:, :, 2 * width :].transpose(1, 0, 2).reshape(1, per_device, z_size * lane)
+    by_z = jnp.broadcast_to(by_z, (z_size, per_device, z_size * lane))
+    by_z = jnp.concatenate([by_x[:, :, : 2 * width], by_z], axis=2)
+    all_parts = send_to_all(by_z, "dp", along_z)
+    shared = x_size * cores
     grad_w_xdt, grad_w_dt, own_total = call(
         total_kernel,
         "total",
         [
             ((per_device, width), f32),
             ((per_device, width), f32),
-            ((dp, per_device, lane), f32),
+            ((shared, per_device, z_size * lane), f32),
         ],
         [],
         32,
         all_parts,
     )
-    totals = send_to_all(own_total, "dp").reshape(width // lane, 64, lane)
-    totals = totals.transpose(1, 0, 2).reshape(64, width)
-    gain_row = state + 8 + bc_width
+    totals = send_to_all(own_total, "dp", along_xc)
+    order = tuple(
+        (x * cores + c, z) for x in range(x_size) for z in range(z_size) for c in range(cores)
+    )
+    grad_w_xbc, grad_a_log, bias_total, skip_total, dt_gain_total, bc_gain_total = call(
+        functools.partial(spread_kernel, order=order),
+        "spread",
+        [
+            ((bc_width, width), f32),
+            ((state, width), f32),
+            ((1, width), f32),
+            ((1, width), f32),
+            ((1, rank), f32),
+            ((1, bc_width), f32),
+        ],
+        [((64, width), f32)],
+        16,
+        totals,
+    )
     return (
         grad_x[None],
         grad_w_xdt,
         grad_w_dt,
-        totals[state + 8 : state + 8 + bc_width],
-        totals[:state],
-        totals[state],
-        totals[state + 1],
-        totals[gain_row, :rank],
-        totals[gain_row, rank : rank + bc_width],
+        grad_w_xbc,
+        grad_a_log,
+        bias_total.reshape(width),
+        skip_total.reshape(width),
+        dt_gain_total.reshape(rank),
+        bc_gain_total.reshape(bc_width),
     )
 
 

time: 178 us -> 152 us (0.85)
  blocking collectives: 148 us -> 92.2 us
  waiting for transfers between devices: 0 us -> 17.1 us
  starting transfers between devices: 0 us -> 10.7 us
    all_to_all x5, blocking collectives: 148 us -> 92.2 us  [send_to_all(): return lax.all_to_all(block, axis, 0, 0, axis_index_groups=groups)]
    all_to_all x0 -> x1, waiting for transfers between devices: none -> 14.7 us  [send_to_all(): return lax.all_to_all(block, axis, 0, 0, axis_index_groups=groups)]
    all_to_all x0 -> x1, starting transfers between devices: none -> 6.08 us  [send_to_all(): return lax.all_to_all(block, axis, 0, 0, axis_index_groups=groups)]
    ppermute x0 -> x1, starting transfers between devices: none -> 4.63 us  [body(): lax.ppermute(sent, 'dp', other_core).astype(f32)]
    slice x4 -> x1, local copies, waits for them, and re-layouts: 2.48 us -> 0.02 us  [body(): by_z = jnp.concatenate([by_x[:, :, :2 * width], by_z], axis=2)]
    unnamed x16, local copies, waits for them, and re-layouts: 0.03 us -> 2.47 us
    ppermute x0 -> x1, waiting for transfers between devices: none -> 2.36 us  [body(): lax.ppermute(sent, 'dp', other_core).astype(f32)]
    pallas_call x4 -> x5, Pallas kernels: 25.7 us -> 27 us  [call(): pl.pallas_call(kernel, out_shape=tuple((jax.ShapeDtypeStruct(shape, dtype...]
  transfers between devices with their start and end apart: 0 -> 2, of which waited for: 0 -> 2; matrix products, arithmetic and copies ran while one was open for 0% -> 0% of each run, Pallas kernels for 0% -> 0%
where the time goes in v2:
time: 152 us
  blocking collectives  92.2 us (61%)
  Pallas kernels  27 us (18%)
  waiting for transfers between devices  17.1 us (11%)
  starting transfers between devices  10.7 us (7%)
  local copies, waits for them, and re-layouts  2.6 us (2%)
    all_to_all x5, blocking collectives, send_to_all(): return lax.all_to_all(block, axis, 0, 0, axis_index_groups=groups)  92.2 us
    pallas_call x5, Pallas kernels, call(): pl.pallas_call(kernel, out_shape=tuple((jax.ShapeDtypeStruct(shape, dtype...  27 us
    all_to_all x1, waiting for transfers between devices, send_to_all(): return lax.all_to_all(block, axis, 0, 0, axis_index_groups=groups)  14.7 us
    all_to_all x1, starting transfers between devices, send_to_all(): return lax.all_to_all(block, axis, 0, 0, axis_index_groups=groups)  6.08 us
    ppermute x1, starting transfers between devices, body(): lax.ppermute(sent, 'dp', other_core).astype(f32)  4.63 us
  transfers between devices with their start and end apart: 2, of which 2 were waited for; matrix products, arithmetic and copies ran while one was open for 0% of the time, Pallas kernels for 0%

profile of v2, /device:TPU:1, one launch (start us, length us, event | category | flops | bytes accessed | tf_op | source)
XLA Modules:
  0.0 151.6 jit_solution(17601094581196710780)
XLA Ops:
  0.7 0.1 pad.4.clone
  0.7 0.7 maximum_maximum_fusion.proj_ref
  1.5 30.2 %all_to_all.30 = bf16[16,16,640]{2,1,0:T(8,128)(2,1)} all-to-all(bf16[16,16,640]{2,1,0:T(8,128)(2,1)S(1)} %broadcast_in_dim.20), channel_id=1, replica_groups=mesh['dp'=32,'tensor'=16] {'tensor'}, dimensions={0} | all-to-all | bytes 655360 | tf_op jit(solution)/shard_map/all_to_all | solution.py:299
  31.7 0.0 copy-start.6
  31.7 0.0 copy-start.7
  31.7 22.9 %scan.1 = (bf16[256,640]{1,0:T(8,128)(2,1)}, bf16[512,1024]{1,0:T(8,128)(2,1)}, f32[256,1024]{1,0:T(8,128)}, f32[24,1024]{1,0:T(8,128)}) custom-call(bf16[256,640]{1,0:T(8,128)(2,1)} %bitcast.32, bf16[256,1024]{1,0:T(8,128)(2,1)} %bitcast.24, bf16[256,1024]{1,0:T(8,128)(2,1)} %bitcast.33, bf16[512,1024]{1,0:T(8,128)(2,1)} %w_ref.1, f32[1,1024]{1,0:T(1,128)} %bitcast.36, ...), custom_call_target="tpu_custom_call" | custom-call | tf_op jit(solution)/shard_map/scan/pallas_call | solution.py:287
  54.5 0.0 copy-start
  54.5 0.0 copy-start.1
  54.6 0.0 copy-start.5
  54.6 18.8 %all_to_all.31.parts_ref = bf16[16,16,640]{2,1,0:T(8,128)(2,1)S(1)} all-to-all(bf16[16,16,640]{2,1,0:T(8,128)(2,1)} %bitcast.34), channel_id=1, replica_groups=mesh['dp'=32,'tensor'=16] {'tensor'}, dimensions={0} | all-to-all | bytes 655360 | tf_op jit(solution)/shard_map/all_to_all | solution.py:299
  73.4 0.0 copy-done.6
  73.4 0.0 copy-done.7
  73.4 1.1 norm.1
  74.5 6.1 %all-to-all-start.2 = ((bf16[16,16,768]{2,1,0:T(8,128)(2,1)}), bf16[16,16,768]{2,1,0:T(8,128)(2,1)S(1)}, u32[]{:S(2)}, u32[]{:S(2)}) async-start(bf16[16,16,768]{2,1,0:T(8,128)(2,1)} %norm.1), calls=%async_computation.2 | async-start | bytes 786432 | tf_op jit(solution)/shard_map/all_to_all | solution.py:299
  80.6 14.7 %all-to-all-done.2 = bf16[16,16,768]{2,1,0:T(8,128)(2,1)S(1)} async-done(((bf16[16,16,768]{2,1,0:T(8,128)(2,1)}), bf16[16,16,768]{2,1,0:T(8,128)(2,1)S(1)}, u32[]{:S(2)}, u32[]{:S(2)}) %all-to-all-start.2) | async-done | bytes 393248 | tf_op jit(solution)/shard_map/all_to_all | solution.py:299
  95.3 0.0 copy-done
  95.3 0.0 copy-done.1
  95.3 0.0 copy-done.4
  95.3 0.0 copy-done.5
  95.3 0.0 copy-start.2
  95.3 1.2 copy-done.2
  96.6 1.2 copy-done.3
  97.8 1.7 %project.1 = (bf16[256,1024]{1,0:T(8,128)(2,1)}, bf16[16,16,2176]{2,1,0:T(8,128)(2,1)S(1)}, bf16[16,16,2176]{2,1,0:T(8,128)(2,1)S(1)}) custom-call(s32[1]{0:T(128)} %bitcast.core_ref, bf16[256,768]{1,0:T(8,128)(2,1)S(1)} %bitcast.26, f32[256,1024]{1,0:T(8,128)S(1)} %copy-done.3, bf16[256,1024]{1,0:T(8,128)(2,1)S(1)} %bitcast.25, ...), custom_call_target="tpu_custom_call" | custom-call | tf_op jit(solution)/shard_map/project/pallas_call | solution.py:287
  99.4 4.6 %collective-permute-start = (bf16[16,16,2176]{2,1,0:T(8,128)(2,1)S(1)}, bf16[16,16,2176]{2,1,0:T(8,128)(2,1)S(1)}, u32[]{:S(2)}, u32[]{:S(2)}) collective-permute-start(bf16[16,16,2176]{2,1,0:T(8,128)(2,1)S(1)} %get-tuple-element.31), channel_id=1, source_target_pairs={{0,16},{16,0},{32,48},{48,32},{64,80},{80,64},{96,112},{112,96},{1... | collective-permute-start | bytes 3342344 | tf_op jit(solution)/shard_map/ppermute | solution.py:403
  104.1 2.4 %collective-permute-done = bf16[16,16,2176]{2,1,0:T(8,128)(2,1)S(1)} collective-permute-done((bf16[16,16,2176]{2,1,0:T(8,128)(2,1)S(1)}, bf16[16,16,2176]{2,1,0:T(8,128)(2,1)S(1)}, u32[]{:S(2)}, u32[]{:S(2)}) %collective-permute-start) | collective-permute-done | bytes 1114144 | tf_op jit(solution)/shard_map/ppermute | solution.py:403
  106.4 0.3 add_convert_fusion
  106.7 19.0 %all_to_all.32 = bf16[4,4,16,2176]{3,2,1,0:T(8,128)(2,1)S(1)} all-to-all(bf16[4,4,16,2176]{3,2,1,0:T(8,128)(2,1)S(1)} %bitcast.31), channel_id=1, replica_groups={{0,128,256,384},{16,144,272,400},{32,160,288,416},{48,176,304,432},{64,..., dimensions={0} | all-to-all | bytes 2228224 | tf_op jit(solution)/shard_map/all_to_all | solution.py:299
  125.8 0.2 reduce_sum.12
  126.1 12.9 %all_to_all.33.parts_ref = bf16[4,16,2560]{2,1,0:T(8,128)(2,1)S(1)} all-to-all(bf16[4,16,2560]{2,1,0:T(8,128)(2,1)S(1)} %pad_maximum_fusion), channel_id=1, replica_groups={{0,32,64,96},{16,48,80,112},{128,160,192,224},{144,176,208,240},{256,28..., dimensions={0} | all-to-all | bytes 655360 | tf_op jit(solution)/shard_map/all_to_all | solution.py:299
  139.0 0.7 total.1
  139.6 11.3 %all_to_all.34.parts_ref = f32[8,16,512]{2,1,0:T(8,128)S(1)} all-to-all(f32[8,16,512]{2,1,0:T(8,128)S(1)} %get-tuple-element.34), channel_id=1, replica_groups={{0,16,128,144,256,272,384,400},{32,48,160,176,288,304,416,432},{64,80,1..., dimensions={0} | all-to-all | bytes 524288 | tf_op jit(solution)/shard_map/all_to_all | solution.py:299
  150.9 0.7 spread.1
  (8 shorter events, 0.1 us)
Async XLA Ops:
  31.7 41.7 %copy-start.6 = (f32[512]{0:T(512)S(1)}, f32[512]{0:T(512)}, u32[]{:S(2)}) copy-start(f32[512]{0:T(512)} %param.22) | copy-start | bytes 6148
  31.7 41.7 %copy-start.7 = (f32[32]{0:T(128)S(1)}, f32[32]{0:T(128)}, u32[]{:S(2)}) copy-start(f32[32]{0:T(128)} %param.23) | copy-start | bytes 388
  54.5 40.8 %copy-start = (bf16[1,256,1024]{2,1,0:T(8,128)(2,1)S(1)}, bf16[1,256,1024]{2,1,0:T(8,128)(2,1)}, u32[]{:S(2)}) copy-start(bf16[1,256,1024]{2,1,0:T(8,128)(2,1)} %param.12) | copy-start | bytes 1572868
  54.5 40.8 %copy-start.1 = (bf16[512,1024]{1,0:T(8,128)(2,1)S(1)}, bf16[512,1024]{1,0:T(8,128)(2,1)}, u32[]{:S(2)}) copy-start(bf16[512,1024]{1,0:T(8,128)(2,1)} %w_xdt_ref.1) | copy-start | bytes 3145732
  54.5 40.8 %copy-start.4 = (f32[24,1024]{1,0:T(8,128)S(1)}, f32[24,1024]{1,0:T(8,128)}, u32[]{:S(2)}) copy-start(f32[24,1024]{1,0:T(8,128)} %get-tuple-element.28.misc_ref) | copy-start | bytes 294916
  54.6 40.8 %copy-start.5 = (bf16[32,1024]{1,0:T(8,128)(2,1)S(1)}, bf16[32,1024]{1,0:T(8,128)(2,1)}, u32[]{:S(2)}) copy-start(bf16[32,1024]{1,0:T(8,128)(2,1)} %w_xbc_ref.1) | copy-start | bytes 196612
  74.5 20.8 %all-to-all-start.2 = ((bf16[16,16,768]{2,1,0:T(8,128)(2,1)}), bf16[16,16,768]{2,1,0:T(8,128)(2,1)S(1)}, u32[]{:S(2)}, u32[]{:S(2)}) async-start(bf16[16,16,768]{2,1,0:T(8,128)(2,1)} %norm.1), calls=%async_computation.2 | async-start | bytes 786432 | tf_op jit(solution)/shard_map/all_to_all | solution.py:299
  95.3 1.2 copy-start.2
  96.6 1.2 copy-start.3
  99.4 7.0 %collective-permute-start = (bf16[16,16,2176]{2,1,0:T(8,128)(2,1)S(1)}, bf16[16,16,2176]{2,1,0:T(8,128)(2,1)S(1)}, u32[]{:S(2)}, u32[]{:S(2)}) collective-permute-start(bf16[16,16,2176]{2,1,0:T(8,128)(2,1)S(1)} %get-tuple-element.31), channel_id=1, source_target_pairs={{0,16},{16,0},{32,48},{48,32},{64,80},{80,64},{96,112},{112,96},{1... | collective-permute-start | bytes 3342344 | tf_op jit(solution)/shard_map/ppermute | solution.py:403

commit v3 on v2

--- a/solution.py
+++ b/solution.py
@@ -96,6 +96,20 @@
             total = total + part[:, rep * lane : (rep + 1) * lane]
         return total
 
+    def fold_states(part):
+        total = part[:8]
+        for rep in range(1, state // 8):
+            total = total + part[rep * 8 : (rep + 1) * 8]
+        return total
+
+    row_ids = lax.broadcasted_iota(jnp.int32, (8, wide_lanes), 0)
+
+    def join_rows(early, late, level):
+        mine = (row_ids & level) == 0
+        kept = jnp.where(mine, early, late)
+        moved = jnp.where(mine, late, early)
+        return kept + pltpu.roll(moved, 8 - level, 0)
+
     for group in range(width // wide_lanes):
         cols = slice(group * wide_lanes, (group + 1) * wide_lanes)
 
@@ -116,18 +130,25 @@
             later, a_total = carry
             block = tokens // 8 - 1 - step
             a2 = a2_s[:, cols]
+            waiting = {}
             for offset in range(7, -1, -1):
                 t = block * 8 + offset
                 dt_now = dt_s[pl.ds(t, 1), cols]
                 adjoint = widen(bcb_s[t, state:]) * gy_s[pl.ds(t, 1), cols] + later
                 through = adjoint * u_s[t, :, cols]
-                s1_s[pl.ds(t, 1), cols] = jnp.sum(
-                    adjoint * widen(bcb_s[t, :state]), axis=0, keepdims=True
-                )
-                s2_s[pl.ds(t, 1), cols] = jnp.sum(through * a2, axis=0, keepdims=True)
+                first = fold_states(adjoint * widen(bcb_s[t, :state]))
+                second = fold_states(through * a2)
+                level = 1
+                while level in waiting:
+                    later_first, later_second = waiting.pop(level)
+                    first = join_rows(first, later_first, level)
+                    second = join_rows(second, later_second, level)
+                    level *= 2
+                waiting[level] = (first, second)
                 b_acc[pl.ds(t, 1)] += fold(adjoint * src_s[pl.ds(t, 1), cols])[None]
                 a_total = a_total + dt_now * through
                 later = jnp.exp2(dt_now * a2) * adjoint
+            s1_s[pl.ds(block * 8, 8), cols], s2_s[pl.ds(block * 8, 8), cols] = waiting[8]
             return later, a_total
 
         _, a_total = lax.fori_loop(0, tokens // 8, backward, (zeros, zeros))
@@ -142,7 +163,7 @@
     misc_ref[state + 1 : state + 2, :] = scale * jnp.sum(
         gy_s[...] * x_ref[...].astype(f32), axis=0, keepdims=True
     )
-    normed_ref[:, :rank] = lax.dot_general(
+    dt_normed = lax.dot_general(
         pre_grad, w_ref[...], contract_cols, preferred_element_type=f32
     ).astype(bf16)
     w_part_ref[...] = (
@@ -152,26 +173,48 @@
     source_sum = jnp.sum(src_s[...] * gy_s[...], axis=1, keepdims=True)
     b_grad = jnp.sum(b_acc[...], axis=2)
     c_grad = jnp.sum(c_acc[...], axis=2) + b_rows * source_sum
-    normed_ref[:, rank : rank + state] = b_grad.astype(bf16)
-    normed_ref[:, rank + state : rank + 2 * state] = c_grad.astype(bf16)
-    normed_ref[:, rank + 2 * state :] = jnp.zeros_like(normed_ref[:, rank + 2 * state :])
-
-
-def norm_kernel(parts_ref, proj_ref, dt_gain_ref, bc_gain_ref, out_ref, pack_s, *, state):
+    b_grad = b_grad.astype(bf16)
+    c_grad = c_grad.astype(bf16)
+    z_size, y_size, own = normed_ref.shape[1], normed_ref.shape[0], normed_ref.shape[2]
+    for y in range(y_size):
+        for z in range(z_size):
+            rows = slice((z * y_size + y) * own, (z * y_size + y + 1) * own)
+            normed_ref[y, z, :, :rank] = dt_normed[rows]
+            normed_ref[y, z, :, rank : rank + state] = b_grad[rows]
+            normed_ref[y, z, :, rank + state : rank + 2 * state] = c_grad[rows]
+            normed_ref[y, z, :, rank + 2 * state :] = jnp.zeros(
+                (own, lane - 2 * state), bf16
+            )
+
+
+def sum_kernel(parts_ref, out_ref):
+    total = parts_ref[0].astype(f32)
+    for peer in range(1, parts_ref.shape[0]):
+        total = total + parts_ref[peer].astype(f32)
+    out_ref[...] = total
+
+
+def norm_kernel(
+    y_ref, mine_ref, other_ref, proj_ref, dt_gain_ref, bc_gain_ref, out_ref, pack_s, *, state
+):
     rank = dt_gain_ref.shape[1]
-    grads = jnp.sum(parts_ref[...].astype(f32), axis=0)
-    dt_norm, b_norm, c_norm = inverse_norms(proj_ref[...].astype(f32), rank, state)
+    rows = mine_ref.shape[0]
+    grads = mine_ref[...] + other_ref[...]
+    proj = jnp.concatenate([proj_ref[z, y_ref[0]] for z in range(proj_ref.shape[0])], axis=0)
+    dt_norm, b_norm, c_norm = inverse_norms(proj.astype(f32), rank, state)
     dt_grad = grads[:, :rank]
     dt_unit = dt_norm[0] * dt_norm[1]
     dt_cot = dt_grad * dt_gain_ref[...]
     dt_mean = jnp.mean(dt_cot * dt_unit, axis=1, keepdims=True)
-    pack_s[...] = jnp.zeros_like(pack_s)
+    pack_s[:, rank:] = jnp.zeros((rows, lane), f32)
     pack_s[:, :rank] = dt_norm[1] * (dt_cot - dt_unit * dt_mean)
-    gain_rows = []
     dt_gain_part = jnp.sum(dt_grad * dt_unit, axis=0, keepdims=True)
-    for piece in range(rank // lane):
-        gain_rows.append(dt_gain_part[:, piece * lane : (piece + 1) * lane])
-    last = rank + lane
+    last = rank + lane // 2
+    for piece in range(rank // (lane // 2)):
+        pack_s[piece : piece + 1, last:] = dt_gain_part[
+            :, piece * (lane // 2) : (piece + 1) * (lane // 2)
+        ]
+    gain_row = rank // (lane // 2)
     for index, part in enumerate((b_norm, c_norm)):
         start = rank + index * state
         grad = grads[:, start : start + state]
@@ -181,13 +224,11 @@
         inner = jnp.where(part[2] > state_floor, mean, 0.0)
         inner = jnp.where(part[2] == state_floor, 0.5 * mean, inner)
         pack_s[:, start : start + state] = part[1] * (cot - unit * inner)
-        gain_part = jnp.sum(grad * unit, axis=0, keepdims=True)
-        pack_s[4:5, last + index * state : last + (index + 1) * state] = gain_part
-    for piece, row in enumerate(gain_rows):
-        pack_s[piece : piece + 1, last : last + lane] = row
-    gains = pack_s[0:8, last : last + lane]
-    high = gains.astype(bf16)
-    pack_s[8:16, last : last + lane] = gains - high.astype(f32)
+        pack_s[gain_row : gain_row + 1, last + index * state : last + (index + 1) * state] = (
+            jnp.sum(grad * unit, axis=0, keepdims=True)
+        )
+    gains = pack_s[: rows // 2, last:]
+    pack_s[rows // 2 :, last:] = gains - gains.astype(bf16).astype(f32)
     packed = pack_s[...].astype(bf16)
     for peer in range(out_ref.shape[0]):
         out_ref[peer] = packed
@@ -207,14 +248,19 @@
     send_ref,
     out_ref,
     all_s,
+    low_s,
     *,
     scale,
 ):
     rank, width = w_xdt_ref.shape
     bc_width = w_xbc_ref.shape[0]
-    own = low_ref.shape[0] // 16
-    dt_low = low_ref[:, :rank]
-    bc_low = low_ref[:, rank : rank + bc_width]
+    y_size, z_size, own, _ = low_ref.shape
+    for y in range(y_size):
+        for z in range(z_size):
+            start = (z * y_size + y) * own
+            low_s[start : start + own, :] = low_ref[y, z]
+    dt_low = low_s[:, :rank]
+    bc_low = low_s[:, rank : rank + bc_width]
     summed = xg_ref[...] + jnp.dot(dt_low, w_xdt_ref[...], preferred_element_type=f32)
     summed = summed + jnp.dot(bc_low, w_xbc_ref[...], preferred_element_type=f32)
     grad_x_ref[...] = summed.astype(bf16)
@@ -229,16 +275,18 @@
     all_s[state + 8 : state + 8 + bc_width, :] = scale * lax.dot_general(
         bc_low, x_ref[...], contract_rows, preferred_element_type=f32
     )
-    gains = low_ref[:, rank + lane : rank + 2 * lane].astype(f32)
-    total = jnp.zeros((8, lane), f32)
-    for peer in range(16):
-        first = peer * own
-        total = total + (gains[first : first + 8] + gains[first + 8 : first + 16])
-    for piece in range(rank // lane + 1):
-        row = state + 8 + bc_width
-        all_s[row : row + 1, piece * lane : (piece + 1) * lane] = (
-            scale * total[piece : piece + 1]
-        )
+    gains = jnp.zeros((own, lane), f32)
+    for y in range(y_size):
+        for z in range(z_size):
+            gains = gains + low_ref[y, z, :, rank:].astype(f32)
+    gains = scale * gains[:, lane // 2 :]
+    gain_row = state + 8 + bc_width
+    for piece in range(rank // (lane // 2)):
+        all_s[gain_row : gain_row + 1, piece * (lane // 2) : (piece + 1) * (lane // 2)] = gains[
+            piece : piece + 1
+        ]
+    piece = rank // (lane // 2)
+    all_s[gain_row : gain_row + 1, rank : rank + bc_width] = gains[piece : piece + 1, :bc_width]
     for piece in range(width // lane):
         out_ref[piece * 64 : (piece + 1) * 64, 2 * width :] = all_s[
             :, piece * lane : (piece + 1) * lane
@@ -329,12 +377,16 @@
         jnp.broadcast_to(own_proj[None], (tensor, own, columns)), "tensor"
     ).reshape(tokens, columns)
 
+    z_pair = 2
+    y_size = tensor // z_pair
+    along_y = [[z * y_size + y for y in range(y_size)] for z in range(z_pair)]
     rows = ((tokens, width), f32)
+    by_token = (y_size, z_pair, own, columns)
     normed_part, w_part, xg, misc = call(
         functools.partial(scan_kernel, wide_lanes=min(512, width), scale=scale),
         "scan",
         [
-            ((tokens, columns), bf16),
+            (by_token, bf16),
             ((rank, width), bf16),
             ((tokens, width), f32),
             ((state + 8, width), f32),
@@ -353,7 +405,7 @@
             rows,
             rows,
         ],
-        56,
+        42,
         full_proj,
         x_rows,
         gy_rows,
@@ -364,20 +416,31 @@
         dt_gain_row,
         bc_gain_row,
     )
-    normed_parts = send_to_all(normed_part.reshape(tensor, own, columns), "tensor")
-    packed_columns = columns + lane
+    shared_rows = z_pair * own
+    normed_parts = send_to_all(
+        normed_part.reshape(y_size, shared_rows, columns), "tensor", along_y
+    )
+    (mine,) = call(
+        sum_kernel, "join", [((shared_rows, columns), f32)], [], 4, normed_parts
+    )
+    other = lax.ppermute(
+        mine, "tensor", [(index, (index + y_size) % tensor) for index in range(tensor)]
+    )
+    y_index = (lax.axis_index("tensor") % y_size).astype(jnp.int32).reshape(1)
     (own_low,) = call(
         functools.partial(norm_kernel, state=state),
         "norm",
-        [((tensor, own, packed_columns), bf16)],
-        [((own, packed_columns), f32)],
-        16,
-        normed_parts,
-        own_proj,
+        [((y_size, shared_rows, columns), bf16)],
+        [((shared_rows, columns), f32)],
+        4,
+        y_index,
+        mine,
+        other,
+        full_proj.reshape(z_pair, y_size, own, columns),
         dt_gain_row,
         bc_gain_row,
     )
-    low = send_to_all(own_low, "tensor").reshape(tokens, packed_columns)
+    low = send_to_all(own_low, "tensor", along_y).reshape(by_token)
     cores, z_size = 2, 4
     x_size = dp // (cores * z_size)
     core = (lax.axis_index("dp") % cores).astype(jnp.int32).reshape(1)
@@ -388,8 +451,12 @@
         functools.partial(project_kernel, scale=scale),
         "project",
         [((tokens, width), bf16), half, half],
-        [((rank, row_width), bf16), ((64, width), f32)],
-        32,
+        [
+            ((rank, row_width), bf16),
+            ((64, width), f32),
+            ((tokens, columns), bf16),
+        ],
+        16,
         core,
         low,
         xg,
@@ -429,7 +496,7 @@
             ((shared, per_device, z_size * lane), f32),
         ],
         [],
-        32,
+        4,
         all_parts,
     )
     totals = send_to_all(own_total, "dp", along_xc)
@@ -448,7 +515,7 @@
             ((1, bc_width), f32),
         ],
         [((64, width), f32)],
-        16,
+        4,
         totals,
     )
     return (

time: 152 us -> 154 us (1.013)
  starting transfers between devices: 10.7 us -> 16.3 us
  blocking collectives: 92.2 us -> 87.3 us
  local copies, waits for them, and re-layouts: 2.6 us -> 7.14 us
  Pallas kernels: 27 us -> 22.8 us
    all_to_all x5, blocking collectives: 92.2 us -> 87.3 us  [send_to_all(): return lax.all_to_all(block, axis, 0, 0, axis_index_groups=groups)]
    ppermute x0 -> x1, waiting for transfers between devices: none -> 4.8 us  [body(): lax.ppermute(mine, 'tensor', [(index, (index + y_size) % tensor) for inde...]
    all_to_all x1, waiting for transfers between devices: 14.7 us -> 10.1 us  [send_to_all(): return lax.all_to_all(block, axis, 0, 0, axis_index_groups=groups)]
    unnamed x16 -> x28, local copies, waits for them, and re-layouts: 2.47 us -> 7 us
    ppermute x0 -> x1, starting transfers between devices: none -> 4.51 us  [body(): lax.ppermute(mine, 'tensor', [(index, (index + y_size) % tensor) for inde...]
    pallas_call x5 -> x6, Pallas kernels: 27 us -> 22.8 us  [call(): pl.pallas_call(kernel, out_shape=tuple((jax.ShapeDtypeStruct(shape, dtype...]
    ppermute x1, starting transfers between devices: 4.63 us -> 8.39 us  [body(): lax.ppermute(sent, 'dp', other_core).astype(f32)]
    all_to_all x1, starting transfers between devices: 6.08 us -> 3.45 us  [send_to_all(): return lax.all_to_all(block, axis, 0, 0, axis_index_groups=groups)]
  transfers between devices with their start and end apart: 2 -> 3, of which waited for: 2 -> 3; matrix products, arithmetic and copies ran while one was open for 0% -> 0% of each run, Pallas kernels for 0% -> 0%
where the time goes in v3:
time: 154 us; the launch traced here: 153 us
  blocking collectives  87.3 us (57%)
  Pallas kernels  22.8 us (15%)
  waiting for transfers between devices  17.3 us (11%)
  starting transfers between devices  16.3 us (11%)
  local copies, waits for them, and re-layouts  7.14 us (5%)
    all_to_all x5, blocking collectives, send_to_all(): return lax.all_to_all(block, axis, 0, 0, axis_index_groups=groups)  87.3 us
    pallas_call x6, Pallas kernels, call(): pl.pallas_call(kernel, out_shape=tuple((jax.ShapeDtypeStruct(shape, dtype...  22.8 us
    all_to_all x1, waiting for transfers between devices, send_to_all(): return lax.all_to_all(block, axis, 0, 0, axis_index_groups=groups)  10.1 us
    ppermute x1, starting transfers between devices, body(): lax.ppermute(sent, 'dp', other_core).astype(f32)  8.39 us
    unnamed x28, local copies, waits for them, and re-layouts  7 us
    ppermute x1, waiting for transfers between devices, body(): lax.ppermute(mine, 'tensor', [(index, (index + y_size) % tensor) for inde...  4.8 us
    ppermute x1, starting transfers between devices, body(): lax.ppermute(mine, 'tensor', [(index, (index + y_size) % tensor) for inde...  4.51 us
    all_to_all x1, starting transfers between devices, send_to_all(): return lax.all_to_all(block, axis, 0, 0, axis_index_groups=groups)  3.45 us
  transfers between devices with their start and end apart: 3, of which 3 were waited for; matrix products, arithmetic and copies ran while one was open for 0% of the time, Pallas kernels for 0%

profile of v3, /device:TPU:1, one launch (start us, length us, event | category | flops | bytes accessed | tf_op | source)
XLA Modules:
  0.0 152.9 jit_solution(5474678061178362945)
XLA Ops:
  0.6 0.0 copy-start.5
  0.7 0.1 pad.4.clone
  0.7 0.8 maximum_maximum_fusion
  1.6 30.1 %all_to_all.30 = bf16[16,16,640]{2,1,0:T(8,128)(2,1)S(1)} all-to-all(bf16[16,16,640]{2,1,0:T(8,128)(2,1)S(1)} %broadcast_in_dim.20), channel_id=1, replica_groups=mesh['dp'=32,'tensor'=16] {'tensor'}, dimensions={0} | all-to-all | bytes 655360 | tf_op jit(solution)/shard_map/all_to_all | solution.py:347
  31.6 0.0 copy-done
  31.6 1.2 copy-done.1
  32.9 0.8 copy-done.7
  33.7 0.7 copy-done.8
  34.4 0.7 copy-done.10
  35.1 0.7 copy-done.11
  35.8 0.7 copy-done.12
  36.4 18.6 %scan.1 = (bf16[8,2,16,640]{3,2,1,0:T(8,128)(2,1)S(1)}, bf16[512,1024]{1,0:T(8,128)(2,1)S(1)}, f32[256,1024]{1,0:T(8,128)S(1)}, f32[24,1024]{1,0:T(8,128)S(1)}) custom-call(bf16[256,640]{1,0:T(8,128)(2,1)S(1)} %bitcast.26, bf16[256,1024]{1,0:T(8,128)(2,1)S(1)} %bitcast.28, bf16[256,1024]{1,0:T(8,128)(2,1)S(1)} %bitcast.31, bf16[512,1024]{1,0:T(8,128)(2,1)S(1)} %copy-done.1, ...), custom_call_target="tpu_custom_call" | custom-call | tf_op jit(solution)/shard_map/scan/pallas_call | solution.py:335
  55.1 1.0 copy-done.3
  56.0 14.1 %all_to_all.31.parts_ref = bf16[8,32,640]{2,1,0:T(8,128)(2,1)S(1)} all-to-all(bf16[8,32,640]{2,1,0:T(8,128)(2,1)S(1)} %bitcast.32), channel_id=1, replica_groups={{0,1,2,3,4,5,6,7},{8,9,10,11,12,13,14,15},{16,17,18,19,20,21,22,23},{24..., dimensions={0} | all-to-all | bytes 655360 | tf_op jit(solution)/shard_map/all_to_all | solution.py:347
  70.2 4.5 %collective-permute-start = (f32[32,640]{1,0:T(8,128)S(1)}, f32[32,640]{1,0:T(8,128)S(1)}, u32[]{:S(2)}, u32[]{:S(2)}) collective-permute-start(f32[32,640]{1,0:T(8,128)S(1)} %join.1.mine_ref), channel_id=1, source_target_pairs={{0,8},{1,9},{2,10},{3,11},{4,12},{5,13},{6,14},{7,15},{8,0},{9,1},... | collective-permute-start | bytes 245768 | tf_op jit(solution)/shard_map/ppermute | solution.py:426
  74.7 4.8 %collective-permute-done.other_ref = f32[32,640]{1,0:T(8,128)S(1)} collective-permute-done((f32[32,640]{1,0:T(8,128)S(1)}, f32[32,640]{1,0:T(8,128)S(1)}, u32[]{:S(2)}, u32[]{:S(2)}) %collective-permute-start) | collective-permute-done | bytes 81952 | tf_op jit(solution)/shard_map/ppermute | solution.py:426
  79.5 0.0 copy-done.13
  79.5 1.1 norm.1
  80.6 3.5 %all-to-all-start.2 = ((bf16[8,32,640]{2,1,0:T(8,128)(2,1)}), bf16[8,32,640]{2,1,0:T(8,128)(2,1)S(1)}, u32[]{:S(2)}, u32[]{:S(2)}) async-start(bf16[8,32,640]{2,1,0:T(8,128)(2,1)} %norm.1), calls=%async_computation.2 | async-start | bytes 655360 | tf_op jit(solution)/shard_map/all_to_all | solution.py:347
  84.0 10.1 %all-to-all-done.2 = bf16[8,32,640]{2,1,0:T(8,128)(2,1)S(1)} async-done(((bf16[8,32,640]{2,1,0:T(8,128)(2,1)}), bf16[8,32,640]{2,1,0:T(8,128)(2,1)S(1)}, u32[]{:S(2)}, u32[]{:S(2)}) %all-to-all-start.2) | async-done | bytes 327712 | tf_op jit(solution)/shard_map/all_to_all | solution.py:347
  94.2 0.0 copy-done.6
  94.2 1.2 copy-done.4
  95.4 1.7 %project.1 = (bf16[256,1024]{1,0:T(8,128)(2,1)}, bf16[16,16,2176]{2,1,0:T(8,128)(2,1)S(1)}, bf16[16,16,2176]{2,1,0:T(8,128)(2,1)S(1)}) custom-call(s32[1]{0:T(128)} %bitcast.core_ref, bf16[8,2,16,640]{3,2,1,0:T(8,128)(2,1)S(1)} %bitcast.30, f32[256,1024]{1,0:T(8,128)S(1)} %copy-done.4, bf16[256,1024]{1,0:T(8,128)(2,1)S(1)} %bitcast.29, ...), custom_call_target="tpu_custom_call" | custom-call | tf_op jit(solution)/shard_map/project/pallas_call | solution.py:335
  97.1 8.4 %collective-permute-start.1 = (bf16[16,16,2176]{2,1,0:T(8,128)(2,1)S(1)}, bf16[16,16,2176]{2,1,0:T(8,128)(2,1)S(1)}, u32[]{:S(2)}, u32[]{:S(2)}) collective-permute-start(bf16[16,16,2176]{2,1,0:T(8,128)(2,1)S(1)} %get-tuple-element.31), channel_id=1, source_target_pairs={{0,16},{16,0},{32,48},{48,32},{64,80},{80,64},{96,112},{112,96},{1... | collective-permute-start | bytes 3342344 | tf_op jit(solution)/shard_map/ppermute | solution.py:470
  105.5 2.4 %collective-permute-done.1 = bf16[16,16,2176]{2,1,0:T(8,128)(2,1)S(1)} collective-permute-done((bf16[16,16,2176]{2,1,0:T(8,128)(2,1)S(1)}, bf16[16,16,2176]{2,1,0:T(8,128)(2,1)S(1)}, u32[]{:S(2)}, u32[]{:S(2)}) %collective-permute-start.1) | collective-permute-done | bytes 1114144 | tf_op jit(solution)/shard_map/ppermute | solution.py:470
  107.9 0.3 add_convert_fusion
  108.1 19.0 %all_to_all.32 = bf16[4,4,16,2176]{3,2,1,0:T(8,128)(2,1)S(1)} all-to-all(bf16[4,4,16,2176]{3,2,1,0:T(8,128)(2,1)S(1)} %bitcast.39), channel_id=1, replica_groups={{0,128,256,384},{16,144,272,400},{32,160,288,416},{48,176,304,432},{64,..., dimensions={0} | all-to-all | bytes 2228224 | tf_op jit(solution)/shard_map/all_to_all | solution.py:347
  127.2 0.2 reduce_sum.12
  127.5 12.8 %all_to_all.33.parts_ref = bf16[4,16,2560]{2,1,0:T(8,128)(2,1)S(1)} all-to-all(bf16[4,16,2560]{2,1,0:T(8,128)(2,1)S(1)} %pad_maximum_fusion), channel_id=1, replica_groups={{0,32,64,96},{16,48,80,112},{128,160,192,224},{144,176,208,240},{256,28..., dimensions={0} | all-to-all | bytes 655360 | tf_op jit(solution)/shard_map/all_to_all | solution.py:347
  140.3 0.7 total.1
  140.9 11.3 %all_to_all.34.parts_ref = f32[8,16,512]{2,1,0:T(8,128)S(1)} all-to-all(f32[8,16,512]{2,1,0:T(8,128)S(1)} %get-tuple-element.34), channel_id=1, replica_groups={{0,16,128,144,256,272,384,400},{32,48,160,176,288,304,416,432},{64,80,1..., dimensions={0} | all-to-all | bytes 524288 | tf_op jit(solution)/shard_map/all_to_all | solution.py:347
  152.2 0.7 spread.1
  (23 shorter events, 0.2 us)
Async XLA Ops:
  0.6 31.0 %copy-start.5 = (bf16[1,256,1024]{2,1,0:T(8,128)(2,1)S(1)}, bf16[1,256,1024]{2,1,0:T(8,128)(2,1)}, u32[]{:S(2)}) copy-start(bf16[1,256,1024]{2,1,0:T(8,128)(2,1)} %param.15) | copy-start | bytes 1572868
  0.7 31.0 %copy-start = (bf16[1,256,1024]{2,1,0:T(8,128)(2,1)S(1)}, bf16[1,256,1024]{2,1,0:T(8,128)(2,1)}, u32[]{:S(2)}) copy-start(bf16[1,256,1024]{2,1,0:T(8,128)(2,1)} %param.12) | copy-start | bytes 1572868
  31.6 1.2 copy-start.1
  32.9 0.8 copy-start.7
  33.7 0.7 copy-start.8
  34.4 0.7 copy-start.10
  35.1 0.7 copy-start.11
  35.8 0.7 copy-start.12
  36.4 43.1 %copy-start.9 = (f32[512]{0:T(512)S(1)}, f32[512]{0:T(512)}, u32[]{:S(2)}) copy-start(f32[512]{0:T(512)} %param.22) | copy-start | bytes 6148
  36.4 43.1 %copy-start.13 = (f32[32]{0:T(128)S(1)}, f32[32]{0:T(128)}, u32[]{:S(2)}) copy-start(f32[32]{0:T(128)} %param.23) | copy-start | bytes 388
  55.0 1.0 copy-start.3
  70.1 24.0 %copy-start.2 = (bf16[512,1024]{1,0:T(8,128)(2,1)S(1)}, bf16[512,1024]{1,0:T(8,128)(2,1)}, u32[]{:S(2)}) copy-start(bf16[512,1024]{1,0:T(8,128)(2,1)} %w_xdt_ref.1) | copy-start | bytes 3145732
  70.1 24.0 %copy-start.6 = (bf16[32,1024]{1,0:T(8,128)(2,1)S(1)}, bf16[32,1024]{1,0:T(8,128)(2,1)}, u32[]{:S(2)}) copy-start(bf16[32,1024]{1,0:T(8,128)(2,1)} %w_xbc_ref.1) | copy-start | bytes 196612
  70.2 9.3 %collective-permute-start = (f32[32,640]{1,0:T(8,128)S(1)}, f32[32,640]{1,0:T(8,128)S(1)}, u32[]{:S(2)}, u32[]{:S(2)}) collective-permute-start(f32[32,640]{1,0:T(8,128)S(1)} %join.1.mine_ref), channel_id=1, source_target_pairs={{0,8},{1,9},{2,10},{3,11},{4,12},{5,13},{6,14},{7,15},{8,0},{9,1},... | collective-permute-start | bytes 245768 | tf_op jit(solution)/shard_map/ppermute | solution.py:426
  80.6 13.6 %all-to-all-start.2 = ((bf16[8,32,640]{2,1,0:T(8,128)(2,1)}), bf16[8,32,640]{2,1,0:T(8,128)(2,1)S(1)}, u32[]{:S(2)}, u32[]{:S(2)}) async-start(bf16[8,32,640]{2,1,0:T(8,128)(2,1)} %norm.1), calls=%async_computation.2 | async-start | bytes 655360 | tf_op jit(solution)/shard_map/all_to_all | solution.py:347
  94.2 1.2 copy-start.4
  97.1 10.8 %collective-permute-start.1 = (bf16[16,16,2176]{2,1,0:T(8,128)(2,1)S(1)}, bf16[16,16,2176]{2,1,0:T(8,128)(2,1)S(1)}, u32[]{:S(2)}, u32[]{:S(2)}) collective-permute-start(bf16[16,16,2176]{2,1,0:T(8,128)(2,1)S(1)} %get-tuple-element.31), channel_id=1, source_target_pairs={{0,16},{16,0},{32,48},{48,32},{64,80},{80,64},{96,112},{112,96},{1... | collective-permute-start | bytes 3342344 | tf_op jit(solution)/shard_map/ppermute | solution.py:470

commit v4 on v3

--- a/solution.py
+++ b/solution.py
@@ -33,7 +33,17 @@
     )
 
 
+def split_cores(core_ref, whole, keep_ref, send_ref):
+    first_core = core_ref[0] == 0
+    for pair in range(keep_ref.shape[0]):
+        even = whole[32 * pair : 32 * pair + 16]
+        odd = whole[32 * pair + 16 : 32 * pair + 32]
+        keep_ref[pair] = jnp.where(first_core, even, odd)
+        send_ref[pair] = jnp.where(first_core, odd, even)
+
+
 def scan_kernel(
+    core_ref,
     proj_ref,
     x_ref,
     gy_ref,
@@ -44,7 +54,8 @@
     dt_gain_ref,
     bc_gain_ref,
     normed_ref,
-    w_part_ref,
+    w_keep_ref,
+    w_send_ref,
     xg_ref,
     misc_ref,
     dt_s,
@@ -166,10 +177,10 @@
     dt_normed = lax.dot_general(
         pre_grad, w_ref[...], contract_cols, preferred_element_type=f32
     ).astype(bf16)
-    w_part_ref[...] = (
-        scale
-        * lax.dot_general(low_s[...], pre_grad, contract_rows, preferred_element_type=f32)
-    ).astype(bf16)
+    w_part = scale * lax.dot_general(
+        low_s[...], pre_grad, contract_rows, preferred_element_type=f32
+    )
+    split_cores(core_ref, w_part.astype(bf16), w_keep_ref, w_send_ref)
     source_sum = jnp.sum(src_s[...] * gy_s[...], axis=1, keepdims=True)
     b_grad = jnp.sum(b_acc[...], axis=2)
     c_grad = jnp.sum(c_acc[...], axis=2) + b_rows * source_sum
@@ -241,12 +252,11 @@
     x_ref,
     w_xdt_ref,
     w_xbc_ref,
-    w_part_ref,
     misc_ref,
     grad_x_ref,
     keep_ref,
     send_ref,
-    out_ref,
+    out_s,
     all_s,
     low_s,
     *,
@@ -264,11 +274,10 @@
     summed = xg_ref[...] + jnp.dot(dt_low, w_xdt_ref[...], preferred_element_type=f32)
     summed = summed + jnp.dot(bc_low, w_xbc_ref[...], preferred_element_type=f32)
     grad_x_ref[...] = summed.astype(bf16)
-    out_ref[:, :width] = (
+    out_s[:, :width] = (
         scale
         * lax.dot_general(dt_low, x_ref[...], contract_rows, preferred_element_type=f32)
     ).astype(bf16)
-    out_ref[:, width : 2 * width] = w_part_ref[...]
     state = bc_width // 2
     all_s[...] = jnp.zeros_like(all_s)
     all_s[: state + 2, :] = misc_ref[: state + 2, :]
@@ -288,15 +297,10 @@
     piece = rank // (lane // 2)
     all_s[gain_row : gain_row + 1, rank : rank + bc_width] = gains[piece : piece + 1, :bc_width]
     for piece in range(width // lane):
-        out_ref[piece * 64 : (piece + 1) * 64, 2 * width :] = all_s[
+        out_s[piece * 64 : (piece + 1) * 64, width:] = all_s[
             :, piece * lane : (piece + 1) * lane
         ].astype(bf16)
-    first_core = core_ref[0] == 0
-    for pair in range(keep_ref.shape[0]):
-        even = out_ref[32 * pair : 32 * pair + 16, :]
-        odd = out_ref[32 * pair + 16 : 32 * pair + 32, :]
-        keep_ref[pair] = jnp.where(first_core, even, odd)
-        send_ref[pair] = jnp.where(first_core, odd, even)
+    split_cores(core_ref, out_s, keep_ref, send_ref)
 
 
 def total_kernel(parts_ref, xdt_ref, dt_ref, own_ref):
@@ -377,17 +381,43 @@
         jnp.broadcast_to(own_proj[None], (tensor, own, columns)), "tensor"
     ).reshape(tokens, columns)
 
-    z_pair = 2
+    cores, z_size, z_pair = 2, 4, 2
+    x_size = dp // (cores * z_size)
     y_size = tensor // z_pair
+    per_device = rank // dp
+    core = (lax.axis_index("dp") % cores).astype(jnp.int32).reshape(1)
+    other_core = [(index, index ^ 1) for index in range(dp)]
+    z_stride, x_stride = cores, cores * z_size
+    along_x = [[x * x_stride + rest for x in range(x_size)] for rest in range(x_stride)]
+    along_z = [
+        [x * x_stride + z * z_stride + c for z in range(z_size)]
+        for x in range(x_size)
+        for c in range(cores)
+    ]
+    along_xc = [
+        [x * x_stride + z * z_stride + c for x in range(x_size) for c in range(cores)]
+        for z in range(z_size)
+    ]
     along_y = [[z * y_size + y for y in range(y_size)] for z in range(z_pair)]
+
+    def swap_cores(sent):
+        return lax.ppermute(sent, "dp", other_core)
+
+    def sum_over_x(kept, other):
+        both = (kept.astype(f32) + other.astype(f32)).astype(bf16)
+        blocks = both.reshape((x_size, z_size) + both.shape[1:])
+        return sum_low(send_to_all(blocks, "dp", along_x))
+
     rows = ((tokens, width), f32)
     by_token = (y_size, z_pair, own, columns)
-    normed_part, w_part, xg, misc = call(
+    half = (x_size * z_size, per_device)
+    normed_part, w_kept, w_sent, xg, misc = call(
         functools.partial(scan_kernel, wide_lanes=min(512, width), scale=scale),
         "scan",
         [
             (by_token, bf16),
-            ((rank, width), bf16),
+            (half + (width,), bf16),
+            (half + (width,), bf16),
             ((tokens, width), f32),
             ((state + 8, width), f32),
         ],
@@ -405,7 +435,8 @@
             rows,
             rows,
         ],
-        42,
+        60,
+        core,
         full_proj,
         x_rows,
         gy_rows,
@@ -423,9 +454,12 @@
     (mine,) = call(
         sum_kernel, "join", [((shared_rows, columns), f32)], [], 4, normed_parts
     )
+    mine, w_other = lax.optimization_barrier((mine, swap_cores(w_sent)))
+    w_by_x = sum_over_x(w_kept, w_other)
     other = lax.ppermute(
         mine, "tensor", [(index, (index + y_size) % tensor) for index in range(tensor)]
     )
+    other, w_by_x = lax.optimization_barrier((other, w_by_x))
     y_index = (lax.axis_index("tensor") % y_size).astype(jnp.int32).reshape(1)
     (own_low,) = call(
         functools.partial(norm_kernel, state=state),
@@ -441,50 +475,29 @@
         bc_gain_row,
     )
     low = send_to_all(own_low, "tensor", along_y).reshape(by_token)
-    cores, z_size = 2, 4
-    x_size = dp // (cores * z_size)
-    core = (lax.axis_index("dp") % cores).astype(jnp.int32).reshape(1)
-    per_device = rank // dp
-    row_width = 2 * width + lane
-    half = ((x_size * z_size, per_device, row_width), bf16)
+    half_row = (half + (width + lane,), bf16)
     grad_x, kept, sent = call(
         functools.partial(project_kernel, scale=scale),
         "project",
-        [((tokens, width), bf16), half, half],
+        [((tokens, width), bf16), half_row, half_row],
         [
-            ((rank, row_width), bf16),
+            ((rank, width + lane), bf16),
             ((64, width), f32),
             ((tokens, columns), bf16),
         ],
-        16,
+        60,
         core,
         low,
         xg,
         x_rows,
         w_xdt,
         w_xbc,
-        w_part,
         misc,
     )
-    other_core = [(index, index ^ 1) for index in range(dp)]
-    kept = (kept.astype(f32) + lax.ppermute(sent, "dp", other_core).astype(f32)).astype(bf16)
-    z_stride, x_stride = cores, cores * z_size
-    along_x = [[x * x_stride + rest for x in range(x_size)] for rest in range(x_stride)]
-    along_z = [
-        [x * x_stride + z * z_stride + c for z in range(z_size)]
-        for x in range(x_size)
-        for c in range(cores)
-    ]
-    along_xc = [
-        [x * x_stride + z * z_stride + c for x in range(x_size) for c in range(cores)]
-        for z in range(z_size)
-    ]
-    by_x = sum_low(
-        send_to_all(kept.reshape(x_size, z_size, per_device, row_width), "dp", along_x)
-    )
-    by_z = by_x[:, :, 2 * width :].transpose(1, 0, 2).reshape(1, per_device, z_size * lane)
+    by_x = sum_over_x(kept, swap_cores(sent))
+    by_z = by_x[:, :, width:].transpose(1, 0, 2).reshape(1, per_device, z_size * lane)
     by_z = jnp.broadcast_to(by_z, (z_size, per_device, z_size * lane))
-    by_z = jnp.concatenate([by_x[:, :, : 2 * width], by_z], axis=2)
+    by_z = jnp.concatenate([by_x[:, :, :width], w_by_x, by_z], axis=2)
     all_parts = send_to_all(by_z, "dp", along_z)
     shared = x_size * cores
     grad_w_xdt, grad_w_dt, own_total = call(

time: 154 us -> 153 us (level)
  blocking collectives: 87.3 us -> 51.2 us
  starting transfers between devices: 16.3 us -> 41.9 us
  waiting for transfers between devices: 17.3 us -> 26.6 us
  local copies, waits for them, and re-layouts: 7.14 us -> 1.6 us
  Pallas kernels: 22.8 us -> 26.6 us
  other arithmetic: 1.3 us -> 3.14 us
    all_to_all x5 -> x4, blocking collectives: 87.3 us -> 51.2 us  [send_to_all(): return lax.all_to_all(block, axis, 0, 0, axis_index_groups=groups)]
    all_to_all x1 -> x3, starting transfers between devices: 3.45 us -> 24.9 us  [send_to_all(): return lax.all_to_all(block, axis, 0, 0, axis_index_groups=groups)]
    all_to_all x1 -> x3, waiting for transfers between devices: 10.1 us -> 22.7 us  [send_to_all(): return lax.all_to_all(block, axis, 0, 0, axis_index_groups=groups)]
    unnamed x28 -> x10, local copies, waits for them, and re-layouts: 7 us -> 0.75 us
    ppermute x1 -> x2, starting transfers between devices: 8.39 us -> 12.7 us  [swap_cores(): return lax.ppermute(sent, 'dp', other_core)]
    pallas_call x6, Pallas kernels: 22.8 us -> 26.6 us  [call(): pl.pallas_call(kernel, out_shape=tuple((jax.ShapeDtypeStruct(shape, dtype...]
    ppermute x1, waiting for transfers between devices: 4.8 us -> 2.16 us  [body(): lax.ppermute(mine, 'tensor', [(index, (index + y_size) % tensor) for inde...]
    convert_element_type x1 -> x2, other arithmetic: 0.26 us -> 2.2 us  [sum_over_x(): both = (kept.astype(f32) + other.astype(f32)).astype(bf16)]
  transfers between devices with their start and end apart: 3 -> 6, of which waited for: 3 -> 5; matrix products, arithmetic and copies ran while one was open for 0% -> 0% of each run, Pallas kernels for 0% -> 0%
where the time goes in v4:
time: 153 us; the launch traced here: 152 us
  blocking collectives  51.2 us (33%)
  starting transfers between devices  41.9 us (27%)
  waiting for transfers between devices  26.6 us (17%)
  Pallas kernels  26.6 us (17%)
  other arithmetic  3.14 us (2%)
  local copies, waits for them, and re-layouts  1.6 us (1%)
    all_to_all x4, blocking collectives, send_to_all(): return lax.all_to_all(block, axis, 0, 0, axis_index_groups=groups)  51.2 us
    pallas_call x6, Pallas kernels, call(): pl.pallas_call(kernel, out_shape=tuple((jax.ShapeDtypeStruct(shape, dtype...  26.6 us
    all_to_all x3, starting transfers between devices, send_to_all(): return lax.all_to_all(block, axis, 0, 0, axis_index_groups=groups)  24.9 us
    all_to_all x3, waiting for transfers between devices, send_to_all(): return lax.all_to_all(block, axis, 0, 0, axis_index_groups=groups)  22.7 us
    ppermute x2, starting transfers between devices, swap_cores(): return lax.ppermute(sent, 'dp', other_core)  12.7 us
    ppermute x1, starting transfers between devices, body(): lax.ppermute(mine, 'tensor', [(index, (index + y_size) % tensor) for inde...  4.23 us
  transfers between devices with their start and end apart: 6, of which 5 were waited for; matrix products, arithmetic and copies ran while one was open for 0% of the time, Pallas kernels for 0%

profile of v4, /device:TPU:1, one launch (start us, length us, event | category | flops | bytes accessed | tf_op | source)
XLA Modules:
  0.0 151.8 jit_solution(10116073967653290301)
XLA Ops:
  0.7 0.1 pad.5.clone
  0.7 0.7 maximum_maximum_fusion
  1.5 0.8 broadcast_in_dim.20
  2.2 16.2 %all-to-all-start = ((bf16[16,16,640]{2,1,0:T(8,128)(2,1)}), bf16[16,16,640]{2,1,0:T(8,128)(2,1)S(1)}, u32[]{:S(2)}, u32[]{:S(2)}) async-start(bf16[16,16,640]{2,1,0:T(8,128)(2,1)} %broadcast_in_dim.20), calls=%async_computation | async-start | bytes 655360 | tf_op jit(solution)/shard_map/all_to_all | solution.py:351
  18.4 14.0 %all-to-all-done = bf16[16,16,640]{2,1,0:T(8,128)(2,1)S(1)} async-done(((bf16[16,16,640]{2,1,0:T(8,128)(2,1)}), bf16[16,16,640]{2,1,0:T(8,128)(2,1)S(1)}, u32[]{:S(2)}, u32[]{:S(2)}) %all-to-all-start) | async-done | bytes 327712 | tf_op jit(solution)/shard_map/all_to_all | solution.py:351
  32.5 0.7 copy-done
  33.2 21.0 %scan.1 = (bf16[8,2,16,640]{3,2,1,0:T(8,128)(2,1)}, bf16[16,16,1024]{2,1,0:T(8,128)(2,1)}, bf16[16,16,1024]{2,1,0:T(8,128)(2,1)}, f32[256,1024]{1,0:T(8,128)}, f32[24,1024]{1,0:T(8,128)}) custom-call(s32[1]{0:T(128)} %bitcast.core_ref, bf16[256,640]{1,0:T(8,128)(2,1)} %bitcast.27, bf16[256,1024]{1,0:T(8,128)(2,1)} %bitcast.34, bf16[256,1024]{1,0:T(8,128)(2,1)} %bitcast.37, ...), custom_call_target="tpu_custom_call" | custom-call | tf_op jit(solution)/shard_map/scan/pallas_call | solution.py:339
  54.2 4.6 %all-to-all-start.1 = ((bf16[8,32,640]{2,1,0:T(8,128)(2,1)}), bf16[8,32,640]{2,1,0:T(8,128)(2,1)S(1)}, u32[]{:S(2)}, u32[]{:S(2)}) async-start(bf16[8,32,640]{2,1,0:T(8,128)(2,1)} %bitcast.38), calls=%async_computation.1 | async-start | bytes 655360 | tf_op jit(solution)/shard_map/all_to_all | solution.py:351
  58.9 4.2 %collective-permute-start = (bf16[16,16,1024]{2,1,0:T(8,128)(2,1)}, bf16[16,16,1024]{2,1,0:T(8,128)(2,1)S(1)}, u32[]{:S(2)}, u32[]{:S(2)}) collective-permute-start(bf16[16,16,1024]{2,1,0:T(8,128)(2,1)} %get-tuple-element.31), channel_id=1, source_target_pairs={{0,16},{16,0},{32,48},{48,32},{64,80},{80,64},{96,112},{112,96},{1... | collective-permute-start | bytes 1572872 | tf_op jit(solution)/shard_map/ppermute | solution.py:404
  63.0 5.9 %all-to-all-done.1.parts_ref = bf16[8,32,640]{2,1,0:T(8,128)(2,1)S(1)} async-done(((bf16[8,32,640]{2,1,0:T(8,128)(2,1)}), bf16[8,32,640]{2,1,0:T(8,128)(2,1)S(1)}, u32[]{:S(2)}, u32[]{:S(2)}) %all-to-all-start.1) | async-done | bytes 327712 | tf_op jit(solution)/shard_map/all_to_all | solution.py:351
  69.0 0.0 collective-permute-done
  69.0 0.0 copy-done.4
  69.0 1.0 add_convert_fusion.1
  70.0 4.1 %all-to-all-start.2 = ((bf16[4,4,16,1024]{3,2,1,0:T(8,128)(2,1)}), bf16[4,4,16,1024]{3,2,1,0:T(8,128)(2,1)S(1)}, u32[]{:S(2)}, u32[]{:S(2)}) async-start(bf16[4,4,16,1024]{3,2,1,0:T(8,128)(2,1)} %bitcast.12), calls=%async_computation.2 | async-start | bytes 1048576 | tf_op jit(solution)/shard_map/all_to_all | solution.py:351
  74.2 4.2 %collective-permute-start.1 = (f32[32,640]{1,0:T(8,128)S(1)}, f32[32,640]{1,0:T(8,128)S(1)}, u32[]{:S(2)}, u32[]{:S(2)}) collective-permute-start(f32[32,640]{1,0:T(8,128)S(1)} %join.1.mine_ref), channel_id=1, source_target_pairs={{0,8},{1,9},{2,10},{3,11},{4,12},{5,13},{6,14},{7,15},{8,0},{9,1},... | collective-permute-start | bytes 245768 | tf_op jit(solution)/shard_map/ppermute | solution.py:459
  78.4 2.7 %all-to-all-done.2 = bf16[4,4,16,1024]{3,2,1,0:T(8,128)(2,1)S(1)} async-done(((bf16[4,4,16,1024]{3,2,1,0:T(8,128)(2,1)}), bf16[4,4,16,1024]{3,2,1,0:T(8,128)(2,1)S(1)}, u32[]{:S(2)}, u32[]{:S(2)}) %all-to-all-start.2) | async-done | bytes 524320 | tf_op jit(solution)/shard_map/all_to_all | solution.py:351
  81.1 0.1 reduce_sum.24
  81.2 2.2 %collective-permute-done.1.other_ref = f32[32,640]{1,0:T(8,128)S(1)} collective-permute-done((f32[32,640]{1,0:T(8,128)S(1)}, f32[32,640]{1,0:T(8,128)S(1)}, u32[]{:S(2)}, u32[]{:S(2)}) %collective-permute-start.1) | collective-permute-done | bytes 81952 | tf_op jit(solution)/shard_map/ppermute | solution.py:459
  83.4 0.0 copy-done.1
  83.4 0.0 copy-done.3
  83.4 0.3 norm.1
  83.7 13.2 %all_to_all.35 = bf16[8,32,640]{2,1,0:T(8,128)(2,1)} all-to-all(bf16[8,32,640]{2,1,0:T(8,128)(2,1)S(1)} %norm.1), channel_id=1, replica_groups={{0,1,2,3,4,5,6,7},{8,9,10,11,12,13,14,15},{16,17,18,19,20,21,22,23},{24..., dimensions={0} | all-to-all | bytes 655360 | tf_op jit(solution)/shard_map/all_to_all | solution.py:351
  96.9 3.8 %project.1 = (bf16[256,1024]{1,0:T(8,128)(2,1)}, bf16[16,16,1152]{2,1,0:T(8,128)(2,1)}, bf16[16,16,1152]{2,1,0:T(8,128)(2,1)}) custom-call(s32[1]{0:T(128)} %bitcast.core_ref, bf16[8,2,16,640]{3,2,1,0:T(8,128)(2,1)} %bitcast.36, f32[256,1024]{1,0:T(8,128)} %get-tuple-element.36.xg_ref, bf16[256,1024]{1,0:T(8,128)(2,1)} %bitcast.35, ...), custom_call_target="tpu_custom_call" | custom-call | tf_op jit(solution)/shard_map/project/pallas_call | solution.py:339
  100.7 8.5 %collective-permute-start.2 = (bf16[16,16,1152]{2,1,0:T(8,128)(2,1)}, bf16[16,16,1152]{2,1,0:T(8,128)(2,1)S(1)}, u32[]{:S(2)}, u32[]{:S(2)}) collective-permute-start(bf16[16,16,1152]{2,1,0:T(8,128)(2,1)} %get-tuple-element.40), channel_id=1, source_target_pairs={{0,16},{16,0},{32,48},{48,32},{64,80},{80,64},{96,112},{112,96},{1... | collective-permute-start | bytes 1769480 | tf_op jit(solution)/shard_map/ppermute | solution.py:404
  109.2 1.8 %collective-permute-done.2 = bf16[16,16,1152]{2,1,0:T(8,128)(2,1)S(1)} collective-permute-done((bf16[16,16,1152]{2,1,0:T(8,128)(2,1)}, bf16[16,16,1152]{2,1,0:T(8,128)(2,1)S(1)}, u32[]{:S(2)}, u32[]{:S(2)}) %collective-permute-start.2) | collective-permute-done | bytes 589856 | tf_op jit(solution)/shard_map/ppermute | solution.py:404
  111.0 1.2 add_convert_fusion
  112.2 13.9 %all_to_all.36 = bf16[4,4,16,1152]{3,2,1,0:T(8,128)(2,1)S(1)} all-to-all(bf16[4,4,16,1152]{3,2,1,0:T(8,128)(2,1)S(1)} %bitcast.33), channel_id=1, replica_groups={{0,128,256,384},{16,144,272,400},{32,160,288,416},{48,176,304,432},{64,..., dimensions={0} | all-to-all | bytes 1179648 | tf_op jit(solution)/shard_map/all_to_all | solution.py:351
  126.2 0.1 reduce_sum.25
  126.3 12.8 %all_to_all.37.parts_ref = bf16[4,16,2560]{2,1,0:T(8,128)(2,1)S(1)} all-to-all(bf16[4,16,2560]{2,1,0:T(8,128)(2,1)S(1)} %pad_maximum_fusion), channel_id=1, replica_groups={{0,32,64,96},{16,48,80,112},{128,160,192,224},{144,176,208,240},{256,28..., dimensions={0} | all-to-all | bytes 655360 | tf_op jit(solution)/shard_map/all_to_all | solution.py:351
  139.1 0.7 total.1
  139.8 11.3 %all_to_all.38.parts_ref = f32[8,16,512]{2,1,0:T(8,128)S(1)} all-to-all(f32[8,16,512]{2,1,0:T(8,128)S(1)} %get-tuple-element.44), channel_id=1, replica_groups={{0,16,128,144,256,272,384,400},{32,48,160,176,288,304,416,432},{64,80,1..., dimensions={0} | all-to-all | bytes 524288 | tf_op jit(solution)/shard_map/all_to_all | solution.py:351
  151.1 0.7 spread.1
  (12 shorter events, 0.1 us)
Async XLA Ops:
  2.2 30.3 %all-to-all-start = ((bf16[16,16,640]{2,1,0:T(8,128)(2,1)}), bf16[16,16,640]{2,1,0:T(8,128)(2,1)S(1)}, u32[]{:S(2)}, u32[]{:S(2)}) async-start(bf16[16,16,640]{2,1,0:T(8,128)(2,1)} %broadcast_in_dim.20), calls=%async_computation | async-start | bytes 655360 | tf_op jit(solution)/shard_map/all_to_all | solution.py:351
  32.5 0.7 copy-start
  54.2 14.8 %copy-start.4 = (bf16[16,16,1024]{2,1,0:T(8,128)(2,1)S(1)}, bf16[16,16,1024]{2,1,0:T(8,128)(2,1)}, u32[]{:S(2)}) copy-start(bf16[16,16,1024]{2,1,0:T(8,128)(2,1)} %get-tuple-element.33) | copy-start | bytes 1572868
  54.2 14.7 %all-to-all-start.1 = ((bf16[8,32,640]{2,1,0:T(8,128)(2,1)}), bf16[8,32,640]{2,1,0:T(8,128)(2,1)S(1)}, u32[]{:S(2)}, u32[]{:S(2)}) async-start(bf16[8,32,640]{2,1,0:T(8,128)(2,1)} %bitcast.38), calls=%async_computation.1 | async-start | bytes 655360 | tf_op jit(solution)/shard_map/all_to_all | solution.py:351
  58.9 10.2 %collective-permute-start = (bf16[16,16,1024]{2,1,0:T(8,128)(2,1)}, bf16[16,16,1024]{2,1,0:T(8,128)(2,1)S(1)}, u32[]{:S(2)}, u32[]{:S(2)}) collective-permute-start(bf16[16,16,1024]{2,1,0:T(8,128)(2,1)} %get-tuple-element.31), channel_id=1, source_target_pairs={{0,16},{16,0},{32,48},{48,32},{64,80},{80,64},{96,112},{112,96},{1... | collective-permute-start | bytes 1572872 | tf_op jit(solution)/shard_map/ppermute | solution.py:404
  70.0 13.3 %copy-start.1 = (bf16[16,16,640]{2,1,0:T(8,128)(2,1)S(1)}, bf16[16,16,640]{2,1,0:T(8,128)(2,1)}, u32[]{:S(2)}) copy-start(bf16[16,16,640]{2,1,0:T(8,128)(2,1)} %copy-done) | copy-start | bytes 983044
  70.0 13.3 %copy-start.2 = (f32[512]{0:T(512)S(1)}, f32[512]{0:T(512)}, u32[]{:S(2)}) copy-start(f32[512]{0:T(512)} %param.22) | copy-start | bytes 6148
  70.0 13.3 %copy-start.3 = (f32[32]{0:T(128)S(1)}, f32[32]{0:T(128)}, u32[]{:S(2)}) copy-start(f32[32]{0:T(128)} %param.23) | copy-start | bytes 388
  70.0 11.1 %all-to-all-start.2 = ((bf16[4,4,16,1024]{3,2,1,0:T(8,128)(2,1)}), bf16[4,4,16,1024]{3,2,1,0:T(8,128)(2,1)S(1)}, u32[]{:S(2)}, u32[]{:S(2)}) async-start(bf16[4,4,16,1024]{3,2,1,0:T(8,128)(2,1)} %bitcast.12), calls=%async_computation.2 | async-start | bytes 1048576 | tf_op jit(solution)/shard_map/all_to_all | solution.py:351
  74.2 9.2 %collective-permute-start.1 = (f32[32,640]{1,0:T(8,128)S(1)}, f32[32,640]{1,0:T(8,128)S(1)}, u32[]{:S(2)}, u32[]{:S(2)}) collective-permute-start(f32[32,640]{1,0:T(8,128)S(1)} %join.1.mine_ref), channel_id=1, source_target_pairs={{0,8},{1,9},{2,10},{3,11},{4,12},{5,13},{6,14},{7,15},{8,0},{9,1},... | collective-permute-start | bytes 245768 | tf_op jit(solution)/shard_map/ppermute | solution.py:459
  100.7 10.4 %collective-permute-start.2 = (bf16[16,16,1152]{2,1,0:T(8,128)(2,1)}, bf16[16,16,1152]{2,1,0:T(8,128)(2,1)S(1)}, u32[]{:S(2)}, u32[]{:S(2)}) collective-permute-start(bf16[16,16,1152]{2,1,0:T(8,128)(2,1)} %get-tuple-element.40), channel_id=1, source_target_pairs={{0,16},{16,0},{32,48},{48,32},{64,80},{80,64},{96,112},{112,96},{1... | collective-permute-start | bytes 1769480 | tf_op jit(solution)/shard_map/ppermute | solution.py:404

commit v5 on v4

--- a/solution.py
+++ b/solution.py
@@ -31,6 +31,15 @@
         (b_part, lax.rsqrt(jnp.maximum(b_square, state_floor)), b_square),
         (c_part, lax.rsqrt(jnp.maximum(c_square, state_floor)), c_square),
     )
+
+
+def pack_kernel(dt_ref, bc_ref, out_ref):
+    rank, bc_width = dt_ref.shape[1], bc_ref.shape[1]
+    spare = out_ref.shape[2] - rank - bc_width
+    for peer in range(out_ref.shape[0]):
+        out_ref[peer, :, :rank] = dt_ref[...]
+        out_ref[peer, :, rank : rank + bc_width] = bc_ref[...]
+        out_ref[peer, :, rank + bc_width :] = jnp.zeros((dt_ref.shape[0], spare), bf16)
 
 
 def split_cores(core_ref, whole, keep_ref, send_ref):
@@ -338,7 +347,10 @@
     in_smem = pl.BlockSpec(memory_space=pltpu.SMEM)
     return pl.pallas_call(
         kernel,
-        out_shape=tuple(jax.ShapeDtypeStruct(shape, dtype) for shape, dtype in outs),
+        out_shape=tuple(
+            pltpu.VMEM(out[0], out[1]) if len(out) > 2 else jax.ShapeDtypeStruct(*out)
+            for out in outs
+        ),
         in_specs=[in_smem if arg.dtype == jnp.int32 else in_vmem for arg in args],
         out_specs=tuple([in_vmem] * len(outs)),
         scratch_shapes=[pltpu.VMEM(shape, dtype) for shape, dtype in scratch],
@@ -374,12 +386,17 @@
     bc_gain_row = bc_gain.reshape(1, bc_width)
 
     columns = rank + lane
-    own_proj = jnp.concatenate(
-        [proj_dt[0], proj_bc[0], jnp.zeros((own, lane - bc_width), bf16)], axis=1
-    )
-    full_proj = send_to_all(
-        jnp.broadcast_to(own_proj[None], (tensor, own, columns)), "tensor"
-    ).reshape(tokens, columns)
+    local = True
+    (own_proj,) = call(
+        pack_kernel,
+        "pack",
+        [((tensor, own, columns), bf16, local)],
+        [],
+        4,
+        proj_dt[0],
+        proj_bc[0],
+    )
+    full_proj = send_to_all(own_proj, "tensor").reshape(tokens, columns)
 
     cores, z_size, z_pair = 2, 4, 2
     x_size = dp // (cores * z_size)
@@ -415,11 +432,11 @@
         functools.partial(scan_kernel, wide_lanes=min(512, width), scale=scale),
         "scan",
         [
-            (by_token, bf16),
-            (half + (width,), bf16),
-            (half + (width,), bf16),
-            ((tokens, width), f32),
-            ((state + 8, width), f32),
+            (by_token, bf16, local),
+            (half + (width,), bf16, local),
+            (half + (width,), bf16, local),
+            ((tokens, width), f32, local),
+            ((state + 8, width), f32, local),
         ],
         [
             rows,
@@ -435,7 +452,7 @@
             rows,
             rows,
         ],
-        60,
+        56,
         core,
         full_proj,
         x_rows,
@@ -452,7 +469,7 @@
         normed_part.reshape(y_size, shared_rows, columns), "tensor", along_y
     )
     (mine,) = call(
-        sum_kernel, "join", [((shared_rows, columns), f32)], [], 4, normed_parts
+        sum_kernel, "join", [((shared_rows, columns), f32, local)], [], 4, normed_parts
     )
     mine, w_other = lax.optimization_barrier((mine, swap_cores(w_sent)))
     w_by_x = sum_over_x(w_kept, w_other)
@@ -464,7 +481,7 @@
     (own_low,) = call(
         functools.partial(norm_kernel, state=state),
         "norm",
-        [((y_size, shared_rows, columns), bf16)],
+        [((y_size, shared_rows, columns), bf16, local)],
         [((shared_rows, columns), f32)],
         4,
         y_index,
@@ -479,13 +496,13 @@
     grad_x, kept, sent = call(
         functools.partial(project_kernel, scale=scale),
         "project",
-        [((tokens, width), bf16), half_row, half_row],
+        [((tokens, width), bf16), half_row + (local,), half_row + (local,)],
         [
             ((rank, width + lane), bf16),
             ((64, width), f32),
             ((tokens, columns), bf16),
         ],
-        60,
+        16,
         core,
         low,
         xg,
@@ -506,7 +523,7 @@
         [
             ((per_device, width), f32),
             ((per_device, width), f32),
-            ((shared, per_device, z_size * lane), f32),
+            ((shared, per_device, z_size * lane), f32, local),
         ],
         [],
         4,

time: 153 us -> 149 us (0.974)
    pallas_call x6 -> x7, Pallas kernels: 26.6 us -> 25.3 us  [call(): pl.pallas_call(kernel, out_shape=tuple((pltpu.VMEM(out[0], out[1]) if len...]
  transfers between devices with their start and end apart: 6 -> 6, of which waited for: 5 -> 5; matrix products, arithmetic and copies ran while one was open for 0% -> 1% of each run, Pallas kernels for 0% -> 0%
where the time goes in v5:
time: 149 us; the launch traced here: 148 us
  blocking collectives  51.1 us (34%)
  starting transfers between devices  41.1 us (28%)
  waiting for transfers between devices  25.4 us (17%)
  Pallas kernels  25.3 us (17%)
  other arithmetic  2.39 us (2%)
  local copies, waits for them, and re-layouts  2.17 us (1%)
    all_to_all x4, blocking collectives, send_to_all(): return lax.all_to_all(block, axis, 0, 0, axis_index_groups=groups)  51.1 us
    pallas_call x7, Pallas kernels, call(): pl.pallas_call(kernel, out_shape=tuple((pltpu.VMEM(out[0], out[1]) if len...  25.3 us
    all_to_all x3, starting transfers between devices, send_to_all(): return lax.all_to_all(block, axis, 0, 0, axis_index_groups=groups)  25 us
    all_to_all x3, waiting for transfers between devices, send_to_all(): return lax.all_to_all(block, axis, 0, 0, axis_index_groups=groups)  22.7 us
    ppermute x2, starting transfers between devices, swap_cores(): return lax.ppermute(sent, 'dp', other_core)  11.9 us
    ppermute x1, starting transfers between devices, body(): lax.ppermute(mine, 'tensor', [(index, (index + y_size) % tensor) for inde...  4.2 us
  transfers between devices with their start and end apart: 6, of which 5 were waited for; matrix products, arithmetic and copies ran while one was open for 1% of the time, Pallas kernels for 0%

profile of v5, /device:TPU:1, one launch (start us, length us, event | category | flops | bytes accessed | tf_op | source)
XLA Modules:
  0.0 148.2 jit_solution(2341522806751560007)
XLA Ops:
  0.7 0.7 copy-done.5
  1.4 0.7 copy-done.7
  2.0 0.8 pack.1
  2.8 16.2 %all-to-all-start = ((bf16[16,16,640]{2,1,0:T(8,128)(2,1)}), bf16[16,16,640]{2,1,0:T(8,128)(2,1)S(1)}, u32[]{:S(2)}, u32[]{:S(2)}) async-start(bf16[16,16,640]{2,1,0:T(8,128)(2,1)} %pack.1), calls=%async_computation | async-start | bytes 655360 | tf_op jit(solution)/shard_map/all_to_all | solution.py:363
  19.0 14.0 %all-to-all-done = bf16[16,16,640]{2,1,0:T(8,128)(2,1)S(1)} async-done(((bf16[16,16,640]{2,1,0:T(8,128)(2,1)}), bf16[16,16,640]{2,1,0:T(8,128)(2,1)S(1)}, u32[]{:S(2)}, u32[]{:S(2)}) %all-to-all-start) | async-done | bytes 327712 | tf_op jit(solution)/shard_map/all_to_all | solution.py:363
  33.1 0.7 copy-done
  33.8 21.2 %scan.1 = (bf16[8,2,16,640]{3,2,1,0:T(8,128)(2,1)}, bf16[16,16,1024]{2,1,0:T(8,128)(2,1)S(1)}, bf16[16,16,1024]{2,1,0:T(8,128)(2,1)S(1)}, f32[256,1024]{1,0:T(8,128)S(1)}, f32[24,1024]{1,0:T(8,128)S(1)}) custom-call(s32[1]{0:T(128)} %bitcast.core_ref, bf16[256,640]{1,0:T(8,128)(2,1)} %bitcast.27, bf16[256,1024]{1,0:T(8,128)(2,1)} %bitcast.29, ...), custom_call_target="tpu_custom_call" | custom-call | tf_op jit(solution)/shard_map/scan/pallas_call | solution.py:348
  55.0 4.5 %all-to-all-start.1 = ((bf16[8,32,640]{2,1,0:T(8,128)(2,1)}), bf16[8,32,640]{2,1,0:T(8,128)(2,1)S(1)}, u32[]{:S(2)}, u32[]{:S(2)}) async-start(bf16[8,32,640]{2,1,0:T(8,128)(2,1)} %bitcast.11), calls=%async_computation.1 | async-start | bytes 655360 | tf_op jit(solution)/shard_map/all_to_all | solution.py:363
  59.4 4.2 %collective-permute-start = (bf16[16,16,1024]{2,1,0:T(8,128)(2,1)S(1)}, bf16[16,16,1024]{2,1,0:T(8,128)(2,1)S(1)}, u32[]{:S(2)}, u32[]{:S(2)}) collective-permute-start(bf16[16,16,1024]{2,1,0:T(8,128)(2,1)S(1)} %get-tuple-element.31), channel_id=1, source_target_pairs={{0,16},{16,0},{32,48},{48,32},{64,80},{80,64},{96,112},{112,96},{1... | collective-permute-start | bytes 1572872 | tf_op jit(solution)/shard_map/ppermute | solution.py:421
  63.6 6.0 %all-to-all-done.1.parts_ref = bf16[8,32,640]{2,1,0:T(8,128)(2,1)S(1)} async-done(((bf16[8,32,640]{2,1,0:T(8,128)(2,1)}), bf16[8,32,640]{2,1,0:T(8,128)(2,1)S(1)}, u32[]{:S(2)}, u32[]{:S(2)}) %all-to-all-start.1) | async-done | bytes 327712 | tf_op jit(solution)/shard_map/all_to_all | solution.py:363
  69.6 0.0 collective-permute-done
  69.6 1.0 add_convert_fusion.1
  70.6 4.3 %all-to-all-start.2 = ((bf16[4,4,16,1024]{3,2,1,0:T(8,128)(2,1)}), bf16[4,4,16,1024]{3,2,1,0:T(8,128)(2,1)}, u32[]{:S(2)}, u32[]{:S(2)}) async-start(bf16[4,4,16,1024]{3,2,1,0:T(8,128)(2,1)} %bitcast.12), calls=%async_computation.2 | async-start | bytes 1048576 | tf_op jit(solution)/shard_map/all_to_all | solution.py:363
  74.9 4.2 %collective-permute-start.1 = (f32[32,640]{1,0:T(8,128)S(1)}, f32[32,640]{1,0:T(8,128)S(1)}, u32[]{:S(2)}, u32[]{:S(2)}) collective-permute-start(f32[32,640]{1,0:T(8,128)S(1)} %join.1.mine_ref), channel_id=1, source_target_pairs={{0,8},{1,9},{2,10},{3,11},{4,12},{5,13},{6,14},{7,15},{8,0},{9,1},... | collective-permute-start | bytes 245768 | tf_op jit(solution)/shard_map/ppermute | solution.py:476
  79.1 0.0 copy-start.2
  79.2 0.0 copy-start.3
  79.2 0.0 copy-start.4
  79.2 2.7 %all-to-all-done.2 = bf16[4,4,16,1024]{3,2,1,0:T(8,128)(2,1)} async-done(((bf16[4,4,16,1024]{3,2,1,0:T(8,128)(2,1)}), bf16[4,4,16,1024]{3,2,1,0:T(8,128)(2,1)}, u32[]{:S(2)}, u32[]{:S(2)}) %all-to-all-start.2) | async-done | bytes 524320 | tf_op jit(solution)/shard_map/all_to_all | solution.py:363
  81.9 1.1 reduce_sum.24
  83.0 1.1 collective-permute-done.1.other_ref
  84.1 0.3 norm.1
  84.5 13.0 %all_to_all.35 = bf16[8,32,640]{2,1,0:T(8,128)(2,1)S(1)} all-to-all(bf16[8,32,640]{2,1,0:T(8,128)(2,1)S(1)} %norm.1), channel_id=1, replica_groups={{0,1,2,3,4,5,6,7},{8,9,10,11,12,13,14,15},{16,17,18,19,20,21,22,23},{24..., dimensions={0} | all-to-all | bytes 655360 | tf_op jit(solution)/shard_map/all_to_all | solution.py:363
  97.5 1.6 %project.1 = (bf16[256,1024]{1,0:T(8,128)(2,1)}, bf16[16,16,1152]{2,1,0:T(8,128)(2,1)S(1)}, bf16[16,16,1152]{2,1,0:T(8,128)(2,1)S(1)}) custom-call(s32[1]{0:T(128)} %bitcast.core_ref, bf16[8,2,16,640]{3,2,1,0:T(8,128)(2,1)S(1)} %bitcast.31, f32[256,1024]{1,0:T(8,128)S(1)} %get-tuple-element.36.xg_ref, bf16[256,1024]{1,0:T(8,128)(2,1)S(1)} %bitcast.30, ...), custom_call_target="tpu_custom_call" | custom-call | tf_op jit(solution)/shard_map/project/pallas_call | solution.py:348
  99.1 7.8 %collective-permute-start.2 = (bf16[16,16,1152]{2,1,0:T(8,128)(2,1)S(1)}, bf16[16,16,1152]{2,1,0:T(8,128)(2,1)S(1)}, u32[]{:S(2)}, u32[]{:S(2)}) collective-permute-start(bf16[16,16,1152]{2,1,0:T(8,128)(2,1)S(1)} %get-tuple-element.40), channel_id=1, source_target_pairs={{0,16},{16,0},{32,48},{48,32},{64,80},{80,64},{96,112},{112,96},{1... | collective-permute-start | bytes 1769480 | tf_op jit(solution)/shard_map/ppermute | solution.py:421
  106.9 1.6 %collective-permute-done.2 = bf16[16,16,1152]{2,1,0:T(8,128)(2,1)S(1)} collective-permute-done((bf16[16,16,1152]{2,1,0:T(8,128)(2,1)S(1)}, bf16[16,16,1152]{2,1,0:T(8,128)(2,1)S(1)}, u32[]{:S(2)}, u32[]{:S(2)}) %collective-permute-start.2) | collective-permute-done | bytes 589856 | tf_op jit(solution)/shard_map/ppermute | solution.py:421
  108.5 0.1 add_convert_fusion
  108.7 13.9 %all_to_all.36 = bf16[4,4,16,1152]{3,2,1,0:T(8,128)(2,1)S(1)} all-to-all(bf16[4,4,16,1152]{3,2,1,0:T(8,128)(2,1)S(1)} %bitcast.38), channel_id=1, replica_groups={{0,128,256,384},{16,144,272,400},{32,160,288,416},{48,176,304,432},{64,..., dimensions={0} | all-to-all | bytes 1179648 | tf_op jit(solution)/shard_map/all_to_all | solution.py:363
  122.6 0.1 reduce_sum.25
  122.8 12.8 %all_to_all.37.parts_ref = bf16[4,16,2560]{2,1,0:T(8,128)(2,1)S(1)} all-to-all(bf16[4,16,2560]{2,1,0:T(8,128)(2,1)S(1)} %pad_maximum_fusion), channel_id=1, replica_groups={{0,32,64,96},{16,48,80,112},{128,160,192,224},{144,176,208,240},{256,28..., dimensions={0} | all-to-all | bytes 655360 | tf_op jit(solution)/shard_map/all_to_all | solution.py:363
  135.6 0.7 total.1
  136.2 11.3 %all_to_all.38.parts_ref = f32[8,16,512]{2,1,0:T(8,128)S(1)} all-to-all(f32[8,16,512]{2,1,0:T(8,128)S(1)} %get-tuple-element.44), channel_id=1, replica_groups={{0,16,128,144,256,272,384,400},{32,48,160,176,288,304,416,432},{64,80,1..., dimensions={0} | all-to-all | bytes 524288 | tf_op jit(solution)/shard_map/all_to_all | solution.py:363
  147.5 0.7 spread.1
  (17 shorter events, 0.1 us)
Async XLA Ops:
  0.6 0.7 copy-start.5
  1.4 0.7 copy-start.7
  2.8 30.3 %all-to-all-start = ((bf16[16,16,640]{2,1,0:T(8,128)(2,1)}), bf16[16,16,640]{2,1,0:T(8,128)(2,1)S(1)}, u32[]{:S(2)}, u32[]{:S(2)}) async-start(bf16[16,16,640]{2,1,0:T(8,128)(2,1)} %pack.1), calls=%async_computation | async-start | bytes 655360 | tf_op jit(solution)/shard_map/all_to_all | solution.py:363
  33.1 0.7 copy-start
  55.0 14.6 %all-to-all-start.1 = ((bf16[8,32,640]{2,1,0:T(8,128)(2,1)}), bf16[8,32,640]{2,1,0:T(8,128)(2,1)S(1)}, u32[]{:S(2)}, u32[]{:S(2)}) async-start(bf16[8,32,640]{2,1,0:T(8,128)(2,1)} %bitcast.11), calls=%async_computation.1 | async-start | bytes 655360 | tf_op jit(solution)/shard_map/all_to_all | solution.py:363
  59.4 10.2 %collective-permute-start = (bf16[16,16,1024]{2,1,0:T(8,128)(2,1)S(1)}, bf16[16,16,1024]{2,1,0:T(8,128)(2,1)S(1)}, u32[]{:S(2)}, u32[]{:S(2)}) collective-permute-start(bf16[16,16,1024]{2,1,0:T(8,128)(2,1)S(1)} %get-tuple-element.31), channel_id=1, source_target_pairs={{0,16},{16,0},{32,48},{48,32},{64,80},{80,64},{96,112},{112,96},{1... | collective-permute-start | bytes 1572872 | tf_op jit(solution)/shard_map/ppermute | solution.py:421
  70.6 13.5 %copy-start.1 = (bf16[16,16,640]{2,1,0:T(8,128)(2,1)S(1)}, bf16[16,16,640]{2,1,0:T(8,128)(2,1)}, u32[]{:S(2)}) copy-start(bf16[16,16,640]{2,1,0:T(8,128)(2,1)} %copy-done) | copy-start | bytes 983044
  70.6 13.5 %copy-start.6 = (f32[512]{0:T(512)S(1)}, f32[512]{0:T(512)}, u32[]{:S(2)}) copy-start(f32[512]{0:T(512)} %param.22) | copy-start | bytes 6148
  70.6 13.5 %copy-start.8 = (f32[32]{0:T(128)S(1)}, f32[32]{0:T(128)}, u32[]{:S(2)}) copy-start(f32[32]{0:T(128)} %param.23) | copy-start | bytes 388
  70.6 11.3 %all-to-all-start.2 = ((bf16[4,4,16,1024]{3,2,1,0:T(8,128)(2,1)}), bf16[4,4,16,1024]{3,2,1,0:T(8,128)(2,1)}, u32[]{:S(2)}, u32[]{:S(2)}) async-start(bf16[4,4,16,1024]{3,2,1,0:T(8,128)(2,1)} %bitcast.12), calls=%async_computation.2 | async-start | bytes 1048576 | tf_op jit(solution)/shard_map/all_to_all | solution.py:363
  74.9 9.2 %collective-permute-start.1 = (f32[32,640]{1,0:T(8,128)S(1)}, f32[32,640]{1,0:T(8,128)S(1)}, u32[]{:S(2)}, u32[]{:S(2)}) collective-permute-start(f32[32,640]{1,0:T(8,128)S(1)} %join.1.mine_ref), channel_id=1, source_target_pairs={{0,8},{1,9},{2,10},{3,11},{4,12},{5,13},{6,14},{7,15},{8,0},{9,1},... | collective-permute-start | bytes 245768 | tf_op jit(solution)/shard_map/ppermute | solution.py:476
  79.1 18.4 %copy-start.2 = (bf16[1,256,1024]{2,1,0:T(8,128)(2,1)S(1)}, bf16[1,256,1024]{2,1,0:T(8,128)(2,1)}, u32[]{:S(2)}) copy-start(bf16[1,256,1024]{2,1,0:T(8,128)(2,1)} %param.12) | copy-start | bytes 1572868
  79.2 18.4 %copy-start.3 = (bf16[512,1024]{1,0:T(8,128)(2,1)S(1)}, bf16[512,1024]{1,0:T(8,128)(2,1)}, u32[]{:S(2)}) copy-start(bf16[512,1024]{1,0:T(8,128)(2,1)} %w_xdt_ref.1) | copy-start | bytes 3145732
  79.2 18.4 %copy-start.4 = (bf16[32,1024]{1,0:T(8,128)(2,1)S(1)}, bf16[32,1024]{1,0:T(8,128)(2,1)}, u32[]{:S(2)}) copy-start(bf16[32,1024]{1,0:T(8,128)(2,1)} %w_xbc_ref.1) | copy-start | bytes 196612
  99.1 9.4 %collective-permute-start.2 = (bf16[16,16,1152]{2,1,0:T(8,128)(2,1)S(1)}, bf16[16,16,1152]{2,1,0:T(8,128)(2,1)S(1)}, u32[]{:S(2)}, u32[]{:S(2)}) collective-permute-start(bf16[16,16,1152]{2,1,0:T(8,128)(2,1)S(1)} %get-tuple-element.40), channel_id=1, source_target_pairs={{0,16},{16,0},{32,48},{48,32},{64,80},{80,64},{96,112},{112,96},{1... | collective-permute-start | bytes 1769480 | tf_op jit(solution)/shard_map/ppermute | solution.py:421

commit v6 on v5

--- a/solution.py
+++ b/solution.py
@@ -33,9 +33,17 @@
     )
 
 
-def pack_kernel(dt_ref, bc_ref, out_ref):
+def pack_kernel(dt_in, bc_in, out_ref, dt_ref, bc_ref, arrived):
     rank, bc_width = dt_ref.shape[1], bc_ref.shape[1]
     spare = out_ref.shape[2] - rank - bc_width
+    arrivals = [
+        pltpu.make_async_copy(dt_in, dt_ref, arrived.at[0]),
+        pltpu.make_async_copy(bc_in, bc_ref, arrived.at[1]),
+    ]
+    for copy in arrivals:
+        copy.start()
+    for copy in arrivals:
+        copy.wait()
     for peer in range(out_ref.shape[0]):
         out_ref[peer, :, :rank] = dt_ref[...]
         out_ref[peer, :, rank : rank + bc_width] = bc_ref[...]
@@ -54,14 +62,14 @@
 def scan_kernel(
     core_ref,
     proj_ref,
-    x_ref,
-    gy_ref,
-    w_ref,
-    bias_ref,
-    alog_ref,
-    skip_ref,
-    dt_gain_ref,
-    bc_gain_ref,
+    dt_gain_in,
+    bc_gain_in,
+    w_in,
+    bias_in,
+    x_in,
+    gy_in,
+    alog_in,
+    skip_in,
     normed_ref,
     w_keep_ref,
     w_send_ref,
@@ -79,23 +87,60 @@
     c_acc,
     s1_s,
     s2_s,
+    dt_gain_ref,
+    bc_gain_ref,
+    w_ref,
+    bias_ref,
+    x_ref,
+    gy_ref,
+    alog_ref,
+    skip_ref,
+    arrived,
     *,
-    wide_lanes,
     scale,
+    forward_lanes=512,
+    forward_rows=32,
+    backward_lanes=512,
+    backward_rows=16,
 ):
     tokens, width = x_ref.shape
     state = alog_ref.shape[0]
     rank = w_ref.shape[0]
+    arrivals = [
+        pltpu.make_async_copy(source, held, arrived.at[index])
+        for index, (source, held) in enumerate(
+            (
+                (dt_gain_in, dt_gain_ref),
+                (bc_gain_in, bc_gain_ref),
+                (w_in, w_ref),
+                (bias_in, bias_ref),
+                (x_in, x_ref),
+                (gy_in, gy_ref),
+                (alog_in, alog_ref),
+                (skip_in, skip_ref),
+            )
+        )
+    ]
+    for copy in arrivals:
+        copy.start()
+    b_acc[...] = jnp.zeros_like(b_acc)
+    c_acc[...] = jnp.zeros_like(c_acc)
     dt_norm, b_norm, c_norm = inverse_norms(proj_ref[...].astype(f32), rank, state)
+    arrivals[0].wait()
+    arrivals[1].wait()
     low_s[...] = (dt_norm[0] * dt_norm[1] * dt_gain_ref[...]).astype(bf16)
     b_rows = b_norm[0] * b_norm[1] * bc_gain_ref[:, :state]
     c_rows = c_norm[0] * c_norm[1] * bc_gain_ref[:, state:]
     bcb_s[:, :state] = jnp.broadcast_to(b_rows[:, :, None], (tokens, state, lane))
     bcb_s[:, state:] = jnp.broadcast_to(c_rows[:, :, None], (tokens, state, lane))
+    arrivals[2].wait()
+    arrivals[3].wait()
     pre = jnp.dot(low_s[...], w_ref[...], preferred_element_type=f32) + bias_ref[...]
     small = jnp.exp(-jnp.abs(pre))
     dt_rows = jnp.maximum(pre, 0.0) + jnp.log1p(small)
     sig_s[...] = jnp.where(pre >= 0, 1.0, small) / (1.0 + small)
+    for copy in arrivals[4:]:
+        copy.wait()
     x_float = x_ref[...].astype(f32)
     gy_float = gy_ref[...].astype(f32)
     dt_s[...] = dt_rows
@@ -103,17 +148,13 @@
     src_s[...] = dt_rows * x_float
     a_mat = -jnp.exp(alog_ref[...])
     a2_s[...] = a_mat * log2_e
-    b_acc[...] = jnp.zeros_like(b_acc)
-    c_acc[...] = jnp.zeros_like(c_acc)
-    reps = wide_lanes // lane
-
-    def widen(part):
-        return jnp.concatenate([part] * reps, axis=1)
+    def widen(part, width):
+        return jnp.concatenate([part] * (width // lane), axis=1)
 
     def fold(part):
         total = part[:, :lane]
-        for rep in range(1, reps):
-            total = total + part[:, rep * lane : (rep + 1) * lane]
+        for start in range(lane, part.shape[1], lane):
+            total = total + part[:, start : start + lane]
         return total
 
     def fold_states(part):
@@ -122,56 +163,63 @@
             total = total + part[rep * 8 : (rep + 1) * 8]
         return total
 
-    row_ids = lax.broadcasted_iota(jnp.int32, (8, wide_lanes), 0)
-
     def join_rows(early, late, level):
-        mine = (row_ids & level) == 0
+        mine = (lax.broadcasted_iota(jnp.int32, early.shape, 0) & level) == 0
         kept = jnp.where(mine, early, late)
         moved = jnp.where(mine, late, early)
         return kept + pltpu.roll(moved, 8 - level, 0)
 
-    for group in range(width // wide_lanes):
-        cols = slice(group * wide_lanes, (group + 1) * wide_lanes)
+    wide = min(forward_lanes, width)
+    for group in range(width // wide):
+        cols = slice(group * wide, (group + 1) * wide)
 
         def forward(block, held):
             a2 = a2_s[:, cols]
-            for offset in range(8):
-                t = block * 8 + offset
+            for offset in range(forward_rows):
+                t = block * forward_rows + offset
                 decayed = jnp.exp2(dt_s[pl.ds(t, 1), cols] * a2) * held
                 u_s[pl.ds(t, 1), :, cols] = decayed[None]
                 c_acc[pl.ds(t, 1)] += fold(decayed * gy_s[pl.ds(t, 1), cols])[None]
-                held = decayed + src_s[pl.ds(t, 1), cols] * widen(bcb_s[t, :state])
+                held = decayed + src_s[pl.ds(t, 1), cols] * widen(bcb_s[t, :state], wide)
             return held
 
-        zeros = jnp.zeros((state, wide_lanes), f32)
-        lax.fori_loop(0, tokens // 8, forward, zeros)
+        lax.fori_loop(0, tokens // forward_rows, forward, jnp.zeros((state, wide), f32))
+
+    wide = min(backward_lanes, width)
+    for group in range(width // wide):
+        cols = slice(group * wide, (group + 1) * wide)
 
         def backward(step, carry):
             later, a_total = carry
-            block = tokens // 8 - 1 - step
             a2 = a2_s[:, cols]
-            waiting = {}
-            for offset in range(7, -1, -1):
-                t = block * 8 + offset
-                dt_now = dt_s[pl.ds(t, 1), cols]
-                adjoint = widen(bcb_s[t, state:]) * gy_s[pl.ds(t, 1), cols] + later
-                through = adjoint * u_s[t, :, cols]
-                first = fold_states(adjoint * widen(bcb_s[t, :state]))
-                second = fold_states(through * a2)
-                level = 1
-                while level in waiting:
-                    later_first, later_second = waiting.pop(level)
-                    first = join_rows(first, later_first, level)
-                    second = join_rows(second, later_second, level)
-                    level *= 2
-                waiting[level] = (first, second)
-                b_acc[pl.ds(t, 1)] += fold(adjoint * src_s[pl.ds(t, 1), cols])[None]
-                a_total = a_total + dt_now * through
-                later = jnp.exp2(dt_now * a2) * adjoint
-            s1_s[pl.ds(block * 8, 8), cols], s2_s[pl.ds(block * 8, 8), cols] = waiting[8]
+            for part in range(backward_rows // 8 - 1, -1, -1):
+                first_row = tokens - (step + 1) * backward_rows + part * 8
+                waiting = {}
+                for offset in range(7, -1, -1):
+                    t = first_row + offset
+                    dt_now = dt_s[pl.ds(t, 1), cols]
+                    adjoint = (
+                        widen(bcb_s[t, state:], wide) * gy_s[pl.ds(t, 1), cols] + later
+                    )
+                    through = adjoint * u_s[t, :, cols]
+                    first = fold_states(adjoint * widen(bcb_s[t, :state], wide))
+                    second = fold_states(through * a2)
+                    level = 1
+                    while level in waiting:
+                        later_first, later_second = waiting.pop(level)
+                        first = join_rows(first, later_first, level)
+                        second = join_rows(second, later_second, level)
+                        level *= 2
+                    waiting[level] = (first, second)
+                    b_acc[pl.ds(t, 1)] += fold(adjoint * src_s[pl.ds(t, 1), cols])[None]
+                    a_total = a_total + dt_now * through
+                    later = jnp.exp2(dt_now * a2) * adjoint
+                rows = pl.ds(pl.multiple_of(first_row, 8), 8)
+                s1_s[rows, cols], s2_s[rows, cols] = waiting[8]
             return later, a_total
 
-        _, a_total = lax.fori_loop(0, tokens // 8, backward, (zeros, zeros))
+        zeros = jnp.zeros((state, wide), f32)
+        _, a_total = lax.fori_loop(0, tokens // backward_rows, backward, (zeros, zeros))
         misc_ref[:state, cols] = (scale / log2_e) * (a_total * a2_s[:, cols])
 
     s1 = s1_s[...]
@@ -254,35 +302,47 @@
         out_ref[peer] = packed
 
 
+def to_tokens(low_ref, low_s):
+    y_size, z_size, own, _ = low_ref.shape
+    for y in range(y_size):
+        for z in range(z_size):
+            start = (z * y_size + y) * own
+            low_s[start : start + own, :] = low_ref[y, z]
+
+
+def grad_x_kernel(low_ref, xg_ref, w_xdt_ref, w_xbc_ref, grad_x_ref, low_s):
+    rank = w_xdt_ref.shape[0]
+    bc_width = w_xbc_ref.shape[0]
+    to_tokens(low_ref, low_s)
+    summed = xg_ref[...] + jnp.dot(
+        low_s[:, :rank], w_xdt_ref[...], preferred_element_type=f32
+    )
+    summed = summed + jnp.dot(
+        low_s[:, rank : rank + bc_width], w_xbc_ref[...], preferred_element_type=f32
+    )
+    grad_x_ref[...] = summed.astype(bf16)
+
+
 def project_kernel(
     core_ref,
     low_ref,
-    xg_ref,
     x_ref,
-    w_xdt_ref,
-    w_xbc_ref,
     misc_ref,
-    grad_x_ref,
     keep_ref,
     send_ref,
     out_s,
     all_s,
     low_s,
     *,
+    rank,
+    bc_width,
     scale,
 ):
-    rank, width = w_xdt_ref.shape
-    bc_width = w_xbc_ref.shape[0]
+    width = x_ref.shape[1]
     y_size, z_size, own, _ = low_ref.shape
-    for y in range(y_size):
-        for z in range(z_size):
-            start = (z * y_size + y) * own
-            low_s[start : start + own, :] = low_ref[y, z]
+    to_tokens(low_ref, low_s)
     dt_low = low_s[:, :rank]
     bc_low = low_s[:, rank : rank + bc_width]
-    summed = xg_ref[...] + jnp.dot(dt_low, w_xdt_ref[...], preferred_element_type=f32)
-    summed = summed + jnp.dot(bc_low, w_xbc_ref[...], preferred_element_type=f32)
-    grad_x_ref[...] = summed.astype(bf16)
     out_s[:, :width] = (
         scale
         * lax.dot_general(dt_low, x_ref[...], contract_rows, preferred_element_type=f32)
@@ -343,20 +403,24 @@
     bc_gain_ref[...] = all_s[gain_row : gain_row + 1, rank : rank + bc_width]
 
 
-def call(kernel, name, outs, scratch, limit_mib, *args):
+def call(kernel, name, outs, scratch, limit_mib, *args, far=()):
     in_smem = pl.BlockSpec(memory_space=pltpu.SMEM)
+    in_hbm = pl.BlockSpec(memory_space=pltpu.HBM)
     return pl.pallas_call(
         kernel,
         out_shape=tuple(
             pltpu.VMEM(out[0], out[1]) if len(out) > 2 else jax.ShapeDtypeStruct(*out)
             for out in outs
         ),
-        in_specs=[in_smem if arg.dtype == jnp.int32 else in_vmem for arg in args],
+        in_specs=[in_smem if arg.dtype == jnp.int32 else in_vmem for arg in args]
+        + [in_hbm] * len(far),
         out_specs=tuple([in_vmem] * len(outs)),
-        scratch_shapes=[pltpu.VMEM(shape, dtype) for shape, dtype in scratch],
+        scratch_shapes=[pltpu.VMEM(shape, dtype) for shape, dtype in scratch]
+        + [pltpu.VMEM(arg.shape, arg.dtype) for arg in far]
+        + ([pltpu.SemaphoreType.DMA((len(far),))] if far else []),
         compiler_params=pltpu.CompilerParams(vmem_limit_bytes=limit_mib * 2**20),
         name=name,
-    )(*args)
+    )(*args, *[pltpu.with_memory_space_constraint(arg, pltpu.HBM) for arg in far])
 
 
 def send_to_all(block, axis, groups=None):
@@ -393,8 +457,7 @@
         [((tensor, own, columns), bf16, local)],
         [],
         4,
-        proj_dt[0],
-        proj_bc[0],
+        far=(proj_dt[0], proj_bc[0]),
     )
     full_proj = send_to_all(own_proj, "tensor").reshape(tokens, columns)
 
@@ -429,7 +492,7 @@
     by_token = (y_size, z_pair, own, columns)
     half = (x_size * z_size, per_device)
     normed_part, w_kept, w_sent, xg, misc = call(
-        functools.partial(scan_kernel, wide_lanes=min(512, width), scale=scale),
+        functools.partial(scan_kernel, scale=scale),
         "scan",
         [
             (by_token, bf16, local),
@@ -452,17 +515,10 @@
             rows,
             rows,
         ],
-        56,
+        44,
         core,
         full_proj,
-        x_rows,
-        gy_rows,
-        w_dt,
-        bias_row,
-        a_log,
-        skip_row,
-        dt_gain_row,
-        bc_gain_row,
+        far=(dt_gain_row, bc_gain_row, w_dt, bias_row, x_rows, gy_rows, a_log, skip_row),
     )
     shared_rows = z_pair * own
     normed_parts = send_to_all(
@@ -493,10 +549,10 @@
     )
     low = send_to_all(own_low, "tensor", along_y).reshape(by_token)
     half_row = (half + (width + lane,), bf16)
-    grad_x, kept, sent = call(
-        functools.partial(project_kernel, scale=scale),
+    kept, sent = call(
+        functools.partial(project_kernel, rank=rank, bc_width=bc_width, scale=scale),
         "project",
-        [((tokens, width), bf16), half_row + (local,), half_row + (local,)],
+        [half_row + (local,), half_row + (local,)],
         [
             ((rank, width + lane), bf16),
             ((64, width), f32),
@@ -505,13 +561,22 @@
         16,
         core,
         low,
+        x_rows,
+        misc,
+    )
+    (grad_x,) = call(
+        grad_x_kernel,
+        "grad_x",
+        [((tokens, width), bf16)],
+        [((tokens, columns), bf16)],
+        16,
+        low,
         xg,
-        x_rows,
         w_xdt,
         w_xbc,
-        misc,
-    )
-    by_x = sum_over_x(kept, swap_cores(sent))
+    )
+    swapped, grad_x = lax.optimization_barrier((swap_cores(sent), grad_x))
+    by_x = sum_over_x(kept, swapped)
     by_z = by_x[:, :, width:].transpose(1, 0, 2).reshape(1, per_device, z_size * lane)
     by_z = jnp.broadcast_to(by_z, (z_size, per_device, z_size * lane))
     by_z = jnp.concatenate([by_x[:, :, :width], w_by_x, by_z], axis=2)

time: 149 us -> 146 us (0.980)
  local copies, waits for them, and re-layouts: 2.17 us -> 0.04 us
    unnamed x18 -> x10, local copies, waits for them, and re-layouts: 2.15 us -> 0.02 us
    pallas_call x7 -> x8, Pallas kernels: 25.3 us -> 24.6 us  [call(): pl.pallas_call(kernel, out_shape=tuple((pltpu.VMEM(out[0], out[1]) if len...]
  transfers between devices with their start and end apart: 6 -> 6, of which waited for: 5 -> 5; matrix products, arithmetic and copies ran while one was open for 1% -> 0% of each run, Pallas kernels for 0% -> 1%
where the time goes in v6:
time: 146 us; the launch traced here: 145 us
  blocking collectives  51.1 us (35%)
  starting transfers between devices  41.2 us (28%)
  waiting for transfers between devices  25 us (17%)
  Pallas kernels  24.6 us (17%)
  other arithmetic  2.38 us (2%)
    all_to_all x4, blocking collectives, send_to_all(): return lax.all_to_all(block, axis, 0, 0, axis_index_groups=groups)  51.1 us
    all_to_all x3, starting transfers between devices, send_to_all(): return lax.all_to_all(block, axis, 0, 0, axis_index_groups=groups)  24.8 us
    pallas_call x8, Pallas kernels, call(): pl.pallas_call(kernel, out_shape=tuple((pltpu.VMEM(out[0], out[1]) if len...  24.6 us
    all_to_all x3, waiting for transfers between devices, send_to_all(): return lax.all_to_all(block, axis, 0, 0, axis_index_groups=groups)  22.6 us
    ppermute x2, starting transfers between devices, swap_cores(): return lax.ppermute(sent, 'dp', other_core)  12.1 us
    ppermute x1, starting transfers between devices, body(): lax.ppermute(mine, 'tensor', [(index, (index + y_size) % tensor) for inde...  4.24 us
  transfers between devices with their start and end apart: 6, of which 5 were waited for; matrix products, arithmetic and copies ran while one was open for 0% of the time, Pallas kernels for 1%

profile of v6, /device:TPU:1, one launch (start us, length us, event | category | flops | bytes accessed | tf_op | source)
XLA Modules:
  0.0 145.1 jit_solution(4955636687414059352)
XLA Ops:
  0.6 1.5 %pack.1 = bf16[16,16,640]{2,1,0:T(8,128)(2,1)} custom-call(bf16[16,512]{1,0:T(8,128)(2,1)} %bitcast.40, bf16[16,32]{1,0:T(8,128)(2,1)} %bitcast.41), custom_call_target="tpu_custom_call" | custom-call | tf_op jit(solution)/shard_map/pack/pallas_call | solution.py:409
  2.1 16.2 %all-to-all-start = ((bf16[16,16,640]{2,1,0:T(8,128)(2,1)}), bf16[16,16,640]{2,1,0:T(8,128)(2,1)S(1)}, u32[]{:S(2)}, u32[]{:S(2)}) async-start(bf16[16,16,640]{2,1,0:T(8,128)(2,1)} %pack.1), calls=%async_computation | async-start | bytes 655360 | tf_op jit(solution)/shard_map/all_to_all | solution.py:427
  18.4 14.0 %all-to-all-done = bf16[16,16,640]{2,1,0:T(8,128)(2,1)S(1)} async-done(((bf16[16,16,640]{2,1,0:T(8,128)(2,1)}), bf16[16,16,640]{2,1,0:T(8,128)(2,1)S(1)}, u32[]{:S(2)}, u32[]{:S(2)}) %all-to-all-start) | async-done | bytes 327712 | tf_op jit(solution)/shard_map/all_to_all | solution.py:427
  32.4 19.5 %scan.1 = (bf16[8,2,16,640]{3,2,1,0:T(8,128)(2,1)}, bf16[16,16,1024]{2,1,0:T(8,128)(2,1)S(1)}, bf16[16,16,1024]{2,1,0:T(8,128)(2,1)S(1)}, f32[256,1024]{1,0:T(8,128)S(1)}, f32[24,1024]{1,0:T(8,128)S(1)}) custom-call(s32[1]{0:T(128)} %bitcast.core_ref, bf16[256,640]{1,0:T(8,128)(2,1)S(1)} %bitcast.29, f32[1,512]{1,0:T(1,128)} %bitcast.33, f32[1,32]{1,0:T(1,128)} %bitcast.35, ...), custom_call_target="tpu_custom_call" | custom-call | tf_op jit(solution)/shard_map/scan/pallas_call | solution.py:409
  51.9 4.5 %all-to-all-start.1 = ((bf16[8,32,640]{2,1,0:T(8,128)(2,1)}), bf16[8,32,640]{2,1,0:T(8,128)(2,1)S(1)}, u32[]{:S(2)}, u32[]{:S(2)}) async-start(bf16[8,32,640]{2,1,0:T(8,128)(2,1)} %bitcast.11), calls=%async_computation.1 | async-start | bytes 655360 | tf_op jit(solution)/shard_map/all_to_all | solution.py:427
  56.4 4.2 %collective-permute-start = (bf16[16,16,1024]{2,1,0:T(8,128)(2,1)S(1)}, bf16[16,16,1024]{2,1,0:T(8,128)(2,1)}, u32[]{:S(2)}, u32[]{:S(2)}) collective-permute-start(bf16[16,16,1024]{2,1,0:T(8,128)(2,1)S(1)} %get-tuple-element.32), channel_id=1, source_target_pairs={{0,16},{16,0},{32,48},{48,32},{64,80},{80,64},{96,112},{112,96},{1... | collective-permute-start | bytes 1572872 | tf_op jit(solution)/shard_map/ppermute | solution.py:484
  60.5 5.9 %all-to-all-done.1.parts_ref = bf16[8,32,640]{2,1,0:T(8,128)(2,1)S(1)} async-done(((bf16[8,32,640]{2,1,0:T(8,128)(2,1)}), bf16[8,32,640]{2,1,0:T(8,128)(2,1)S(1)}, u32[]{:S(2)}, u32[]{:S(2)}) %all-to-all-start.1) | async-done | bytes 327712 | tf_op jit(solution)/shard_map/all_to_all | solution.py:427
  66.5 0.0 collective-permute-done
  66.5 2.0 %add_convert_fusion.1 = bf16[16,16,1024]{2,1,0:T(8,128)(2,1)} fusion(bf16[16,16,1024]{2,1,0:T(8,128)(2,1)} %collective-permute-done, bf16[16,16,1024]{2,1,0:T(8,128)(2,1)S(1)} %get-tuple-element.34), kind=kLoop, calls=%fused_computation.1 | loop fusion | flops 1048576 | bytes 1572864 | tf_op jit(solution)/shard_map/convert_element_type | solution.py:487
  68.6 4.1 %all-to-all-start.2 = ((bf16[4,4,16,1024]{3,2,1,0:T(8,128)(2,1)}), bf16[4,4,16,1024]{3,2,1,0:T(8,128)(2,1)S(1)}, u32[]{:S(2)}, u32[]{:S(2)}) async-start(bf16[4,4,16,1024]{3,2,1,0:T(8,128)(2,1)} %bitcast.12), calls=%async_computation.2 | async-start | bytes 1048576 | tf_op jit(solution)/shard_map/all_to_all | solution.py:427
  72.7 4.2 %collective-permute-start.1 = (f32[32,640]{1,0:T(8,128)S(1)}, f32[32,640]{1,0:T(8,128)S(1)}, u32[]{:S(2)}, u32[]{:S(2)}) collective-permute-start(f32[32,640]{1,0:T(8,128)S(1)} %join.1.mine_ref), channel_id=1, source_target_pairs={{0,8},{1,9},{2,10},{3,11},{4,12},{5,13},{6,14},{7,15},{8,0},{9,1},... | collective-permute-start | bytes 245768 | tf_op jit(solution)/shard_map/ppermute | solution.py:532
  77.0 0.0 copy-start
  77.0 2.7 %all-to-all-done.2 = bf16[4,4,16,1024]{3,2,1,0:T(8,128)(2,1)S(1)} async-done(((bf16[4,4,16,1024]{3,2,1,0:T(8,128)(2,1)}), bf16[4,4,16,1024]{3,2,1,0:T(8,128)(2,1)S(1)}, u32[]{:S(2)}, u32[]{:S(2)}) %all-to-all-start.2) | async-done | bytes 524320 | tf_op jit(solution)/shard_map/all_to_all | solution.py:427
  79.6 0.1 reduce_sum.24
  79.7 2.2 %collective-permute-done.1.other_ref = f32[32,640]{1,0:T(8,128)S(1)} collective-permute-done((f32[32,640]{1,0:T(8,128)S(1)}, f32[32,640]{1,0:T(8,128)S(1)}, u32[]{:S(2)}, u32[]{:S(2)}) %collective-permute-start.1) | collective-permute-done | bytes 81952 | tf_op jit(solution)/shard_map/ppermute | solution.py:532
  81.9 0.0 copy-done.3
  81.9 0.0 copy-done.4
  81.9 0.3 norm.1
  82.2 13.1 %all_to_all.35 = bf16[8,32,640]{2,1,0:T(8,128)(2,1)S(1)} all-to-all(bf16[8,32,640]{2,1,0:T(8,128)(2,1)S(1)} %norm.1), channel_id=1, replica_groups={{0,1,2,3,4,5,6,7},{8,9,10,11,12,13,14,15},{16,17,18,19,20,21,22,23},{24..., dimensions={0} | all-to-all | bytes 655360 | tf_op jit(solution)/shard_map/all_to_all | solution.py:427
  95.3 0.0 copy-done
  95.3 0.5 project.1
  95.9 8.0 %collective-permute-start.2 = (bf16[16,16,1152]{2,1,0:T(8,128)(2,1)S(1)}, bf16[16,16,1152]{2,1,0:T(8,128)(2,1)S(1)}, u32[]{:S(2)}, u32[]{:S(2)}) collective-permute-start(bf16[16,16,1152]{2,1,0:T(8,128)(2,1)S(1)} %get-tuple-element.38), channel_id=1, source_target_pairs={{0,16},{16,0},{32,48},{48,32},{64,80},{80,64},{96,112},{112,96},{1... | collective-permute-start | bytes 1769480 | tf_op jit(solution)/shard_map/ppermute | solution.py:484
  103.8 0.0 copy-done.1
  103.9 1.4 grad_x.1
  105.3 0.2 collective-permute-done.2
  105.4 0.1 add_convert_fusion
  105.6 13.9 %all_to_all.36 = bf16[4,4,16,1152]{3,2,1,0:T(8,128)(2,1)S(1)} all-to-all(bf16[4,4,16,1152]{3,2,1,0:T(8,128)(2,1)S(1)} %bitcast.37), channel_id=1, replica_groups={{0,128,256,384},{16,144,272,400},{32,160,288,416},{48,176,304,432},{64,..., dimensions={0} | all-to-all | bytes 1179648 | tf_op jit(solution)/shard_map/all_to_all | solution.py:427
  119.5 0.1 reduce_sum.25
  119.7 12.8 %all_to_all.37.parts_ref = bf16[4,16,2560]{2,1,0:T(8,128)(2,1)S(1)} all-to-all(bf16[4,16,2560]{2,1,0:T(8,128)(2,1)S(1)} %pad_maximum_fusion), channel_id=1, replica_groups={{0,32,64,96},{16,48,80,112},{128,160,192,224},{144,176,208,240},{256,28..., dimensions={0} | all-to-all | bytes 655360 | tf_op jit(solution)/shard_map/all_to_all | solution.py:427
  132.5 0.7 total.1
  133.2 11.3 %all_to_all.38.parts_ref = f32[8,16,512]{2,1,0:T(8,128)S(1)} all-to-all(f32[8,16,512]{2,1,0:T(8,128)S(1)} %get-tuple-element.46), channel_id=1, replica_groups={{0,16,128,144,256,272,384,400},{32,48,160,176,288,304,416,432},{64,80,1..., dimensions={0} | all-to-all | bytes 524288 | tf_op jit(solution)/shard_map/all_to_all | solution.py:427
  144.5 0.7 spread.1
  (10 shorter events, 0.1 us)
Async XLA Ops:
  2.1 30.3 %all-to-all-start = ((bf16[16,16,640]{2,1,0:T(8,128)(2,1)}), bf16[16,16,640]{2,1,0:T(8,128)(2,1)S(1)}, u32[]{:S(2)}, u32[]{:S(2)}) async-start(bf16[16,16,640]{2,1,0:T(8,128)(2,1)} %pack.1), calls=%async_computation | async-start | bytes 655360 | tf_op jit(solution)/shard_map/all_to_all | solution.py:427
  51.9 14.6 %all-to-all-start.1 = ((bf16[8,32,640]{2,1,0:T(8,128)(2,1)}), bf16[8,32,640]{2,1,0:T(8,128)(2,1)S(1)}, u32[]{:S(2)}, u32[]{:S(2)}) async-start(bf16[8,32,640]{2,1,0:T(8,128)(2,1)} %bitcast.11), calls=%async_computation.1 | async-start | bytes 655360 | tf_op jit(solution)/shard_map/all_to_all | solution.py:427
  56.4 10.2 %collective-permute-start = (bf16[16,16,1024]{2,1,0:T(8,128)(2,1)S(1)}, bf16[16,16,1024]{2,1,0:T(8,128)(2,1)}, u32[]{:S(2)}, u32[]{:S(2)}) collective-permute-start(bf16[16,16,1024]{2,1,0:T(8,128)(2,1)S(1)} %get-tuple-element.32), channel_id=1, source_target_pairs={{0,16},{16,0},{32,48},{48,32},{64,80},{80,64},{96,112},{112,96},{1... | collective-permute-start | bytes 1572872 | tf_op jit(solution)/shard_map/ppermute | solution.py:484
  68.6 13.3 %copy-start.3 = (f32[512]{0:T(512)S(1)}, f32[512]{0:T(512)}, u32[]{:S(2)}) copy-start(f32[512]{0:T(512)} %param.22) | copy-start | bytes 6148
  68.6 13.3 %copy-start.4 = (f32[32]{0:T(128)S(1)}, f32[32]{0:T(128)}, u32[]{:S(2)}) copy-start(f32[32]{0:T(128)} %param.23) | copy-start | bytes 388
  68.6 11.0 %all-to-all-start.2 = ((bf16[4,4,16,1024]{3,2,1,0:T(8,128)(2,1)}), bf16[4,4,16,1024]{3,2,1,0:T(8,128)(2,1)S(1)}, u32[]{:S(2)}, u32[]{:S(2)}) async-start(bf16[4,4,16,1024]{3,2,1,0:T(8,128)(2,1)} %bitcast.12), calls=%async_computation.2 | async-start | bytes 1048576 | tf_op jit(solution)/shard_map/all_to_all | solution.py:427
  72.7 9.2 %collective-permute-start.1 = (f32[32,640]{1,0:T(8,128)S(1)}, f32[32,640]{1,0:T(8,128)S(1)}, u32[]{:S(2)}, u32[]{:S(2)}) collective-permute-start(f32[32,640]{1,0:T(8,128)S(1)} %join.1.mine_ref), channel_id=1, source_target_pairs={{0,8},{1,9},{2,10},{3,11},{4,12},{5,13},{6,14},{7,15},{8,0},{9,1},... | collective-permute-start | bytes 245768 | tf_op jit(solution)/shard_map/ppermute | solution.py:532
  77.0 18.4 %copy-start = (bf16[1,256,1024]{2,1,0:T(8,128)(2,1)S(1)}, bf16[1,256,1024]{2,1,0:T(8,128)(2,1)}, u32[]{:S(2)}) copy-start(bf16[1,256,1024]{2,1,0:T(8,128)(2,1)} %param.12) | copy-start | bytes 1572868
  81.9 22.0 %copy-start.1 = (bf16[512,1024]{1,0:T(8,128)(2,1)S(1)}, bf16[512,1024]{1,0:T(8,128)(2,1)}, u32[]{:S(2)}) copy-start(bf16[512,1024]{1,0:T(8,128)(2,1)} %w_xdt_ref.1) | copy-start | bytes 3145732
  81.9 22.0 %copy-start.2 = (bf16[32,1024]{1,0:T(8,128)(2,1)S(1)}, bf16[32,1024]{1,0:T(8,128)(2,1)}, u32[]{:S(2)}) copy-start(bf16[32,1024]{1,0:T(8,128)(2,1)} %w_xbc_ref.1) | copy-start | bytes 196612
  95.9 9.6 %collective-permute-start.2 = (bf16[16,16,1152]{2,1,0:T(8,128)(2,1)S(1)}, bf16[16,16,1152]{2,1,0:T(8,128)(2,1)S(1)}, u32[]{:S(2)}, u32[]{:S(2)}) collective-permute-start(bf16[16,16,1152]{2,1,0:T(8,128)(2,1)S(1)} %get-tuple-element.38), channel_id=1, source_target_pairs={{0,16},{16,0},{32,48},{48,32},{64,80},{80,64},{96,112},{112,96},{1... | collective-permute-start | bytes 1769480 | tf_op jit(solution)/shard_map/ppermute | solution.py:484

commit v7 on v6

--- a/solution.py
+++ b/solution.py
@@ -52,11 +52,11 @@
 
 def split_cores(core_ref, whole, keep_ref, send_ref):
     first_core = core_ref[0] == 0
-    for pair in range(keep_ref.shape[0]):
+    for pair in range(keep_ref.shape[0] // 16):
         even = whole[32 * pair : 32 * pair + 16]
         odd = whole[32 * pair + 16 : 32 * pair + 32]
-        keep_ref[pair] = jnp.where(first_core, even, odd)
-        send_ref[pair] = jnp.where(first_core, odd, even)
+        keep_ref[16 * pair : 16 * pair + 16] = jnp.where(first_core, even, odd)
+        send_ref[16 * pair : 16 * pair + 16] = jnp.where(first_core, odd, even)
 
 
 def scan_kernel(
@@ -255,7 +255,8 @@
             )
 
 
-def sum_kernel(parts_ref, out_ref):
+def join_kernel(parts_ref, kept_ref, other_ref, out_ref, both_ref):
+    both_ref[...] = (kept_ref[...].astype(f32) + other_ref[...].astype(f32)).astype(bf16)
     total = parts_ref[0].astype(f32)
     for peer in range(1, parts_ref.shape[0]):
         total = total + parts_ref[peer].astype(f32)
@@ -330,7 +331,7 @@
     misc_ref,
     keep_ref,
     send_ref,
-    out_s,
+    sums_ref,
     all_s,
     low_s,
     *,
@@ -343,7 +344,7 @@
     to_tokens(low_ref, low_s)
     dt_low = low_s[:, :rank]
     bc_low = low_s[:, rank : rank + bc_width]
-    out_s[:, :width] = (
+    part = (
         scale
         * lax.dot_general(dt_low, x_ref[...], contract_rows, preferred_element_type=f32)
     ).astype(bf16)
@@ -365,42 +366,39 @@
         ]
     piece = rank // (lane // 2)
     all_s[gain_row : gain_row + 1, rank : rank + bc_width] = gains[piece : piece + 1, :bc_width]
-    for piece in range(width // lane):
-        out_s[piece * 64 : (piece + 1) * 64, width:] = all_s[
-            :, piece * lane : (piece + 1) * lane
-        ].astype(bf16)
-    split_cores(core_ref, out_s, keep_ref, send_ref)
-
-
-def total_kernel(parts_ref, xdt_ref, dt_ref, own_ref):
+    split_cores(core_ref, part, keep_ref, send_ref)
+    sums = all_s[...].astype(bf16)
+    sums_ref[...] = sums
+    send_ref[rank // 2 :, :] = sums
+
+
+def total_kernel(parts_ref, xdt_ref, dt_ref):
     width = xdt_ref.shape[1]
     total = parts_ref[0].astype(f32)
     for peer in range(1, parts_ref.shape[0]):
         total = total + parts_ref[peer].astype(f32)
     xdt_ref[...] = total[:, :width]
-    dt_ref[...] = total[:, width : 2 * width]
-    for peer in range(own_ref.shape[0]):
-        own_ref[peer] = total[:, 2 * width :]
+    dt_ref[...] = total[:, width:]
+
+
+def add_kernel(one_ref, other_ref, out_ref):
+    out_ref[...] = (one_ref[...].astype(f32) + other_ref[...].astype(f32)).astype(bf16)
 
 
 def spread_kernel(
-    parts_ref, xbc_ref, alog_ref, bias_ref, skip_ref, dt_gain_ref, bc_gain_ref, all_s, *, order
+    one_ref, other_ref, xbc_ref, alog_ref, bias_ref, skip_ref, dt_gain_ref, bc_gain_ref
 ):
     state = alog_ref.shape[0]
     bc_width = xbc_ref.shape[0]
     rank = dt_gain_ref.shape[1]
-    for block, (peer, place) in enumerate(order):
-        row, piece = 16 * (block % 4), lane * (block // 4)
-        all_s[row : row + 16, piece : piece + lane] = parts_ref[
-            peer, :, place * lane : (place + 1) * lane
-        ]
-    alog_ref[...] = all_s[:state, :]
-    bias_ref[...] = all_s[state : state + 1, :]
-    skip_ref[...] = all_s[state + 1 : state + 2, :]
-    xbc_ref[...] = all_s[state + 8 : state + 8 + bc_width, :]
+    total = one_ref[...].astype(f32) + other_ref[...].astype(f32)
+    alog_ref[...] = total[:state, :]
+    bias_ref[...] = total[state : state + 1, :]
+    skip_ref[...] = total[state + 1 : state + 2, :]
+    xbc_ref[...] = total[state + 8 : state + 8 + bc_width, :]
     gain_row = state + 8 + bc_width
-    dt_gain_ref[...] = all_s[gain_row : gain_row + 1, :rank]
-    bc_gain_ref[...] = all_s[gain_row : gain_row + 1, rank : rank + bc_width]
+    dt_gain_ref[...] = total[gain_row : gain_row + 1, :rank]
+    bc_gain_ref[...] = total[gain_row : gain_row + 1, rank : rank + bc_width]
 
 
 def call(kernel, name, outs, scratch, limit_mib, *args, far=()):
@@ -466,7 +464,6 @@
     y_size = tensor // z_pair
     per_device = rank // dp
     core = (lax.axis_index("dp") % cores).astype(jnp.int32).reshape(1)
-    other_core = [(index, index ^ 1) for index in range(dp)]
     z_stride, x_stride = cores, cores * z_size
     along_x = [[x * x_stride + rest for x in range(x_size)] for rest in range(x_stride)]
     along_z = [
@@ -474,30 +471,25 @@
         for x in range(x_size)
         for c in range(cores)
     ]
-    along_xc = [
-        [x * x_stride + z * z_stride + c for x in range(x_size) for c in range(cores)]
-        for z in range(z_size)
-    ]
     along_y = [[z * y_size + y for y in range(y_size)] for z in range(z_pair)]
 
-    def swap_cores(sent):
-        return lax.ppermute(sent, "dp", other_core)
-
-    def sum_over_x(kept, other):
-        both = (kept.astype(f32) + other.astype(f32)).astype(bf16)
-        blocks = both.reshape((x_size, z_size) + both.shape[1:])
+    def swap(sent, flip):
+        return lax.ppermute(sent, "dp", [(index, index ^ flip) for index in range(dp)])
+
+    def sum_over_x(both):
+        blocks = both.reshape(x_size, z_size, per_device, width)
         return sum_low(send_to_all(blocks, "dp", along_x))
 
     rows = ((tokens, width), f32)
     by_token = (y_size, z_pair, own, columns)
-    half = (x_size * z_size, per_device)
+    half = (rank // cores, width)
     normed_part, w_kept, w_sent, xg, misc = call(
         functools.partial(scan_kernel, scale=scale),
         "scan",
         [
             (by_token, bf16, local),
-            (half + (width,), bf16, local),
-            (half + (width,), bf16, local),
+            (half, bf16, local),
+            (half, bf16, local),
             ((tokens, width), f32, local),
             ((state + 8, width), f32, local),
         ],
@@ -524,11 +516,17 @@
     normed_parts = send_to_all(
         normed_part.reshape(y_size, shared_rows, columns), "tensor", along_y
     )
-    (mine,) = call(
-        sum_kernel, "join", [((shared_rows, columns), f32, local)], [], 4, normed_parts
-    )
-    mine, w_other = lax.optimization_barrier((mine, swap_cores(w_sent)))
-    w_by_x = sum_over_x(w_kept, w_other)
+    mine, w_both = call(
+        join_kernel,
+        "join",
+        [((shared_rows, columns), f32, local), (half, bf16)],
+        [],
+        16,
+        normed_parts,
+        w_kept,
+        swap(w_sent, 1),
+    )
+    w_by_x = sum_over_x(w_both)
     other = lax.ppermute(
         mine, "tensor", [(index, (index + y_size) % tensor) for index in range(tensor)]
     )
@@ -548,16 +546,16 @@
         bc_gain_row,
     )
     low = send_to_all(own_low, "tensor", along_y).reshape(by_token)
-    half_row = (half + (width + lane,), bf16)
-    kept, sent = call(
+    sums_shape = (64, width)
+    kept, sent, sums = call(
         functools.partial(project_kernel, rank=rank, bc_width=bc_width, scale=scale),
         "project",
-        [half_row + (local,), half_row + (local,)],
         [
-            ((rank, width + lane), bf16),
-            ((64, width), f32),
-            ((tokens, columns), bf16),
+            (half, bf16, local),
+            ((half[0] + sums_shape[0], width), bf16, local),
+            (sums_shape, bf16, local),
         ],
+        [(sums_shape, f32), ((tokens, columns), bf16)],
         16,
         core,
         low,
@@ -575,31 +573,32 @@
         w_xdt,
         w_xbc,
     )
-    swapped, grad_x = lax.optimization_barrier((swap_cores(sent), grad_x))
-    by_x = sum_over_x(kept, swapped)
-    by_z = by_x[:, :, width:].transpose(1, 0, 2).reshape(1, per_device, z_size * lane)
-    by_z = jnp.broadcast_to(by_z, (z_size, per_device, z_size * lane))
-    by_z = jnp.concatenate([by_x[:, :, :width], w_by_x, by_z], axis=2)
-    all_parts = send_to_all(by_z, "dp", along_z)
-    shared = x_size * cores
-    grad_w_xdt, grad_w_dt, own_total = call(
+    swapped, grad_x = lax.optimization_barrier((swap(sent, 1), grad_x))
+    both = (kept.astype(f32) + swapped[: half[0]].astype(f32)).astype(bf16)
+    sums = (sums.astype(f32) + swapped[half[0] :].astype(f32)).astype(bf16)
+
+    def add(one, other):
+        (total,) = call(add_kernel, "add", [(sums_shape, bf16, local)], [], 4, one, other)
+        return total
+
+    by_x = sum_over_x(both)
+    for flip in (x_stride, 3 * x_stride):
+        sums = add(sums, swap(sums, flip))
+    by_x, sums = lax.optimization_barrier((by_x, sums))
+    all_parts = send_to_all(jnp.concatenate([by_x, w_by_x], axis=2), "dp", along_z)
+    sums = add(sums, swap(sums, z_stride))
+    last = swap(sums, 2 * z_stride)
+    all_parts, last = lax.optimization_barrier((all_parts, last))
+    grad_w_xdt, grad_w_dt = call(
         total_kernel,
         "total",
-        [
-            ((per_device, width), f32),
-            ((per_device, width), f32),
-            ((shared, per_device, z_size * lane), f32, local),
-        ],
+        [((per_device, width), f32), ((per_device, width), f32)],
         [],
         4,
         all_parts,
     )
-    totals = send_to_all(own_total, "dp", along_xc)
-    order = tuple(
-        (x * cores + c, z) for x in range(x_size) for z in range(z_size) for c in range(cores)
-    )
     grad_w_xbc, grad_a_log, bias_total, skip_total, dt_gain_total, bc_gain_total = call(
-        functools.partial(spread_kernel, order=order),
+        spread_kernel,
         "spread",
         [
             ((bc_width, width), f32),
@@ -609,9 +608,10 @@
             ((1, rank), f32),
             ((1, bc_width), f32),
         ],
-        [((64, width), f32)],
+        [],
         4,
-        totals,
+        sums,
+        last,
     )
     return (
         grad_x[None],

time: 146 us -> 153 us (1.048); the launches traced: 145 us -> 150 us
  blocking collectives: 51.1 us -> 13.2 us
  starting transfers between devices: 41.2 us -> 63.5 us
  waiting for transfers between devices: 25 us -> 44.5 us
    all_to_all x4 -> x1, blocking collectives: 51.1 us -> 13.2 us  [send_to_all(): return lax.all_to_all(block, axis, 0, 0, axis_index_groups=groups)]
    ppermute x2 -> x6, waiting for transfers between devices: 0.19 us -> 21.2 us  [swap(): lax.ppermute(sent, 'dp', [(index, index ^ flip) for index in range(dp)])]
    ppermute x2 -> x6, starting transfers between devices: 12.1 us -> 25.9 us  [swap(): lax.ppermute(sent, 'dp', [(index, index ^ flip) for index in range(dp)])]
    all_to_all x3 -> x5, starting transfers between devices: 24.8 us -> 33.4 us  [send_to_all(): return lax.all_to_all(block, axis, 0, 0, axis_index_groups=groups)]
    all_to_all x3 -> x5, waiting for transfers between devices: 22.6 us -> 21.1 us  [send_to_all(): return lax.all_to_all(block, axis, 0, 0, axis_index_groups=groups)]
    pallas_call x8 -> x11, Pallas kernels: 24.6 us -> 25.6 us  [call(): pl.pallas_call(kernel, out_shape=tuple((pltpu.VMEM(out[0], out[1]) if len...]
  transfers between devices with their start and end apart: 6 -> 12, of which waited for: 5 -> 10; matrix products, arithmetic and copies ran while one was open for 0% -> 0% of each run, Pallas kernels for 1% -> 1%
where the time goes in v7:
time: 153 us; the launch traced here: 150 us
  starting transfers between devices  63.5 us (42%)
  waiting for transfers between devices  44.5 us (29%)
  Pallas kernels  25.6 us (17%)
  blocking collectives  13.2 us (9%)
  other arithmetic  1.91 us (1%)
    all_to_all x5, starting transfers between devices, send_to_all(): return lax.all_to_all(block, axis, 0, 0, axis_index_groups=groups)  33.4 us
    ppermute x6, starting transfers between devices, swap(): lax.ppermute(sent, 'dp', [(index, index ^ flip) for index in range(dp)])  25.9 us
    pallas_call x11, Pallas kernels, call(): pl.pallas_call(kernel, out_shape=tuple((pltpu.VMEM(out[0], out[1]) if len...  25.6 us
    ppermute x6, waiting for transfers between devices, swap(): lax.ppermute(sent, 'dp', [(index, index ^ flip) for index in range(dp)])  21.2 us
    all_to_all x5, waiting for transfers between devices, send_to_all(): return lax.all_to_all(block, axis, 0, 0, axis_index_groups=groups)  21.1 us
    all_to_all x1, blocking collectives, send_to_all(): return lax.all_to_all(block, axis, 0, 0, axis_index_groups=groups)  13.2 us
    ppermute x1, starting transfers between devices, body(): lax.ppermute(mine, 'tensor', [(index, (index + y_size) % tensor) for inde...  4.23 us
  transfers between devices with their start and end apart: 12, of which 10 were waited for; matrix products, arithmetic and copies ran while one was open for 0% of the time, Pallas kernels for 1%

profile of v7, /device:TPU:1, one launch (start us, length us, event | category | flops | bytes accessed | tf_op | source)
XLA Modules:
  0.0 150.2 jit_solution(2687952354228255046)
XLA Ops:
  0.6 1.5 pack.1
  2.1 16.2 %all-to-all-start = ((bf16[16,16,640]{2,1,0:T(8,128)(2,1)}), bf16[16,16,640]{2,1,0:T(8,128)(2,1)S(1)}, u32[]{:S(2)}, u32[]{:S(2)}) async-start(bf16[16,16,640]{2,1,0:T(8,128)(2,1)} %pack.1), calls=%async_computation | async-start | bytes 655360 | tf_op jit(solution)/shard_map/all_to_all | solution.py:425
  18.4 14.0 %all-to-all-done = bf16[16,16,640]{2,1,0:T(8,128)(2,1)S(1)} async-done(((bf16[16,16,640]{2,1,0:T(8,128)(2,1)}), bf16[16,16,640]{2,1,0:T(8,128)(2,1)S(1)}, u32[]{:S(2)}, u32[]{:S(2)}) %all-to-all-start) | async-done | bytes 327712 | tf_op jit(solution)/shard_map/all_to_all | solution.py:425
  32.4 19.5 %scan.1 = (bf16[8,2,16,640]{3,2,1,0:T(8,128)(2,1)}, bf16[256,1024]{1,0:T(8,128)(2,1)S(1)}, bf16[256,1024]{1,0:T(8,128)(2,1)S(1)}, f32[256,1024]{1,0:T(8,128)S(1)}, f32[24,1024]{1,0:T(8,128)S(1)}) custom-call(s32[1]{0:T(128)} %bitcast.core_ref, bf16[256,640]{1,0:T(8,128)(2,1)S(1)} %bitcast.23, f32[1,512]{1,0:T(1,128)} %bitcast.27, f32[1,32]{1,0:T(1,128)} %bitcast.29, ...), custom_call_target="tpu_custom_call" | custom-call | tf_op jit(solution)/shard_map/scan/pallas_call | solution.py:407
  51.9 4.5 %all-to-all-start.1 = ((bf16[8,32,640]{2,1,0:T(8,128)(2,1)}), bf16[8,32,640]{2,1,0:T(8,128)(2,1)S(1)}, u32[]{:S(2)}, u32[]{:S(2)}) async-start(bf16[8,32,640]{2,1,0:T(8,128)(2,1)} %bitcast.11), calls=%async_computation.1 | async-start | bytes 655360 | tf_op jit(solution)/shard_map/all_to_all | solution.py:425
  56.4 4.2 %collective-permute-start = (bf16[256,1024]{1,0:T(8,128)(2,1)S(1)}, bf16[256,1024]{1,0:T(8,128)(2,1)S(1)}, u32[]{:S(2)}, u32[]{:S(2)}) collective-permute-start(bf16[256,1024]{1,0:T(8,128)(2,1)S(1)} %get-tuple-element.37), channel_id=1, source_target_pairs={{0,16},{16,0},{32,48},{48,32},{64,80},{80,64},{96,112},{112,96},{1... | collective-permute-start | bytes 1572872 | tf_op jit(solution)/shard_map/ppermute | solution.py:477
  60.5 1.5 %collective-permute-done.other_ref = bf16[256,1024]{1,0:T(8,128)(2,1)S(1)} collective-permute-done((bf16[256,1024]{1,0:T(8,128)(2,1)S(1)}, bf16[256,1024]{1,0:T(8,128)(2,1)S(1)}, u32[]{:S(2)}, u32[]{:S(2)}) %collective-permute-start) | collective-permute-done | bytes 524320 | tf_op jit(solution)/shard_map/ppermute | solution.py:477
  62.1 4.4 %all-to-all-done.1.parts_ref = bf16[8,32,640]{2,1,0:T(8,128)(2,1)S(1)} async-done(((bf16[8,32,640]{2,1,0:T(8,128)(2,1)}), bf16[8,32,640]{2,1,0:T(8,128)(2,1)S(1)}, u32[]{:S(2)}, u32[]{:S(2)}) %all-to-all-start.1) | async-done | bytes 327712 | tf_op jit(solution)/shard_map/all_to_all | solution.py:425
  66.5 0.9 join.1
  67.4 4.0 %all-to-all-start.2 = ((bf16[4,4,16,1024]{3,2,1,0:T(8,128)(2,1)}), bf16[4,4,16,1024]{3,2,1,0:T(8,128)(2,1)S(1)}, u32[]{:S(2)}, u32[]{:S(2)}) async-start(bf16[4,4,16,1024]{3,2,1,0:T(8,128)(2,1)} %bitcast.12), calls=%async_computation.2 | async-start | bytes 1048576 | tf_op jit(solution)/shard_map/all_to_all | solution.py:425
  71.4 4.2 %collective-permute-start.1 = (f32[32,640]{1,0:T(8,128)S(1)}, f32[32,640]{1,0:T(8,128)S(1)}, u32[]{:S(2)}, u32[]{:S(2)}) collective-permute-start(f32[32,640]{1,0:T(8,128)S(1)} %get-tuple-element.38.mine_ref), channel_id=1, source_target_pairs={{0,8},{1,9},{2,10},{3,11},{4,12},{5,13},{6,14},{7,15},{8,0},{9,1},... | collective-permute-start | bytes 245768 | tf_op jit(solution)/shard_map/ppermute | solution.py:530
  75.6 2.7 %all-to-all-done.2 = bf16[4,4,16,1024]{3,2,1,0:T(8,128)(2,1)S(1)} async-done(((bf16[4,4,16,1024]{3,2,1,0:T(8,128)(2,1)}), bf16[4,4,16,1024]{3,2,1,0:T(8,128)(2,1)S(1)}, u32[]{:S(2)}, u32[]{:S(2)}) %all-to-all-start.2) | async-done | bytes 524320 | tf_op jit(solution)/shard_map/all_to_all | solution.py:425
  78.4 2.2 %collective-permute-done.1.other_ref = f32[32,640]{1,0:T(8,128)S(1)} collective-permute-done((f32[32,640]{1,0:T(8,128)S(1)}, f32[32,640]{1,0:T(8,128)S(1)}, u32[]{:S(2)}, u32[]{:S(2)}) %collective-permute-start.1) | collective-permute-done | bytes 81952 | tf_op jit(solution)/shard_map/ppermute | solution.py:530
  80.6 0.7 copy-done.4
  81.6 13.2 %all_to_all.30 = bf16[8,32,640]{2,1,0:T(8,128)(2,1)S(1)} all-to-all(bf16[8,32,640]{2,1,0:T(8,128)(2,1)S(1)} %norm.1), channel_id=1, replica_groups={{0,1,2,3,4,5,6,7},{8,9,10,11,12,13,14,15},{16,17,18,19,20,21,22,23},{24..., dimensions={0} | all-to-all | bytes 655360 | tf_op jit(solution)/shard_map/all_to_all | solution.py:425
  94.8 0.5 project.1
  95.3 8.0 %collective-permute-start.2 = (bf16[320,1024]{1,0:T(8,128)(2,1)S(1)}, bf16[320,1024]{1,0:T(8,128)(2,1)S(1)}, u32[]{:S(2)}, u32[]{:S(2)}) collective-permute-start(bf16[320,1024]{1,0:T(8,128)(2,1)S(1)} %get-tuple-element.42), channel_id=1, source_target_pairs={{0,16},{16,0},{32,48},{48,32},{64,80},{80,64},{96,112},{112,96},{1... | collective-permute-start | bytes 1966088 | tf_op jit(solution)/shard_map/ppermute | solution.py:477
  103.3 1.4 grad_x.1
  105.0 1.0 add_convert_fusion
  106.0 4.5 %all-to-all-start.4 = ((bf16[4,4,16,1024]{3,2,1,0:T(8,128)(2,1)}), bf16[4,4,16,1024]{3,2,1,0:T(8,128)(2,1)S(1)}, u32[]{:S(2)}, u32[]{:S(2)}) async-start(bf16[4,4,16,1024]{3,2,1,0:T(8,128)(2,1)} %bitcast.16), calls=%async_computation.4 | async-start | bytes 1048576 | tf_op jit(solution)/shard_map/all_to_all | solution.py:425
  110.6 3.4 %collective-permute-start.3 = (bf16[64,1024]{1,0:T(8,128)(2,1)S(1)}, bf16[64,1024]{1,0:T(8,128)(2,1)S(1)}, u32[]{:S(2)}, u32[]{:S(2)}) collective-permute-start(bf16[64,1024]{1,0:T(8,128)(2,1)S(1)} %add_convert_fusion.1.one_ref), channel_id=1, source_target_pairs={{0,128},{16,144},{32,160},{48,176},{64,192},{80,208},{96,224},{112... | collective-permute-start | bytes 393224 | tf_op jit(solution)/shard_map/ppermute | solution.py:477
  113.9 6.8 %collective-permute-done.3.other_ref = bf16[64,1024]{1,0:T(8,128)(2,1)S(1)} collective-permute-done((bf16[64,1024]{1,0:T(8,128)(2,1)S(1)}, bf16[64,1024]{1,0:T(8,128)(2,1)S(1)}, u32[]{:S(2)}, u32[]{:S(2)}) %collective-permute-start.3) | collective-permute-done | bytes 131104 | tf_op jit(solution)/shard_map/ppermute | solution.py:477
  120.8 3.7 %collective-permute-start.4 = (bf16[64,1024]{1,0:T(8,128)(2,1)S(1)}, bf16[64,1024]{1,0:T(8,128)(2,1)S(1)}, u32[]{:S(2)}, u32[]{:S(2)}) collective-permute-start(bf16[64,1024]{1,0:T(8,128)(2,1)S(1)} %add.22.one_ref), channel_id=1, source_target_pairs={{0,384},{16,400},{32,416},{48,432},{64,448},{80,464},{96,480},{112... | collective-permute-start | bytes 393224 | tf_op jit(solution)/shard_map/ppermute | solution.py:477
  124.5 3.2 %collective-permute-done.4.other_ref = bf16[64,1024]{1,0:T(8,128)(2,1)S(1)} collective-permute-done((bf16[64,1024]{1,0:T(8,128)(2,1)S(1)}, bf16[64,1024]{1,0:T(8,128)(2,1)S(1)}, u32[]{:S(2)}, u32[]{:S(2)}) %collective-permute-start.4) | collective-permute-done | bytes 131104 | tf_op jit(solution)/shard_map/ppermute | solution.py:477
  127.8 0.7 pad_maximum_fusion
  128.5 4.2 %all-to-all-start.5 = ((bf16[4,16,2048]{2,1,0:T(8,128)(2,1)}), bf16[4,16,2048]{2,1,0:T(8,128)(2,1)S(1)}, u32[]{:S(2)}, u32[]{:S(2)}) async-start(bf16[4,16,2048]{2,1,0:T(8,128)(2,1)} %pad_maximum_fusion), calls=%async_computation.5 | async-start | bytes 524288 | tf_op jit(solution)/shard_map/all_to_all | solution.py:425
  132.7 3.4 %collective-permute-start.5 = (bf16[64,1024]{1,0:T(8,128)(2,1)S(1)}, bf16[64,1024]{1,0:T(8,128)(2,1)S(1)}, u32[]{:S(2)}, u32[]{:S(2)}) collective-permute-start(bf16[64,1024]{1,0:T(8,128)(2,1)S(1)} %add.23.one_ref), channel_id=1, source_target_pairs={{0,32},{16,48},{32,0},{48,16},{64,96},{80,112},{96,64},{112,80},{1... | collective-permute-start | bytes 393224 | tf_op jit(solution)/shard_map/ppermute | solution.py:477
  136.1 4.7 %collective-permute-done.5.other_ref = bf16[64,1024]{1,0:T(8,128)(2,1)S(1)} collective-permute-done((bf16[64,1024]{1,0:T(8,128)(2,1)S(1)}, bf16[64,1024]{1,0:T(8,128)(2,1)S(1)}, u32[]{:S(2)}, u32[]{:S(2)}) %collective-permute-start.5) | collective-permute-done | bytes 131104 | tf_op jit(solution)/shard_map/ppermute | solution.py:477
  140.8 3.3 %collective-permute-start.6 = (bf16[64,1024]{1,0:T(8,128)(2,1)S(1)}, bf16[64,1024]{1,0:T(8,128)(2,1)S(1)}, u32[]{:S(2)}, u32[]{:S(2)}) collective-permute-start(bf16[64,1024]{1,0:T(8,128)(2,1)S(1)} %add.24.one_ref), channel_id=1, source_target_pairs={{0,64},{16,80},{32,96},{48,112},{64,0},{80,16},{96,32},{112,48},{1... | collective-permute-start | bytes 393224 | tf_op jit(solution)/shard_map/ppermute | solution.py:477
  144.1 4.7 %collective-permute-done.6.other_ref = bf16[64,1024]{1,0:T(8,128)(2,1)S(1)} collective-permute-done((bf16[64,1024]{1,0:T(8,128)(2,1)S(1)}, bf16[64,1024]{1,0:T(8,128)(2,1)S(1)}, u32[]{:S(2)}, u32[]{:S(2)}) %collective-permute-start.6) | collective-permute-done | bytes 131104 | tf_op jit(solution)/shard_map/ppermute | solution.py:477
  148.8 0.7 total.1
  149.5 0.7 spread.1
  (19 shorter events, 1.0 us)
Async XLA Ops:
  2.1 30.3 %all-to-all-start = ((bf16[16,16,640]{2,1,0:T(8,128)(2,1)}), bf16[16,16,640]{2,1,0:T(8,128)(2,1)S(1)}, u32[]{:S(2)}, u32[]{:S(2)}) async-start(bf16[16,16,640]{2,1,0:T(8,128)(2,1)} %pack.1), calls=%async_computation | async-start | bytes 655360 | tf_op jit(solution)/shard_map/all_to_all | solution.py:425
  51.9 14.6 %all-to-all-start.1 = ((bf16[8,32,640]{2,1,0:T(8,128)(2,1)}), bf16[8,32,640]{2,1,0:T(8,128)(2,1)S(1)}, u32[]{:S(2)}, u32[]{:S(2)}) async-start(bf16[8,32,640]{2,1,0:T(8,128)(2,1)} %bitcast.11), calls=%async_computation.1 | async-start | bytes 655360 | tf_op jit(solution)/shard_map/all_to_all | solution.py:425
  56.4 5.7 %collective-permute-start = (bf16[256,1024]{1,0:T(8,128)(2,1)S(1)}, bf16[256,1024]{1,0:T(8,128)(2,1)S(1)}, u32[]{:S(2)}, u32[]{:S(2)}) collective-permute-start(bf16[256,1024]{1,0:T(8,128)(2,1)S(1)} %get-tuple-element.37), channel_id=1, source_target_pairs={{0,16},{16,0},{32,48},{48,32},{64,80},{80,64},{96,112},{112,96},{1... | collective-permute-start | bytes 1572872 | tf_op jit(solution)/shard_map/ppermute | solution.py:477
  67.4 10.9 %all-to-all-start.2 = ((bf16[4,4,16,1024]{3,2,1,0:T(8,128)(2,1)}), bf16[4,4,16,1024]{3,2,1,0:T(8,128)(2,1)S(1)}, u32[]{:S(2)}, u32[]{:S(2)}) async-start(bf16[4,4,16,1024]{3,2,1,0:T(8,128)(2,1)} %bitcast.12), calls=%async_computation.2 | async-start | bytes 1048576 | tf_op jit(solution)/shard_map/all_to_all | solution.py:425
  71.4 9.2 %collective-permute-start.1 = (f32[32,640]{1,0:T(8,128)S(1)}, f32[32,640]{1,0:T(8,128)S(1)}, u32[]{:S(2)}, u32[]{:S(2)}) collective-permute-start(f32[32,640]{1,0:T(8,128)S(1)} %get-tuple-element.38.mine_ref), channel_id=1, source_target_pairs={{0,8},{1,9},{2,10},{3,11},{4,12},{5,13},{6,14},{7,15},{8,0},{9,1},... | collective-permute-start | bytes 245768 | tf_op jit(solution)/shard_map/ppermute | solution.py:530
  78.4 2.2 %copy-start.3 = (f32[512]{0:T(512)S(1)}, f32[512]{0:T(512)}, u32[]{:S(2)}) copy-start(f32[512]{0:T(512)} %param.22) | copy-start | bytes 6148
  80.6 0.7 copy-start.4
  81.2 22.1 %copy-start.2 = (bf16[32,1024]{1,0:T(8,128)(2,1)S(1)}, bf16[32,1024]{1,0:T(8,128)(2,1)}, u32[]{:S(2)}) copy-start(bf16[32,1024]{1,0:T(8,128)(2,1)} %w_xbc_ref.1) | copy-start | bytes 196612
  81.6 13.2 %copy-start = (bf16[1,256,1024]{2,1,0:T(8,128)(2,1)S(1)}, bf16[1,256,1024]{2,1,0:T(8,128)(2,1)}, u32[]{:S(2)}) copy-start(bf16[1,256,1024]{2,1,0:T(8,128)(2,1)} %param.12) | copy-start | bytes 1572868
  81.6 21.7 %copy-start.1 = (bf16[512,1024]{1,0:T(8,128)(2,1)S(1)}, bf16[512,1024]{1,0:T(8,128)(2,1)}, u32[]{:S(2)}) copy-start(bf16[512,1024]{1,0:T(8,128)(2,1)} %w_xdt_ref.1) | copy-start | bytes 3145732
  95.3 9.7 %collective-permute-start.2 = (bf16[320,1024]{1,0:T(8,128)(2,1)S(1)}, bf16[320,1024]{1,0:T(8,128)(2,1)S(1)}, u32[]{:S(2)}, u32[]{:S(2)}) collective-permute-start(bf16[320,1024]{1,0:T(8,128)(2,1)S(1)} %get-tuple-element.42), channel_id=1, source_target_pairs={{0,16},{16,0},{32,48},{48,32},{64,80},{80,64},{96,112},{112,96},{1... | collective-permute-start | bytes 1966088 | tf_op jit(solution)/shard_map/ppermute | solution.py:477
  106.0 21.7 %all-to-all-start.4 = ((bf16[4,4,16,1024]{3,2,1,0:T(8,128)(2,1)}), bf16[4,4,16,1024]{3,2,1,0:T(8,128)(2,1)S(1)}, u32[]{:S(2)}, u32[]{:S(2)}) async-start(bf16[4,4,16,1024]{3,2,1,0:T(8,128)(2,1)} %bitcast.16), calls=%async_computation.4 | async-start | bytes 1048576 | tf_op jit(solution)/shard_map/all_to_all | solution.py:425
  110.6 10.2 %collective-permute-start.3 = (bf16[64,1024]{1,0:T(8,128)(2,1)S(1)}, bf16[64,1024]{1,0:T(8,128)(2,1)S(1)}, u32[]{:S(2)}, u32[]{:S(2)}) collective-permute-start(bf16[64,1024]{1,0:T(8,128)(2,1)S(1)} %add_convert_fusion.1.one_ref), channel_id=1, source_target_pairs={{0,128},{16,144},{32,160},{48,176},{64,192},{80,208},{96,224},{112... | collective-permute-start | bytes 393224 | tf_op jit(solution)/shard_map/ppermute | solution.py:477
  120.8 6.9 %collective-permute-start.4 = (bf16[64,1024]{1,0:T(8,128)(2,1)S(1)}, bf16[64,1024]{1,0:T(8,128)(2,1)S(1)}, u32[]{:S(2)}, u32[]{:S(2)}) collective-permute-start(bf16[64,1024]{1,0:T(8,128)(2,1)S(1)} %add.22.one_ref), channel_id=1, source_target_pairs={{0,384},{16,400},{32,416},{48,432},{64,448},{80,464},{96,480},{112... | collective-permute-start | bytes 393224 | tf_op jit(solution)/shard_map/ppermute | solution.py:477
  128.5 20.3 %all-to-all-start.5 = ((bf16[4,16,2048]{2,1,0:T(8,128)(2,1)}), bf16[4,16,2048]{2,1,0:T(8,128)(2,1)S(1)}, u32[]{:S(2)}, u32[]{:S(2)}) async-start(bf16[4,16,2048]{2,1,0:T(8,128)(2,1)} %pad_maximum_fusion), calls=%async_computation.5 | async-start | bytes 524288 | tf_op jit(solution)/shard_map/all_to_all | solution.py:425
  132.7 8.0 %collective-permute-start.5 = (bf16[64,1024]{1,0:T(8,128)(2,1)S(1)}, bf16[64,1024]{1,0:T(8,128)(2,1)S(1)}, u32[]{:S(2)}, u32[]{:S(2)}) collective-permute-start(bf16[64,1024]{1,0:T(8,128)(2,1)S(1)} %add.23.one_ref), channel_id=1, source_target_pairs={{0,32},{16,48},{32,0},{48,16},{64,96},{80,112},{96,64},{112,80},{1... | collective-permute-start | bytes 393224 | tf_op jit(solution)/shard_map/ppermute | solution.py:477
  140.8 8.0 %collective-permute-start.6 = (bf16[64,1024]{1,0:T(8,128)(2,1)S(1)}, bf16[64,1024]{1,0:T(8,128)(2,1)S(1)}, u32[]{:S(2)}, u32[]{:S(2)}) collective-permute-start(bf16[64,1024]{1,0:T(8,128)(2,1)S(1)} %add.24.one_ref), channel_id=1, source_target_pairs={{0,64},{16,80},{32,96},{48,112},{64,0},{80,16},{96,32},{112,48},{1... | collective-permute-start | bytes 393224 | tf_op jit(solution)/shard_map/ppermute | solution.py:477

commit v8 on v6

--- a/solution.py
+++ b/solution.py
@@ -56,7 +56,7 @@
         even = whole[32 * pair : 32 * pair + 16]
         odd = whole[32 * pair + 16 : 32 * pair + 32]
         keep_ref[pair] = jnp.where(first_core, even, odd)
-        send_ref[pair] = jnp.where(first_core, odd, even)
+        send_ref[pair] = jnp.where(first_core, odd, even).astype(bf16)
 
 
 def scan_kernel(
@@ -237,7 +237,7 @@
     w_part = scale * lax.dot_general(
         low_s[...], pre_grad, contract_rows, preferred_element_type=f32
     )
-    split_cores(core_ref, w_part.astype(bf16), w_keep_ref, w_send_ref)
+    split_cores(core_ref, w_part, w_keep_ref, w_send_ref)
     source_sum = jnp.sum(src_s[...] * gy_s[...], axis=1, keepdims=True)
     b_grad = jnp.sum(b_acc[...], axis=2)
     c_grad = jnp.sum(c_acc[...], axis=2) + b_rows * source_sum
@@ -255,7 +255,8 @@
             )
 
 
-def sum_kernel(parts_ref, out_ref):
+def join_kernel(parts_ref, kept_ref, other_ref, out_ref, both_ref):
+    both_ref[...] = (kept_ref[...] + other_ref[...].astype(f32)).astype(bf16)
     total = parts_ref[0].astype(f32)
     for peer in range(1, parts_ref.shape[0]):
         total = total + parts_ref[peer].astype(f32)
@@ -343,10 +344,9 @@
     to_tokens(low_ref, low_s)
     dt_low = low_s[:, :rank]
     bc_low = low_s[:, rank : rank + bc_width]
-    out_s[:, :width] = (
-        scale
-        * lax.dot_general(dt_low, x_ref[...], contract_rows, preferred_element_type=f32)
-    ).astype(bf16)
+    out_s[:, :width] = scale * lax.dot_general(
+        dt_low, x_ref[...], contract_rows, preferred_element_type=f32
+    )
     state = bc_width // 2
     all_s[...] = jnp.zeros_like(all_s)
     all_s[: state + 2, :] = misc_ref[: state + 2, :]
@@ -368,7 +368,7 @@
     for piece in range(width // lane):
         out_s[piece * 64 : (piece + 1) * 64, width:] = all_s[
             :, piece * lane : (piece + 1) * lane
-        ].astype(bf16)
+        ]
     split_cores(core_ref, out_s, keep_ref, send_ref)
 
 
@@ -380,7 +380,7 @@
     xdt_ref[...] = total[:, :width]
     dt_ref[...] = total[:, width : 2 * width]
     for peer in range(own_ref.shape[0]):
-        own_ref[peer] = total[:, 2 * width :]
+        own_ref[peer] = total[:, 2 * width :].astype(bf16)
 
 
 def spread_kernel(
@@ -393,7 +393,7 @@
         row, piece = 16 * (block % 4), lane * (block // 4)
         all_s[row : row + 16, piece : piece + lane] = parts_ref[
             peer, :, place * lane : (place + 1) * lane
-        ]
+        ].astype(f32)
     alog_ref[...] = all_s[:state, :]
     bias_ref[...] = all_s[state : state + 1, :]
     skip_ref[...] = all_s[state + 1 : state + 2, :]
@@ -450,6 +450,13 @@
     bc_gain_row = bc_gain.reshape(1, bc_width)
 
     columns = rank + lane
+    cores, z_size, z_pair = 2, 4, 2
+    x_size = dp // (cores * z_size)
+    y_size = tensor // z_pair
+    per_device = rank // dp
+    other_core = [(index, index ^ 1) for index in range(dp)]
+    core = (lax.axis_index("dp") % cores).astype(jnp.int32).reshape(1)
+    y_index = (lax.axis_index("tensor") % y_size).astype(jnp.int32).reshape(1)
     local = True
     (own_proj,) = call(
         pack_kernel,
@@ -459,14 +466,9 @@
         4,
         far=(proj_dt[0], proj_bc[0]),
     )
+    own_proj, core, y_index = lax.optimization_barrier((own_proj, core, y_index))
     full_proj = send_to_all(own_proj, "tensor").reshape(tokens, columns)
 
-    cores, z_size, z_pair = 2, 4, 2
-    x_size = dp // (cores * z_size)
-    y_size = tensor // z_pair
-    per_device = rank // dp
-    core = (lax.axis_index("dp") % cores).astype(jnp.int32).reshape(1)
-    other_core = [(index, index ^ 1) for index in range(dp)]
     z_stride, x_stride = cores, cores * z_size
     along_x = [[x * x_stride + rest for x in range(x_size)] for rest in range(x_stride)]
     along_z = [
@@ -483,8 +485,7 @@
     def swap_cores(sent):
         return lax.ppermute(sent, "dp", other_core)
 
-    def sum_over_x(kept, other):
-        both = (kept.astype(f32) + other.astype(f32)).astype(bf16)
+    def sum_over_x(both):
         blocks = both.reshape((x_size, z_size) + both.shape[1:])
         return sum_low(send_to_all(blocks, "dp", along_x))
 
@@ -496,7 +497,7 @@
         "scan",
         [
             (by_token, bf16, local),
-            (half + (width,), bf16, local),
+            (half + (width,), f32, local),
             (half + (width,), bf16, local),
             ((tokens, width), f32, local),
             ((state + 8, width), f32, local),
@@ -524,16 +525,21 @@
     normed_parts = send_to_all(
         normed_part.reshape(y_size, shared_rows, columns), "tensor", along_y
     )
-    (mine,) = call(
-        sum_kernel, "join", [((shared_rows, columns), f32, local)], [], 4, normed_parts
-    )
-    mine, w_other = lax.optimization_barrier((mine, swap_cores(w_sent)))
-    w_by_x = sum_over_x(w_kept, w_other)
+    mine, w_both = call(
+        join_kernel,
+        "join",
+        [((shared_rows, columns), f32, local), (half + (width,), bf16)],
+        [],
+        16,
+        normed_parts,
+        w_kept,
+        swap_cores(w_sent),
+    )
+    w_by_x = sum_over_x(w_both)
     other = lax.ppermute(
         mine, "tensor", [(index, (index + y_size) % tensor) for index in range(tensor)]
     )
     other, w_by_x = lax.optimization_barrier((other, w_by_x))
-    y_index = (lax.axis_index("tensor") % y_size).astype(jnp.int32).reshape(1)
     (own_low,) = call(
         functools.partial(norm_kernel, state=state),
         "norm",
@@ -552,9 +558,9 @@
     kept, sent = call(
         functools.partial(project_kernel, rank=rank, bc_width=bc_width, scale=scale),
         "project",
-        [half_row + (local,), half_row + (local,)],
+        [(half_row[0], f32, local), half_row + (local,)],
         [
-            ((rank, width + lane), bf16),
+            ((rank, width + lane), f32),
             ((64, width), f32),
             ((tokens, columns), bf16),
         ],
@@ -576,7 +582,7 @@
         w_xbc,
     )
     swapped, grad_x = lax.optimization_barrier((swap_cores(sent), grad_x))
-    by_x = sum_over_x(kept, swapped)
+    by_x = sum_over_x((kept + swapped.astype(f32)).astype(bf16))
     by_z = by_x[:, :, width:].transpose(1, 0, 2).reshape(1, per_device, z_size * lane)
     by_z = jnp.broadcast_to(by_z, (z_size, per_device, z_size * lane))
     by_z = jnp.concatenate([by_x[:, :, :width], w_by_x, by_z], axis=2)
@@ -588,7 +594,7 @@
         [
             ((per_device, width), f32),
             ((per_device, width), f32),
-            ((shared, per_device, z_size * lane), f32, local),
+            ((shared, per_device, z_size * lane), bf16, local),
         ],
         [],
         4,

time: 146 us -> 144 us (0.986)
  blocking collectives: 51.1 us -> 79.9 us
  starting transfers between devices: 41.2 us -> 25.1 us
  waiting for transfers between devices: 25 us -> 11 us
  other arithmetic: 2.38 us -> 0.31 us
    all_to_all x4 -> x5, blocking collectives: 51.1 us -> 79.9 us  [send_to_all(): return lax.all_to_all(block, axis, 0, 0, axis_index_groups=groups)]
    all_to_all x3 -> x2, starting transfers between devices: 24.8 us -> 8.64 us  [send_to_all(): return lax.all_to_all(block, axis, 0, 0, axis_index_groups=groups)]
    all_to_all x3 -> x2, waiting for transfers between devices: 22.6 us -> 6.78 us  [send_to_all(): return lax.all_to_all(block, axis, 0, 0, axis_index_groups=groups)]
    convert_element_type x2 -> x1, other arithmetic: 2.18 us -> 0.11 us  [body(): by_x = sum_over_x((kept + swapped.astype(f32)).astype(bf16))]
    ppermute x2, waiting for transfers between devices: 0.19 us -> 1.92 us  [swap_cores(): return lax.ppermute(sent, 'dp', other_core)]
  transfers between devices with their start and end apart: 6 -> 5, of which waited for: 5 -> 5; matrix products, arithmetic and copies ran while one was open for 0% -> 0% of each run, Pallas kernels for 1% -> 1%
where the time goes in v8:
time: 144 us; the launch traced here: 143 us
  blocking collectives  79.9 us (55%)
  starting transfers between devices  25.1 us (17%)
  Pallas kernels  24.7 us (17%)
  waiting for transfers between devices  11 us (8%)
  local copies, waits for them, and re-layouts  1.47 us (1%)
    all_to_all x5, blocking collectives, send_to_all(): return lax.all_to_all(block, axis, 0, 0, axis_index_groups=groups)  79.9 us
    pallas_call x8, Pallas kernels, call(): pl.pallas_call(kernel, out_shape=tuple((pltpu.VMEM(out[0], out[1]) if len...  24.7 us
    ppermute x2, starting transfers between devices, swap_cores(): return lax.ppermute(sent, 'dp', other_core)  12.1 us
    all_to_all x2, starting transfers between devices, send_to_all(): return lax.all_to_all(block, axis, 0, 0, axis_index_groups=groups)  8.64 us
    all_to_all x2, waiting for transfers between devices, send_to_all(): return lax.all_to_all(block, axis, 0, 0, axis_index_groups=groups)  6.78 us
    ppermute x1, starting transfers between devices, body(): lax.ppermute(mine, 'tensor', [(index, (index + y_size) % tensor) for inde...  4.34 us
  transfers between devices with their start and end apart: 5, of which 5 were waited for; matrix products, arithmetic and copies ran while one was open for 0% of the time, Pallas kernels for 1%

profile of v8, /device:TPU:1, one launch (start us, length us, event | category | flops | bytes accessed | tf_op | source)
XLA Modules:
  0.0 143.3 jit_solution(1090369463231500877)
XLA Ops:
  0.7 0.8 pack.1
  1.4 30.1 %all_to_all.35 = bf16[16,16,640]{2,1,0:T(8,128)(2,1)S(1)} all-to-all(bf16[16,16,640]{2,1,0:T(8,128)(2,1)S(1)} %pack.1), channel_id=1, replica_groups=mesh['dp'=32,'tensor'=16] {'tensor'}, dimensions={0} | all-to-all | bytes 655360 | tf_op jit(solution)/shard_map/all_to_all | solution.py:427
  31.5 19.5 %scan.1 = (bf16[8,2,16,640]{3,2,1,0:T(8,128)(2,1)}, f32[16,16,1024]{2,1,0:T(8,128)S(1)}, bf16[16,16,1024]{2,1,0:T(8,128)(2,1)S(1)}, f32[256,1024]{1,0:T(8,128)S(1)}, f32[24,1024]{1,0:T(8,128)S(1)}) custom-call(s32[1]{0:T(128)} %bitcast.2.core_ref, bf16[256,640]{1,0:T(8,128)(2,1)S(1)} %bitcast.29, f32[1,512]{1,0:T(1,128)} %bitcast.33, f32[1,32]{1,0:T(1,128)} %bitcast.35, ...), custom_call_target="tpu_custom_call" | custom-call | tf_op jit(solution)/shard_map/scan/pallas_call | solution.py:409
  51.0 0.0 copy-start.2
  51.0 0.6 copy-done.2
  51.6 0.8 copy-done.7
  52.4 4.5 %all-to-all-start.1 = ((bf16[8,32,640]{2,1,0:T(8,128)(2,1)}), bf16[8,32,640]{2,1,0:T(8,128)(2,1)S(1)}, u32[]{:S(2)}, u32[]{:S(2)}) async-start(bf16[8,32,640]{2,1,0:T(8,128)(2,1)} %bitcast.11), calls=%async_computation.1 | async-start | bytes 655360 | tf_op jit(solution)/shard_map/all_to_all | solution.py:427
  56.9 4.2 %collective-permute-start = (bf16[16,16,1024]{2,1,0:T(8,128)(2,1)}, bf16[16,16,1024]{2,1,0:T(8,128)(2,1)S(1)}, u32[]{:S(2)}, u32[]{:S(2)}) collective-permute-start(bf16[16,16,1024]{2,1,0:T(8,128)(2,1)} %copy-done.7), channel_id=1, source_target_pairs={{0,16},{16,0},{32,48},{48,32},{64,80},{80,64},{96,112},{112,96},{1... | collective-permute-start | bytes 1572872 | tf_op jit(solution)/shard_map/ppermute | solution.py:486
  61.0 1.7 %collective-permute-done.other_ref = bf16[16,16,1024]{2,1,0:T(8,128)(2,1)S(1)} collective-permute-done((bf16[16,16,1024]{2,1,0:T(8,128)(2,1)}, bf16[16,16,1024]{2,1,0:T(8,128)(2,1)S(1)}, u32[]{:S(2)}, u32[]{:S(2)}) %collective-permute-start) | collective-permute-done | bytes 524320 | tf_op jit(solution)/shard_map/ppermute | solution.py:486
  62.8 4.2 %all-to-all-done.1.parts_ref = bf16[8,32,640]{2,1,0:T(8,128)(2,1)S(1)} async-done(((bf16[8,32,640]{2,1,0:T(8,128)(2,1)}), bf16[8,32,640]{2,1,0:T(8,128)(2,1)S(1)}, u32[]{:S(2)}, u32[]{:S(2)}) %all-to-all-start.1) | async-done | bytes 327712 | tf_op jit(solution)/shard_map/all_to_all | solution.py:427
  67.0 0.9 join.1
  67.8 4.2 %all-to-all-start.2 = ((bf16[4,4,16,1024]{3,2,1,0:T(8,128)(2,1)}), bf16[4,4,16,1024]{3,2,1,0:T(8,128)(2,1)S(1)}, u32[]{:S(2)}, u32[]{:S(2)}) async-start(bf16[4,4,16,1024]{3,2,1,0:T(8,128)(2,1)} %bitcast.12), calls=%async_computation.2 | async-start | bytes 1048576 | tf_op jit(solution)/shard_map/all_to_all | solution.py:427
  72.0 4.3 %collective-permute-start.1 = (f32[32,640]{1,0:T(8,128)S(1)}, f32[32,640]{1,0:T(8,128)S(1)}, u32[]{:S(2)}, u32[]{:S(2)}) collective-permute-start(f32[32,640]{1,0:T(8,128)S(1)} %get-tuple-element.40.mine_ref), channel_id=1, source_target_pairs={{0,8},{1,9},{2,10},{3,11},{4,12},{5,13},{6,14},{7,15},{8,0},{9,1},... | collective-permute-start | bytes 245768 | tf_op jit(solution)/shard_map/ppermute | solution.py:539
  76.4 2.6 %all-to-all-done.2 = bf16[4,4,16,1024]{3,2,1,0:T(8,128)(2,1)S(1)} async-done(((bf16[4,4,16,1024]{3,2,1,0:T(8,128)(2,1)}), bf16[4,4,16,1024]{3,2,1,0:T(8,128)(2,1)S(1)}, u32[]{:S(2)}, u32[]{:S(2)}) %all-to-all-start.2) | async-done | bytes 524320 | tf_op jit(solution)/shard_map/all_to_all | solution.py:427
  78.9 0.1 reduce_sum.24
  79.0 2.3 %collective-permute-done.1.other_ref = f32[32,640]{1,0:T(8,128)S(1)} collective-permute-done((f32[32,640]{1,0:T(8,128)S(1)}, f32[32,640]{1,0:T(8,128)S(1)}, u32[]{:S(2)}, u32[]{:S(2)}) %collective-permute-start.1) | collective-permute-done | bytes 81952 | tf_op jit(solution)/shard_map/ppermute | solution.py:539
  81.3 0.3 norm.1
  81.7 13.0 %all_to_all.36 = bf16[8,32,640]{2,1,0:T(8,128)(2,1)S(1)} all-to-all(bf16[8,32,640]{2,1,0:T(8,128)(2,1)S(1)} %norm.1), channel_id=1, replica_groups={{0,1,2,3,4,5,6,7},{8,9,10,11,12,13,14,15},{16,17,18,19,20,21,22,23},{24..., dimensions={0} | all-to-all | bytes 655360 | tf_op jit(solution)/shard_map/all_to_all | solution.py:427
  94.7 0.0 copy-done.3
  94.7 0.5 project.1
  95.3 8.0 %collective-permute-start.2 = (bf16[16,16,1152]{2,1,0:T(8,128)(2,1)S(1)}, bf16[16,16,1152]{2,1,0:T(8,128)(2,1)S(1)}, u32[]{:S(2)}, u32[]{:S(2)}) collective-permute-start(bf16[16,16,1152]{2,1,0:T(8,128)(2,1)S(1)} %get-tuple-element.44), channel_id=1, source_target_pairs={{0,16},{16,0},{32,48},{48,32},{64,80},{80,64},{96,112},{112,96},{1... | collective-permute-start | bytes 1769480 | tf_op jit(solution)/shard_map/ppermute | solution.py:486
  103.3 0.0 copy-done.1
  103.3 0.0 copy-done.4
  103.3 1.4 grad_x.1
  104.7 0.2 collective-permute-done.2
  104.9 0.1 add_convert_fusion
  105.0 13.9 %all_to_all.37 = bf16[4,4,16,1152]{3,2,1,0:T(8,128)(2,1)S(1)} all-to-all(bf16[4,4,16,1152]{3,2,1,0:T(8,128)(2,1)S(1)} %bitcast.37), channel_id=1, replica_groups={{0,128,256,384},{16,144,272,400},{32,160,288,416},{48,176,304,432},{64,..., dimensions={0} | all-to-all | bytes 1179648 | tf_op jit(solution)/shard_map/all_to_all | solution.py:427
  118.9 0.1 reduce_sum.25
  119.1 12.8 %all_to_all.38.parts_ref = bf16[4,16,2560]{2,1,0:T(8,128)(2,1)S(1)} all-to-all(bf16[4,16,2560]{2,1,0:T(8,128)(2,1)S(1)} %pad_maximum_fusion), channel_id=1, replica_groups={{0,32,64,96},{16,48,80,112},{128,160,192,224},{144,176,208,240},{256,28..., dimensions={0} | all-to-all | bytes 655360 | tf_op jit(solution)/shard_map/all_to_all | solution.py:427
  131.9 0.7 total.1
  132.5 10.1 %all_to_all.39.parts_ref = bf16[8,16,512]{2,1,0:T(8,128)(2,1)S(1)} all-to-all(bf16[8,16,512]{2,1,0:T(8,128)(2,1)S(1)} %get-tuple-element.52), channel_id=1, replica_groups={{0,16,128,144,256,272,384,400},{32,48,160,176,288,304,416,432},{64,80,1..., dimensions={0} | all-to-all | bytes 262144 | tf_op jit(solution)/shard_map/all_to_all | solution.py:427
  142.6 0.7 spread.1
  (14 shorter events, 0.1 us)
Async XLA Ops:
  51.0 0.6 copy-start.2
  51.6 0.8 copy-start.7
  52.4 14.6 %all-to-all-start.1 = ((bf16[8,32,640]{2,1,0:T(8,128)(2,1)}), bf16[8,32,640]{2,1,0:T(8,128)(2,1)S(1)}, u32[]{:S(2)}, u32[]{:S(2)}) async-start(bf16[8,32,640]{2,1,0:T(8,128)(2,1)} %bitcast.11), calls=%async_computation.1 | async-start | bytes 655360 | tf_op jit(solution)/shard_map/all_to_all | solution.py:427
  56.9 5.9 %collective-permute-start = (bf16[16,16,1024]{2,1,0:T(8,128)(2,1)}, bf16[16,16,1024]{2,1,0:T(8,128)(2,1)S(1)}, u32[]{:S(2)}, u32[]{:S(2)}) collective-permute-start(bf16[16,16,1024]{2,1,0:T(8,128)(2,1)} %copy-done.7), channel_id=1, source_target_pairs={{0,16},{16,0},{32,48},{48,32},{64,80},{80,64},{96,112},{112,96},{1... | collective-permute-start | bytes 1572872 | tf_op jit(solution)/shard_map/ppermute | solution.py:486
  67.8 13.5 %copy-start.5 = (f32[512]{0:T(512)S(1)}, f32[512]{0:T(512)}, u32[]{:S(2)}) copy-start(f32[512]{0:T(512)} %param.22) | copy-start | bytes 6148
  67.8 13.5 %copy-start.6 = (f32[32]{0:T(128)S(1)}, f32[32]{0:T(128)}, u32[]{:S(2)}) copy-start(f32[32]{0:T(128)} %param.23) | copy-start | bytes 388
  67.8 11.1 %all-to-all-start.2 = ((bf16[4,4,16,1024]{3,2,1,0:T(8,128)(2,1)}), bf16[4,4,16,1024]{3,2,1,0:T(8,128)(2,1)S(1)}, u32[]{:S(2)}, u32[]{:S(2)}) async-start(bf16[4,4,16,1024]{3,2,1,0:T(8,128)(2,1)} %bitcast.12), calls=%async_computation.2 | async-start | bytes 1048576 | tf_op jit(solution)/shard_map/all_to_all | solution.py:427
  72.0 22.7 %copy-start = (bf16[1,256,1024]{2,1,0:T(8,128)(2,1)S(1)}, bf16[1,256,1024]{2,1,0:T(8,128)(2,1)}, u32[]{:S(2)}) copy-start(bf16[1,256,1024]{2,1,0:T(8,128)(2,1)} %param.12) | copy-start | bytes 1572868
  72.0 22.7 %copy-start.3 = (f32[24,1024]{1,0:T(8,128)S(1)}, f32[24,1024]{1,0:T(8,128)}, u32[]{:S(2)}) copy-start(f32[24,1024]{1,0:T(8,128)} %copy-done.2) | copy-start | bytes 294916
  72.0 9.3 %collective-permute-start.1 = (f32[32,640]{1,0:T(8,128)S(1)}, f32[32,640]{1,0:T(8,128)S(1)}, u32[]{:S(2)}, u32[]{:S(2)}) collective-permute-start(f32[32,640]{1,0:T(8,128)S(1)} %get-tuple-element.40.mine_ref), channel_id=1, source_target_pairs={{0,8},{1,9},{2,10},{3,11},{4,12},{5,13},{6,14},{7,15},{8,0},{9,1},... | collective-permute-start | bytes 245768 | tf_op jit(solution)/shard_map/ppermute | solution.py:539
  81.3 21.9 %copy-start.1 = (bf16[512,1024]{1,0:T(8,128)(2,1)S(1)}, bf16[512,1024]{1,0:T(8,128)(2,1)}, u32[]{:S(2)}) copy-start(bf16[512,1024]{1,0:T(8,128)(2,1)} %w_xdt_ref.1) | copy-start | bytes 3145732
  81.3 21.9 %copy-start.4 = (bf16[32,1024]{1,0:T(8,128)(2,1)S(1)}, bf16[32,1024]{1,0:T(8,128)(2,1)}, u32[]{:S(2)}) copy-start(bf16[32,1024]{1,0:T(8,128)(2,1)} %w_xbc_ref.1) | copy-start | bytes 196612
  95.3 9.6 %collective-permute-start.2 = (bf16[16,16,1152]{2,1,0:T(8,128)(2,1)S(1)}, bf16[16,16,1152]{2,1,0:T(8,128)(2,1)S(1)}, u32[]{:S(2)}, u32[]{:S(2)}) collective-permute-start(bf16[16,16,1152]{2,1,0:T(8,128)(2,1)S(1)} %get-tuple-element.44), channel_id=1, source_target_pairs={{0,16},{16,0},{32,48},{48,32},{64,80},{80,64},{96,112},{112,96},{1... | collective-permute-start | bytes 1769480 | tf_op jit(solution)/shard_map/ppermute | solution.py:486

commit v9 on v8

--- a/solution.py
+++ b/solution.py
@@ -98,6 +98,7 @@
     arrived,
     *,
     scale,
+    z_pair,
     forward_lanes=512,
     forward_rows=32,
     backward_lanes=512,
@@ -241,18 +242,26 @@
     source_sum = jnp.sum(src_s[...] * gy_s[...], axis=1, keepdims=True)
     b_grad = jnp.sum(b_acc[...], axis=2)
     c_grad = jnp.sum(c_acc[...], axis=2) + b_rows * source_sum
+    y_size = normed_ref.shape[0]
+    own = tokens // (y_size * z_pair)
     b_grad = b_grad.astype(bf16)
     c_grad = c_grad.astype(bf16)
-    z_size, y_size, own = normed_ref.shape[1], normed_ref.shape[0], normed_ref.shape[2]
+    bc_width = 2 * state
     for y in range(y_size):
-        for z in range(z_size):
+        last = normed_ref.shape[1] - own
+        normed_ref[y, last:, z_pair * bc_width :] = jnp.zeros(
+            (own, lane - z_pair * bc_width), bf16
+        )
+        for z in range(z_pair):
             rows = slice((z * y_size + y) * own, (z * y_size + y + 1) * own)
-            normed_ref[y, z, :, :rank] = dt_normed[rows]
-            normed_ref[y, z, :, rank : rank + state] = b_grad[rows]
-            normed_ref[y, z, :, rank + state : rank + 2 * state] = c_grad[rows]
-            normed_ref[y, z, :, rank + 2 * state :] = jnp.zeros(
-                (own, lane - 2 * state), bf16
-            )
+            for piece in range(rank // lane):
+                place = (piece * z_pair + z) * own
+                normed_ref[y, place : place + own, :] = dt_normed[
+                    rows, piece * lane : (piece + 1) * lane
+                ]
+            start = z * bc_width
+            normed_ref[y, last:, start : start + state] = b_grad[rows]
+            normed_ref[y, last:, start + state : start + bc_width] = c_grad[rows]
 
 
 def join_kernel(parts_ref, kept_ref, other_ref, out_ref, both_ref):
@@ -267,54 +276,74 @@
     y_ref, mine_ref, other_ref, proj_ref, dt_gain_ref, bc_gain_ref, out_ref, pack_s, *, state
 ):
     rank = dt_gain_ref.shape[1]
-    rows = mine_ref.shape[0]
-    grads = mine_ref[...] + other_ref[...]
-    proj = jnp.concatenate([proj_ref[z, y_ref[0]] for z in range(proj_ref.shape[0])], axis=0)
+    z_pair, _, own, _ = proj_ref.shape
+    rows = z_pair * own
+    last = mine_ref.shape[0] - own
+    bc_width = 2 * state
+    packed = mine_ref[...] + other_ref[...]
+    pieces = range(rank // lane)
+    dt_grad = jnp.concatenate([packed[p * rows : (p + 1) * rows] for p in pieces], axis=1)
+    bc_grad = jnp.concatenate(
+        [packed[last:, z * bc_width : (z + 1) * bc_width] for z in range(z_pair)], axis=0
+    )
+    proj = jnp.concatenate([proj_ref[z, y_ref[0]] for z in range(z_pair)], axis=0)
     dt_norm, b_norm, c_norm = inverse_norms(proj.astype(f32), rank, state)
-    dt_grad = grads[:, :rank]
     dt_unit = dt_norm[0] * dt_norm[1]
     dt_cot = dt_grad * dt_gain_ref[...]
     dt_mean = jnp.mean(dt_cot * dt_unit, axis=1, keepdims=True)
-    pack_s[:, rank:] = jnp.zeros((rows, lane), f32)
-    pack_s[:, :rank] = dt_norm[1] * (dt_cot - dt_unit * dt_mean)
+    dt_back = dt_norm[1] * (dt_cot - dt_unit * dt_mean)
+    for p in pieces:
+        pack_s[p * rows : (p + 1) * rows, :] = dt_back[:, p * lane : (p + 1) * lane]
+    pack_s[last:, :] = jnp.zeros((own, lane), f32)
+    side = z_pair * bc_width
+    free = lane - side
     dt_gain_part = jnp.sum(dt_grad * dt_unit, axis=0, keepdims=True)
-    last = rank + lane // 2
-    for piece in range(rank // (lane // 2)):
-        pack_s[piece : piece + 1, last:] = dt_gain_part[
-            :, piece * (lane // 2) : (piece + 1) * (lane // 2)
+    for piece in range(rank // free):
+        pack_s[last + piece : last + piece + 1, side:] = dt_gain_part[
+            :, piece * free : (piece + 1) * free
         ]
-    gain_row = rank // (lane // 2)
+    gain_row = last + rank // free
     for index, part in enumerate((b_norm, c_norm)):
-        start = rank + index * state
-        grad = grads[:, start : start + state]
+        start = index * state
+        grad = bc_grad[:, start : start + state]
         unit = part[0] * part[1]
-        cot = grad * bc_gain_ref[:, index * state : (index + 1) * state]
+        cot = grad * bc_gain_ref[:, start : start + state]
         mean = jnp.mean(cot * unit, axis=1, keepdims=True)
         inner = jnp.where(part[2] > state_floor, mean, 0.0)
         inner = jnp.where(part[2] == state_floor, 0.5 * mean, inner)
-        pack_s[:, start : start + state] = part[1] * (cot - unit * inner)
-        pack_s[gain_row : gain_row + 1, last + index * state : last + (index + 1) * state] = (
-            jnp.sum(grad * unit, axis=0, keepdims=True)
+        back = part[1] * (cot - unit * inner)
+        for z in range(z_pair):
+            place = z * bc_width + start
+            pack_s[last:, place : place + state] = back[z * own : (z + 1) * own]
+        pack_s[gain_row : gain_row + 1, side + start : side + start + state] = jnp.sum(
+            grad * unit, axis=0, keepdims=True
         )
-    gains = pack_s[: rows // 2, last:]
-    pack_s[rows // 2 :, last:] = gains - gains.astype(bf16).astype(f32)
-    packed = pack_s[...].astype(bf16)
+    sent = pack_s[...].astype(bf16)
     for peer in range(out_ref.shape[0]):
-        out_ref[peer] = packed
-
-
-def to_tokens(low_ref, low_s):
-    y_size, z_size, own, _ = low_ref.shape
+        out_ref[peer] = sent
+
+
+def to_tokens(low_ref, low_s, z_pair, bc_width):
+    y_size, packed_rows, _ = low_ref.shape
+    own = low_s.shape[0] // (y_size * z_pair)
+    pieces = packed_rows // (z_pair * own)
     for y in range(y_size):
-        for z in range(z_size):
+        for z in range(z_pair):
             start = (z * y_size + y) * own
-            low_s[start : start + own, :] = low_ref[y, z]
-
-
-def grad_x_kernel(low_ref, xg_ref, w_xdt_ref, w_xbc_ref, grad_x_ref, low_s):
+            for p in range(pieces):
+                place = (p * z_pair + z) * own
+                low_s[start : start + own, p * lane : (p + 1) * lane] = low_ref[
+                    y, place : place + own, :
+                ]
+            low_s[start : start + own, pieces * lane : pieces * lane + bc_width] = low_ref[
+                y, packed_rows - own :, z * bc_width : (z + 1) * bc_width
+            ]
+
+
+def grad_x_kernel(low_ref, xg_ref, w_xdt_ref, w_xbc_ref, grad_x_ref, low_s, *, z_pair):
     rank = w_xdt_ref.shape[0]
     bc_width = w_xbc_ref.shape[0]
-    to_tokens(low_ref, low_s)
+    to_tokens(low_ref, low_s, z_pair, bc_width)
     summed = xg_ref[...] + jnp.dot(
         low_s[:, :rank], w_xdt_ref[...], preferred_element_type=f32
     )
@@ -337,11 +366,13 @@
     *,
     rank,
     bc_width,
+    z_pair,
     scale,
 ):
     width = x_ref.shape[1]
-    y_size, z_size, own, _ = low_ref.shape
-    to_tokens(low_ref, low_s)
+    y_size = low_ref.shape[0]
+    own = low_s.shape[0] // (y_size * z_pair)
+    to_tokens(low_ref, low_s, z_pair, bc_width)
     dt_low = low_s[:, :rank]
     bc_low = low_s[:, rank : rank + bc_width]
     out_s[:, :width] = scale * lax.dot_general(
@@ -355,15 +386,16 @@
     )
     gains = jnp.zeros((own, lane), f32)
     for y in range(y_size):
-        for z in range(z_size):
-            gains = gains + low_ref[y, z, :, rank:].astype(f32)
-    gains = scale * gains[:, lane // 2 :]
+        gains = gains + low_ref[y, low_ref.shape[1] - own :, :].astype(f32)
+    side = z_pair * bc_width
+    free = lane - side
+    gains = scale * gains[:, side:]
     gain_row = state + 8 + bc_width
-    for piece in range(rank // (lane // 2)):
-        all_s[gain_row : gain_row + 1, piece * (lane // 2) : (piece + 1) * (lane // 2)] = gains[
+    for piece in range(rank // free):
+        all_s[gain_row : gain_row + 1, piece * free : (piece + 1) * free] = gains[
             piece : piece + 1
         ]
-    piece = rank // (lane // 2)
+    piece = rank // free
     all_s[gain_row : gain_row + 1, rank : rank + bc_width] = gains[piece : piece + 1, :bc_width]
     for piece in range(width // lane):
         out_s[piece * 64 : (piece + 1) * 64, width:] = all_s[
@@ -490,17 +522,18 @@
         return sum_low(send_to_all(blocks, "dp", along_x))
 
     rows = ((tokens, width), f32)
-    by_token = (y_size, z_pair, own, columns)
+    packed_rows = z_pair * own * (rank // lane) + own
+    by_y = (y_size, packed_rows, lane)
     half = (x_size * z_size, per_device)
     normed_part, w_kept, w_sent, xg, misc = call(
-        functools.partial(scan_kernel, scale=scale),
+        functools.partial(scan_kernel, scale=scale, z_pair=z_pair),
         "scan",
         [
-            (by_token, bf16, local),
+            (by_y, bf16, local),
             (half + (width,), f32, local),
-            (half + (width,), bf16, local),
+            (half + (width,), bf16),
             ((tokens, width), f32, local),
-            ((state + 8, width), f32, local),
+            ((state + 8, width), f32),
         ],
         [
             rows,
@@ -521,14 +554,11 @@
         full_proj,
         far=(dt_gain_row, bc_gain_row, w_dt, bias_row, x_rows, gy_rows, a_log, skip_row),
     )
-    shared_rows = z_pair * own
-    normed_parts = send_to_all(
-        normed_part.reshape(y_size, shared_rows, columns), "tensor", along_y
-    )
+    normed_parts = send_to_all(normed_part, "tensor", along_y)
     mine, w_both = call(
         join_kernel,
         "join",
-        [((shared_rows, columns), f32, local), (half + (width,), bf16)],
+        [((packed_rows, lane), f32, local), (half + (width,), bf16)],
         [],
         16,
         normed_parts,
@@ -543,8 +573,8 @@
     (own_low,) = call(
         functools.partial(norm_kernel, state=state),
         "norm",
-        [((y_size, shared_rows, columns), bf16, local)],
-        [((shared_rows, columns), f32)],
+        [(by_y, bf16, local)],
+        [((packed_rows, lane), f32)],
         4,
         y_index,
         mine,
@@ -553,10 +583,12 @@
         dt_gain_row,
         bc_gain_row,
     )
-    low = send_to_all(own_low, "tensor", along_y).reshape(by_token)
+    low = send_to_all(own_low, "tensor", along_y)
     half_row = (half + (width + lane,), bf16)
     kept, sent = call(
-        functools.partial(project_kernel, rank=rank, bc_width=bc_width, scale=scale),
+        functools.partial(
+            project_kernel, rank=rank, bc_width=bc_width, z_pair=z_pair, scale=scale
+        ),
         "project",
         [(half_row[0], f32, local), half_row + (local,)],
         [
@@ -571,7 +603,7 @@
         misc,
     )
     (grad_x,) = call(
-        grad_x_kernel,
+        functools.partial(grad_x_kernel, z_pair=z_pair),
         "grad_x",
         [((tokens, width), bf16)],
         [((tokens, columns), bf16)],

time: 144 us -> 144 us (level)
  blocking collectives: 79.9 us -> 95.2 us
  starting transfers between devices: 25.1 us -> 16.5 us
  waiting for transfers between devices: 11 us -> 7.01 us
    all_to_all x5 -> x6, blocking collectives: 79.9 us -> 95.2 us  [send_to_all(): return lax.all_to_all(block, axis, 0, 0, axis_index_groups=groups)]
    all_to_all x2 -> x1, starting transfers between devices: 8.64 us -> 4.13 us  [send_to_all(): return lax.all_to_all(block, axis, 0, 0, axis_index_groups=groups)]
    ppermute x2, starting transfers between devices: 12.1 us -> 10.1 us  [swap_cores(): return lax.ppermute(sent, 'dp', other_core)]
    ppermute x1, starting transfers between devices: 4.34 us -> 2.31 us  [body(): lax.ppermute(mine, 'tensor', [(index, (index + y_size) % tensor) for inde...]
    ppermute x2, waiting for transfers between devices: 1.92 us -> 0.21 us  [swap_cores(): return lax.ppermute(sent, 'dp', other_core)]
    all_to_all x2 -> x1, waiting for transfers between devices: 6.78 us -> 5.77 us  [send_to_all(): return lax.all_to_all(block, axis, 0, 0, axis_index_groups=groups)]
  transfers between devices with their start and end apart: 5 -> 4, of which waited for: 5 -> 3; matrix products, arithmetic and copies ran while one was open for 0% -> 0% of each run, Pallas kernels for 1% -> 1%
where the time goes in v9:
time: 144 us
  blocking collectives  95.2 us (66%)
  Pallas kernels  24.1 us (17%)
  starting transfers between devices  16.5 us (11%)
  waiting for transfers between devices  7.01 us (5%)
    all_to_all x6, blocking collectives, send_to_all(): return lax.all_to_all(block, axis, 0, 0, axis_index_groups=groups)  95.2 us
    pallas_call x8, Pallas kernels, call(): pl.pallas_call(kernel, out_shape=tuple((pltpu.VMEM(out[0], out[1]) if len...  24.1 us
    ppermute x2, starting transfers between devices, swap_cores(): return lax.ppermute(sent, 'dp', other_core)  10.1 us
    all_to_all x1, waiting for transfers between devices, send_to_all(): return lax.all_to_all(block, axis, 0, 0, axis_index_groups=groups)  5.77 us
    all_to_all x1, starting transfers between devices, send_to_all(): return lax.all_to_all(block, axis, 0, 0, axis_index_groups=groups)  4.13 us
  transfers between devices with their start and end apart: 4, of which 3 were waited for; matrix products, arithmetic and copies ran while one was open for 0% of the time, Pallas kernels for 1%

profile of v9, /device:TPU:1, one launch (start us, length us, event | category | flops | bytes accessed | tf_op | source)
XLA Modules:
  0.0 143.9 jit_solution(16542113041318610117)
XLA Ops:
  0.7 0.8 pack.1
  1.4 30.1 %all_to_all.35 = bf16[16,16,640]{2,1,0:T(8,128)(2,1)S(1)} all-to-all(bf16[16,16,640]{2,1,0:T(8,128)(2,1)S(1)} %pack.1), channel_id=1, replica_groups=mesh['dp'=32,'tensor'=16] {'tensor'}, dimensions={0} | all-to-all | bytes 655360 | tf_op jit(solution)/shard_map/all_to_all | solution.py:459
  31.5 18.7 %scan.1 = (bf16[8,144,128]{2,1,0:T(8,128)(2,1)S(1)}, f32[16,16,1024]{2,1,0:T(8,128)S(1)}, bf16[16,16,1024]{2,1,0:T(8,128)(2,1)S(1)}, f32[256,1024]{1,0:T(8,128)S(1)}, f32[24,1024]{1,0:T(8,128)S(1)}) custom-call(s32[1]{0:T(128)} %bitcast.2.core_ref, bf16[256,640]{1,0:T(8,128)(2,1)S(1)} %bitcast.25, f32[1,512]{1,0:T(1,128)} %bitcast.29, f32[1,32]{1,0:T(1,128)} %bitcast.31, ...), custom_call_target="tpu_custom_call" | custom-call | tf_op jit(solution)/shard_map/scan/pallas_call | solution.py:441
  50.2 4.3 %collective-permute-start = (bf16[16,16,1024]{2,1,0:T(8,128)(2,1)S(1)}, bf16[16,16,1024]{2,1,0:T(8,128)(2,1)S(1)}, u32[]{:S(2)}, u32[]{:S(2)}) collective-permute-start(bf16[16,16,1024]{2,1,0:T(8,128)(2,1)S(1)} %get-tuple-element.39), channel_id=1, source_target_pairs={{0,16},{16,0},{32,48},{48,32},{64,80},{80,64},{96,112},{112,96},{1... | collective-permute-start | bytes 1572872 | tf_op jit(solution)/shard_map/ppermute | solution.py:518
  54.6 16.5 %all_to_all.36.parts_ref = bf16[8,144,128]{2,1,0:T(8,128)(2,1)S(1)} all-to-all(bf16[8,144,128]{2,1,0:T(8,128)(2,1)S(1)} %get-tuple-element.37), channel_id=1, replica_groups={{0,1,2,3,4,5,6,7},{8,9,10,11,12,13,14,15},{16,17,18,19,20,21,22,23},{24..., dimensions={0} | all-to-all | bytes 589824 | tf_op jit(solution)/shard_map/all_to_all | solution.py:459
  71.1 0.0 collective-permute-done.other_ref
  71.1 0.9 join.1
  72.0 4.1 %all-to-all-start.2 = ((bf16[4,4,16,1024]{3,2,1,0:T(8,128)(2,1)}), bf16[4,4,16,1024]{3,2,1,0:T(8,128)(2,1)S(1)}, u32[]{:S(2)}, u32[]{:S(2)}) async-start(bf16[4,4,16,1024]{3,2,1,0:T(8,128)(2,1)} %bitcast.11), calls=%async_computation.2 | async-start | bytes 1048576 | tf_op jit(solution)/shard_map/all_to_all | solution.py:459
  76.1 2.3 %collective-permute-start.1 = (f32[144,128]{1,0:T(8,128)S(1)}, f32[144,128]{1,0:T(8,128)S(1)}, u32[]{:S(2)}, u32[]{:S(2)}) collective-permute-start(f32[144,128]{1,0:T(8,128)S(1)} %get-tuple-element.40.mine_ref), channel_id=1, source_target_pairs={{0,8},{1,9},{2,10},{3,11},{4,12},{5,13},{6,14},{7,15},{8,0},{9,1},... | collective-permute-start | bytes 221192 | tf_op jit(solution)/shard_map/ppermute | solution.py:569
  78.4 5.8 %all-to-all-done.2 = bf16[4,4,16,1024]{3,2,1,0:T(8,128)(2,1)S(1)} async-done(((bf16[4,4,16,1024]{3,2,1,0:T(8,128)(2,1)}), bf16[4,4,16,1024]{3,2,1,0:T(8,128)(2,1)S(1)}, u32[]{:S(2)}, u32[]{:S(2)}) %all-to-all-start.2) | async-done | bytes 524320 | tf_op jit(solution)/shard_map/all_to_all | solution.py:459
  84.2 0.1 reduce_sum.24
  84.3 0.0 copy-start.1
  84.3 0.0 copy-start.2
  84.3 1.0 collective-permute-done.1.other_ref
  85.4 0.0 copy-done.3
  85.4 0.0 copy-done.4
  85.4 0.4 norm.1
  85.8 12.1 %all_to_all.37.low_ref = bf16[8,144,128]{2,1,0:T(8,128)(2,1)S(1)} all-to-all(bf16[8,144,128]{2,1,0:T(8,128)(2,1)S(1)} %norm.1), channel_id=1, replica_groups={{0,1,2,3,4,5,6,7},{8,9,10,11,12,13,14,15},{16,17,18,19,20,21,22,23},{24..., dimensions={0} | all-to-all | bytes 589824 | tf_op jit(solution)/shard_map/all_to_all | solution.py:459
  97.9 0.0 copy-done
  97.9 0.5 project.1
  98.4 5.7 %collective-permute-start.2 = (bf16[16,16,1152]{2,1,0:T(8,128)(2,1)S(1)}, bf16[16,16,1152]{2,1,0:T(8,128)(2,1)S(1)}, u32[]{:S(2)}, u32[]{:S(2)}) collective-permute-start(bf16[16,16,1152]{2,1,0:T(8,128)(2,1)S(1)} %get-tuple-element.44), channel_id=1, source_target_pairs={{0,16},{16,0},{32,48},{48,32},{64,80},{80,64},{96,112},{112,96},{1... | collective-permute-start | bytes 1769480 | tf_op jit(solution)/shard_map/ppermute | solution.py:518
  104.2 0.0 copy-done.1
  104.2 0.0 copy-done.2
  104.2 1.4 grad_x.1
  105.6 0.2 collective-permute-done.2
  105.8 0.1 add_convert_fusion
  105.9 13.7 %all_to_all.38 = bf16[4,4,16,1152]{3,2,1,0:T(8,128)(2,1)S(1)} all-to-all(bf16[4,4,16,1152]{3,2,1,0:T(8,128)(2,1)S(1)} %bitcast.33), channel_id=1, replica_groups={{0,128,256,384},{16,144,272,400},{32,160,288,416},{48,176,304,432},{64,..., dimensions={0} | all-to-all | bytes 1179648 | tf_op jit(solution)/shard_map/all_to_all | solution.py:459
  119.5 0.1 reduce_sum.25
  119.7 12.8 %all_to_all.39.parts_ref = bf16[4,16,2560]{2,1,0:T(8,128)(2,1)S(1)} all-to-all(bf16[4,16,2560]{2,1,0:T(8,128)(2,1)S(1)} %pad_maximum_fusion), channel_id=1, replica_groups={{0,32,64,96},{16,48,80,112},{128,160,192,224},{144,176,208,240},{256,28..., dimensions={0} | all-to-all | bytes 655360 | tf_op jit(solution)/shard_map/all_to_all | solution.py:459
  132.5 0.7 total.1
  133.2 10.1 %all_to_all.40.parts_ref = bf16[8,16,512]{2,1,0:T(8,128)(2,1)S(1)} all-to-all(bf16[8,16,512]{2,1,0:T(8,128)(2,1)S(1)} %get-tuple-element.52), channel_id=1, replica_groups={{0,16,128,144,256,272,384,400},{32,48,160,176,288,304,416,432},{64,80,1..., dimensions={0} | all-to-all | bytes 262144 | tf_op jit(solution)/shard_map/all_to_all | solution.py:459
  143.2 0.7 spread.1
  (7 shorter events, 0.0 us)
Async XLA Ops:
  50.2 20.9 %collective-permute-start = (bf16[16,16,1024]{2,1,0:T(8,128)(2,1)S(1)}, bf16[16,16,1024]{2,1,0:T(8,128)(2,1)S(1)}, u32[]{:S(2)}, u32[]{:S(2)}) collective-permute-start(bf16[16,16,1024]{2,1,0:T(8,128)(2,1)S(1)} %get-tuple-element.39), channel_id=1, source_target_pairs={{0,16},{16,0},{32,48},{48,32},{64,80},{80,64},{96,112},{112,96},{1... | collective-permute-start | bytes 1572872 | tf_op jit(solution)/shard_map/ppermute | solution.py:518
  72.0 13.4 %copy-start.3 = (f32[512]{0:T(512)S(1)}, f32[512]{0:T(512)}, u32[]{:S(2)}) copy-start(f32[512]{0:T(512)} %param.22) | copy-start | bytes 6148
  72.0 13.4 %copy-start.4 = (f32[32]{0:T(128)S(1)}, f32[32]{0:T(128)}, u32[]{:S(2)}) copy-start(f32[32]{0:T(128)} %param.23) | copy-start | bytes 388
  72.0 12.2 %all-to-all-start.2 = ((bf16[4,4,16,1024]{3,2,1,0:T(8,128)(2,1)}), bf16[4,4,16,1024]{3,2,1,0:T(8,128)(2,1)S(1)}, u32[]{:S(2)}, u32[]{:S(2)}) async-start(bf16[4,4,16,1024]{3,2,1,0:T(8,128)(2,1)} %bitcast.11), calls=%async_computation.2 | async-start | bytes 1048576 | tf_op jit(solution)/shard_map/all_to_all | solution.py:459
  76.1 21.8 %copy-start = (bf16[1,256,1024]{2,1,0:T(8,128)(2,1)S(1)}, bf16[1,256,1024]{2,1,0:T(8,128)(2,1)}, u32[]{:S(2)}) copy-start(bf16[1,256,1024]{2,1,0:T(8,128)(2,1)} %param.12) | copy-start | bytes 1572868
  76.1 9.2 %collective-permute-start.1 = (f32[144,128]{1,0:T(8,128)S(1)}, f32[144,128]{1,0:T(8,128)S(1)}, u32[]{:S(2)}, u32[]{:S(2)}) collective-permute-start(f32[144,128]{1,0:T(8,128)S(1)} %get-tuple-element.40.mine_ref), channel_id=1, source_target_pairs={{0,8},{1,9},{2,10},{3,11},{4,12},{5,13},{6,14},{7,15},{8,0},{9,1},... | collective-permute-start | bytes 221192 | tf_op jit(solution)/shard_map/ppermute | solution.py:569
  84.3 19.9 %copy-start.1 = (bf16[512,1024]{1,0:T(8,128)(2,1)S(1)}, bf16[512,1024]{1,0:T(8,128)(2,1)}, u32[]{:S(2)}) copy-start(bf16[512,1024]{1,0:T(8,128)(2,1)} %w_xdt_ref.1) | copy-start | bytes 3145732
  84.3 19.9 %copy-start.2 = (bf16[32,1024]{1,0:T(8,128)(2,1)S(1)}, bf16[32,1024]{1,0:T(8,128)(2,1)}, u32[]{:S(2)}) copy-start(bf16[32,1024]{1,0:T(8,128)(2,1)} %w_xbc_ref.1) | copy-start | bytes 196612
  98.4 7.3 %collective-permute-start.2 = (bf16[16,16,1152]{2,1,0:T(8,128)(2,1)S(1)}, bf16[16,16,1152]{2,1,0:T(8,128)(2,1)S(1)}, u32[]{:S(2)}, u32[]{:S(2)}) collective-permute-start(bf16[16,16,1152]{2,1,0:T(8,128)(2,1)S(1)} %get-tuple-element.44), channel_id=1, source_target_pairs={{0,16},{16,0},{32,48},{48,32},{64,80},{80,64},{96,112},{112,96},{1... | collective-permute-start | bytes 1769480 | tf_op jit(solution)/shard_map/ppermute | solution.py:518

commit v10 on v9

--- a/solution.py
+++ b/solution.py
@@ -55,7 +55,7 @@
     for pair in range(keep_ref.shape[0]):
         even = whole[32 * pair : 32 * pair + 16]
         odd = whole[32 * pair + 16 : 32 * pair + 32]
-        keep_ref[pair] = jnp.where(first_core, even, odd)
+        keep_ref[pair] = jnp.where(first_core, even, odd).astype(keep_ref.dtype)
         send_ref[pair] = jnp.where(first_core, odd, even).astype(bf16)
 
 
@@ -265,7 +265,7 @@
 
 
 def join_kernel(parts_ref, kept_ref, other_ref, out_ref, both_ref):
-    both_ref[...] = (kept_ref[...] + other_ref[...].astype(f32)).astype(bf16)
+    both_ref[...] = (kept_ref[...].astype(f32) + other_ref[...].astype(f32)).astype(bf16)
     total = parts_ref[0].astype(f32)
     for peer in range(1, parts_ref.shape[0]):
         total = total + parts_ref[peer].astype(f32)
@@ -530,10 +530,10 @@
         "scan",
         [
             (by_y, bf16, local),
-            (half + (width,), f32, local),
-            (half + (width,), bf16),
+            (half + (width,), bf16, local),
+            (half + (width,), bf16, local),
             ((tokens, width), f32, local),
-            ((state + 8, width), f32),
+            ((state + 8, width), f32, local),
         ],
         [
             rows,
@@ -549,7 +549,7 @@
             rows,
             rows,
         ],
-        44,
+        42,
         core,
         full_proj,
         far=(dt_gain_row, bc_gain_row, w_dt, bias_row, x_rows, gy_rows, a_log, skip_row),

time: 144 us -> 144 us (level)
  no operation moved by 1% of the time
where the time goes in v10:
time: 144 us
  blocking collectives  94.8 us (66%)
  Pallas kernels  24.1 us (17%)
  starting transfers between devices  16.8 us (12%)
  waiting for transfers between devices  7.01 us (5%)
    all_to_all x6, blocking collectives, send_to_all(): return lax.all_to_all(block, axis, 0, 0, axis_index_groups=groups)  94.8 us
    pallas_call x8, Pallas kernels, call(): pl.pallas_call(kernel, out_shape=tuple((pltpu.VMEM(out[0], out[1]) if len...  24.1 us
    ppermute x2, starting transfers between devices, swap_cores(): return lax.ppermute(sent, 'dp', other_core)  10.3 us
    all_to_all x1, waiting for transfers between devices, send_to_all(): return lax.all_to_all(block, axis, 0, 0, axis_index_groups=groups)  5.77 us
    all_to_all x1, starting transfers between devices, send_to_all(): return lax.all_to_all(block, axis, 0, 0, axis_index_groups=groups)  4.15 us
  transfers between devices with their start and end apart: 4, of which 3 were waited for; matrix products, arithmetic and copies ran while one was open for 0% of the time, Pallas kernels for 1%

profile of v10, /device:TPU:1, one launch (start us, length us, event | category | flops | bytes accessed | tf_op | source)
XLA Modules:
  0.0 143.9 jit_solution(7303004696670544309)
XLA Ops:
  0.7 0.8 pack.1
  1.4 30.1 %all_to_all.35 = bf16[16,16,640]{2,1,0:T(8,128)(2,1)S(1)} all-to-all(bf16[16,16,640]{2,1,0:T(8,128)(2,1)S(1)} %pack.1), channel_id=1, replica_groups=mesh['dp'=32,'tensor'=16] {'tensor'}, dimensions={0} | all-to-all | bytes 655360 | tf_op jit(solution)/shard_map/all_to_all | solution.py:459
  31.5 18.7 %scan.1 = (bf16[8,144,128]{2,1,0:T(8,128)(2,1)S(1)}, bf16[16,16,1024]{2,1,0:T(8,128)(2,1)S(1)}, bf16[16,16,1024]{2,1,0:T(8,128)(2,1)S(1)}, f32[256,1024]{1,0:T(8,128)S(1)}, f32[24,1024]{1,0:T(8,128)S(1)}) custom-call(s32[1]{0:T(128)} %bitcast.2.core_ref, bf16[256,640]{1,0:T(8,128)(2,1)S(1)} %bitcast.25, f32[1,512]{1,0:T(1,128)} %bitcast.29, ...), custom_call_target="tpu_custom_call" | custom-call | tf_op jit(solution)/shard_map/scan/pallas_call | solution.py:441
  50.2 4.3 %collective-permute-start = (bf16[16,16,1024]{2,1,0:T(8,128)(2,1)S(1)}, bf16[16,16,1024]{2,1,0:T(8,128)(2,1)S(1)}, u32[]{:S(2)}, u32[]{:S(2)}) collective-permute-start(bf16[16,16,1024]{2,1,0:T(8,128)(2,1)S(1)} %get-tuple-element.39), channel_id=1, source_target_pairs={{0,16},{16,0},{32,48},{48,32},{64,80},{80,64},{96,112},{112,96},{1... | collective-permute-start | bytes 1572872 | tf_op jit(solution)/shard_map/ppermute | solution.py:518
  54.6 16.5 %all_to_all.36.parts_ref = bf16[8,144,128]{2,1,0:T(8,128)(2,1)S(1)} all-to-all(bf16[8,144,128]{2,1,0:T(8,128)(2,1)S(1)} %get-tuple-element.37), channel_id=1, replica_groups={{0,1,2,3,4,5,6,7},{8,9,10,11,12,13,14,15},{16,17,18,19,20,21,22,23},{24..., dimensions={0} | all-to-all | bytes 589824 | tf_op jit(solution)/shard_map/all_to_all | solution.py:459
  71.1 0.0 collective-permute-done.other_ref
  71.1 0.9 join.1
  72.0 4.1 %all-to-all-start.2 = ((bf16[4,4,16,1024]{3,2,1,0:T(8,128)(2,1)}), bf16[4,4,16,1024]{3,2,1,0:T(8,128)(2,1)S(1)}, u32[]{:S(2)}, u32[]{:S(2)}) async-start(bf16[4,4,16,1024]{3,2,1,0:T(8,128)(2,1)} %bitcast.11), calls=%async_computation.2 | async-start | bytes 1048576 | tf_op jit(solution)/shard_map/all_to_all | solution.py:459
  76.2 2.3 %collective-permute-start.1 = (f32[144,128]{1,0:T(8,128)S(1)}, f32[144,128]{1,0:T(8,128)S(1)}, u32[]{:S(2)}, u32[]{:S(2)}) collective-permute-start(f32[144,128]{1,0:T(8,128)S(1)} %get-tuple-element.40.mine_ref), channel_id=1, source_target_pairs={{0,8},{1,9},{2,10},{3,11},{4,12},{5,13},{6,14},{7,15},{8,0},{9,1},... | collective-permute-start | bytes 221192 | tf_op jit(solution)/shard_map/ppermute | solution.py:569
  78.5 5.8 %all-to-all-done.2 = bf16[4,4,16,1024]{3,2,1,0:T(8,128)(2,1)S(1)} async-done(((bf16[4,4,16,1024]{3,2,1,0:T(8,128)(2,1)}), bf16[4,4,16,1024]{3,2,1,0:T(8,128)(2,1)S(1)}, u32[]{:S(2)}, u32[]{:S(2)}) %all-to-all-start.2) | async-done | bytes 524320 | tf_op jit(solution)/shard_map/all_to_all | solution.py:459
  84.2 0.1 reduce_sum.24
  84.3 0.0 copy-start.1
  84.3 0.0 copy-start.2
  84.4 1.0 collective-permute-done.1.other_ref
  85.4 0.0 copy-done.3
  85.4 0.0 copy-done.4
  85.4 0.4 norm.1
  85.8 12.1 %all_to_all.37.low_ref = bf16[8,144,128]{2,1,0:T(8,128)(2,1)S(1)} all-to-all(bf16[8,144,128]{2,1,0:T(8,128)(2,1)S(1)} %norm.1), channel_id=1, replica_groups={{0,1,2,3,4,5,6,7},{8,9,10,11,12,13,14,15},{16,17,18,19,20,21,22,23},{24..., dimensions={0} | all-to-all | bytes 589824 | tf_op jit(solution)/shard_map/all_to_all | solution.py:459
  97.9 0.0 copy-done
  97.9 0.5 project.1
  98.5 6.0 %collective-permute-start.2 = (bf16[16,16,1152]{2,1,0:T(8,128)(2,1)S(1)}, bf16[16,16,1152]{2,1,0:T(8,128)(2,1)S(1)}, u32[]{:S(2)}, u32[]{:S(2)}) collective-permute-start(bf16[16,16,1152]{2,1,0:T(8,128)(2,1)S(1)} %get-tuple-element.44), channel_id=1, source_target_pairs={{0,16},{16,0},{32,48},{48,32},{64,80},{80,64},{96,112},{112,96},{1... | collective-permute-start | bytes 1769480 | tf_op jit(solution)/shard_map/ppermute | solution.py:518
  104.5 0.0 copy-done.1
  104.5 0.0 copy-done.2
  104.5 1.4 grad_x.1
  105.9 0.2 collective-permute-done.2
  106.1 0.1 add_convert_fusion
  106.2 13.4 %all_to_all.38 = bf16[4,4,16,1152]{3,2,1,0:T(8,128)(2,1)S(1)} all-to-all(bf16[4,4,16,1152]{3,2,1,0:T(8,128)(2,1)S(1)} %bitcast.33), channel_id=1, replica_groups={{0,128,256,384},{16,144,272,400},{32,160,288,416},{48,176,304,432},{64,..., dimensions={0} | all-to-all | bytes 1179648 | tf_op jit(solution)/shard_map/all_to_all | solution.py:459
  119.6 0.1 reduce_sum.25
  119.7 12.8 %all_to_all.39.parts_ref = bf16[4,16,2560]{2,1,0:T(8,128)(2,1)S(1)} all-to-all(bf16[4,16,2560]{2,1,0:T(8,128)(2,1)S(1)} %pad_maximum_fusion), channel_id=1, replica_groups={{0,32,64,96},{16,48,80,112},{128,160,192,224},{144,176,208,240},{256,28..., dimensions={0} | all-to-all | bytes 655360 | tf_op jit(solution)/shard_map/all_to_all | solution.py:459
  132.5 0.7 total.1
  133.2 10.1 %all_to_all.40.parts_ref = bf16[8,16,512]{2,1,0:T(8,128)(2,1)S(1)} all-to-all(bf16[8,16,512]{2,1,0:T(8,128)(2,1)S(1)} %get-tuple-element.52), channel_id=1, replica_groups={{0,16,128,144,256,272,384,400},{32,48,160,176,288,304,416,432},{64,80,1..., dimensions={0} | all-to-all | bytes 262144 | tf_op jit(solution)/shard_map/all_to_all | solution.py:459
  143.2 0.7 spread.1
  (7 shorter events, 0.0 us)
Async XLA Ops:
  50.2 20.9 %collective-permute-start = (bf16[16,16,1024]{2,1,0:T(8,128)(2,1)S(1)}, bf16[16,16,1024]{2,1,0:T(8,128)(2,1)S(1)}, u32[]{:S(2)}, u32[]{:S(2)}) collective-permute-start(bf16[16,16,1024]{2,1,0:T(8,128)(2,1)S(1)} %get-tuple-element.39), channel_id=1, source_target_pairs={{0,16},{16,0},{32,48},{48,32},{64,80},{80,64},{96,112},{112,96},{1... | collective-permute-start | bytes 1572872 | tf_op jit(solution)/shard_map/ppermute | solution.py:518
  72.0 13.4 %copy-start.3 = (f32[512]{0:T(512)S(1)}, f32[512]{0:T(512)}, u32[]{:S(2)}) copy-start(f32[512]{0:T(512)} %param.22) | copy-start | bytes 6148
  72.0 13.4 %copy-start.4 = (f32[32]{0:T(128)S(1)}, f32[32]{0:T(128)}, u32[]{:S(2)}) copy-start(f32[32]{0:T(128)} %param.23) | copy-start | bytes 388
  72.0 12.2 %all-to-all-start.2 = ((bf16[4,4,16,1024]{3,2,1,0:T(8,128)(2,1)}), bf16[4,4,16,1024]{3,2,1,0:T(8,128)(2,1)S(1)}, u32[]{:S(2)}, u32[]{:S(2)}) async-start(bf16[4,4,16,1024]{3,2,1,0:T(8,128)(2,1)} %bitcast.11), calls=%async_computation.2 | async-start | bytes 1048576 | tf_op jit(solution)/shard_map/all_to_all | solution.py:459
  76.2 21.7 %copy-start = (bf16[1,256,1024]{2,1,0:T(8,128)(2,1)S(1)}, bf16[1,256,1024]{2,1,0:T(8,128)(2,1)}, u32[]{:S(2)}) copy-start(bf16[1,256,1024]{2,1,0:T(8,128)(2,1)} %param.12) | copy-start | bytes 1572868
  76.2 9.2 %collective-permute-start.1 = (f32[144,128]{1,0:T(8,128)S(1)}, f32[144,128]{1,0:T(8,128)S(1)}, u32[]{:S(2)}, u32[]{:S(2)}) collective-permute-start(f32[144,128]{1,0:T(8,128)S(1)} %get-tuple-element.40.mine_ref), channel_id=1, source_target_pairs={{0,8},{1,9},{2,10},{3,11},{4,12},{5,13},{6,14},{7,15},{8,0},{9,1},... | collective-permute-start | bytes 221192 | tf_op jit(solution)/shard_map/ppermute | solution.py:569
  84.3 20.1 %copy-start.1 = (bf16[512,1024]{1,0:T(8,128)(2,1)S(1)}, bf16[512,1024]{1,0:T(8,128)(2,1)}, u32[]{:S(2)}) copy-start(bf16[512,1024]{1,0:T(8,128)(2,1)} %w_xdt_ref.1) | copy-start | bytes 3145732
  84.3 20.1 %copy-start.2 = (bf16[32,1024]{1,0:T(8,128)(2,1)S(1)}, bf16[32,1024]{1,0:T(8,128)(2,1)}, u32[]{:S(2)}) copy-start(bf16[32,1024]{1,0:T(8,128)(2,1)} %w_xbc_ref.1) | copy-start | bytes 196612
  98.5 7.6 %collective-permute-start.2 = (bf16[16,16,1152]{2,1,0:T(8,128)(2,1)S(1)}, bf16[16,16,1152]{2,1,0:T(8,128)(2,1)S(1)}, u32[]{:S(2)}, u32[]{:S(2)}) collective-permute-start(bf16[16,16,1152]{2,1,0:T(8,128)(2,1)S(1)} %get-tuple-element.44), channel_id=1, source_target_pairs={{0,16},{16,0},{32,48},{48,32},{64,80},{80,64},{96,112},{112,96},{1... | collective-permute-start | bytes 1769480 | tf_op jit(solution)/shard_map/ppermute | solution.py:518

commit v11 on v10

--- a/solution.py
+++ b/solution.py
@@ -498,7 +498,7 @@
         4,
         far=(proj_dt[0], proj_bc[0]),
     )
-    own_proj, core, y_index = lax.optimization_barrier((own_proj, core, y_index))
+    own_proj, core = lax.optimization_barrier((own_proj, core))
     full_proj = send_to_all(own_proj, "tensor").reshape(tokens, columns)
 
     z_stride, x_stride = cores, cores * z_size

time: 144 us -> 144 us (level)
  no operation moved by 1% of the time
where the time goes in v11:
time: 144 us
  blocking collectives  94.8 us (66%)
  Pallas kernels  24.1 us (17%)
  starting transfers between devices  16.8 us (12%)
  waiting for transfers between devices  7 us (5%)
    all_to_all x6, blocking collectives, send_to_all(): return lax.all_to_all(block, axis, 0, 0, axis_index_groups=groups)  94.8 us
    pallas_call x8, Pallas kernels, call(): pl.pallas_call(kernel, out_shape=tuple((pltpu.VMEM(out[0], out[1]) if len...  24.1 us
    ppermute x2, starting transfers between devices, swap_cores(): return lax.ppermute(sent, 'dp', other_core)  10.3 us
    all_to_all x1, waiting for transfers between devices, send_to_all(): return lax.all_to_all(block, axis, 0, 0, axis_index_groups=groups)  5.76 us
    all_to_all x1, starting transfers between devices, send_to_all(): return lax.all_to_all(block, axis, 0, 0, axis_index_groups=groups)  4.15 us
  transfers between devices with their start and end apart: 4, of which 3 were waited for; matrix products, arithmetic and copies ran while one was open for 0% of the time, Pallas kernels for 1%

profile of v11, /device:TPU:1, one launch (start us, length us, event | category | flops | bytes accessed | tf_op | source)
XLA Modules:
  0.0 143.9 jit_solution(3502735895027554898)
XLA Ops:
  0.7 0.8 pack.1
  1.4 30.1 %all_to_all.35 = bf16[16,16,640]{2,1,0:T(8,128)(2,1)S(1)} all-to-all(bf16[16,16,640]{2,1,0:T(8,128)(2,1)S(1)} %pack.1), channel_id=1, replica_groups=mesh['dp'=32,'tensor'=16] {'tensor'}, dimensions={0} | all-to-all | bytes 655360 | tf_op jit(solution)/shard_map/all_to_all | solution.py:459
  31.5 18.7 %scan.1 = (bf16[8,144,128]{2,1,0:T(8,128)(2,1)S(1)}, bf16[16,16,1024]{2,1,0:T(8,128)(2,1)S(1)}, bf16[16,16,1024]{2,1,0:T(8,128)(2,1)S(1)}, f32[256,1024]{1,0:T(8,128)S(1)}, f32[24,1024]{1,0:T(8,128)S(1)}) custom-call(s32[1]{0:T(128)} %bitcast.2.core_ref, bf16[256,640]{1,0:T(8,128)(2,1)S(1)} %bitcast.25, f32[1,512]{1,0:T(1,128)} %bitcast.29, ...), custom_call_target="tpu_custom_call" | custom-call | tf_op jit(solution)/shard_map/scan/pallas_call | solution.py:441
  50.2 4.3 %collective-permute-start = (bf16[16,16,1024]{2,1,0:T(8,128)(2,1)S(1)}, bf16[16,16,1024]{2,1,0:T(8,128)(2,1)S(1)}, u32[]{:S(2)}, u32[]{:S(2)}) collective-permute-start(bf16[16,16,1024]{2,1,0:T(8,128)(2,1)S(1)} %get-tuple-element.37), channel_id=1, source_target_pairs={{0,16},{16,0},{32,48},{48,32},{64,80},{80,64},{96,112},{112,96},{1... | collective-permute-start | bytes 1572872 | tf_op jit(solution)/shard_map/ppermute | solution.py:518
  54.6 16.5 %all_to_all.36.parts_ref = bf16[8,144,128]{2,1,0:T(8,128)(2,1)S(1)} all-to-all(bf16[8,144,128]{2,1,0:T(8,128)(2,1)S(1)} %get-tuple-element.35), channel_id=1, replica_groups={{0,1,2,3,4,5,6,7},{8,9,10,11,12,13,14,15},{16,17,18,19,20,21,22,23},{24..., dimensions={0} | all-to-all | bytes 589824 | tf_op jit(solution)/shard_map/all_to_all | solution.py:459
  71.1 0.0 collective-permute-done.other_ref
  71.1 0.9 join.1
  72.0 4.1 %all-to-all-start.2 = ((bf16[4,4,16,1024]{3,2,1,0:T(8,128)(2,1)}), bf16[4,4,16,1024]{3,2,1,0:T(8,128)(2,1)S(1)}, u32[]{:S(2)}, u32[]{:S(2)}) async-start(bf16[4,4,16,1024]{3,2,1,0:T(8,128)(2,1)} %bitcast.11), calls=%async_computation.2 | async-start | bytes 1048576 | tf_op jit(solution)/shard_map/all_to_all | solution.py:459
  76.2 2.3 %collective-permute-start.1 = (f32[144,128]{1,0:T(8,128)S(1)}, f32[144,128]{1,0:T(8,128)S(1)}, u32[]{:S(2)}, u32[]{:S(2)}) collective-permute-start(f32[144,128]{1,0:T(8,128)S(1)} %get-tuple-element.38.mine_ref), channel_id=1, source_target_pairs={{0,8},{1,9},{2,10},{3,11},{4,12},{5,13},{6,14},{7,15},{8,0},{9,1},... | collective-permute-start | bytes 221192 | tf_op jit(solution)/shard_map/ppermute | solution.py:569
  78.5 5.8 %all-to-all-done.2 = bf16[4,4,16,1024]{3,2,1,0:T(8,128)(2,1)S(1)} async-done(((bf16[4,4,16,1024]{3,2,1,0:T(8,128)(2,1)}), bf16[4,4,16,1024]{3,2,1,0:T(8,128)(2,1)S(1)}, u32[]{:S(2)}, u32[]{:S(2)}) %all-to-all-start.2) | async-done | bytes 524320 | tf_op jit(solution)/shard_map/all_to_all | solution.py:459
  84.2 0.1 reduce_sum.24
  84.3 0.0 copy-start.1
  84.3 0.0 copy-start.2
  84.3 1.0 collective-permute-done.1.other_ref
  85.4 0.0 copy-done.3
  85.4 0.0 copy-done.4
  85.4 0.4 norm.1
  85.8 12.1 %all_to_all.37.low_ref = bf16[8,144,128]{2,1,0:T(8,128)(2,1)S(1)} all-to-all(bf16[8,144,128]{2,1,0:T(8,128)(2,1)S(1)} %norm.1), channel_id=1, replica_groups={{0,1,2,3,4,5,6,7},{8,9,10,11,12,13,14,15},{16,17,18,19,20,21,22,23},{24..., dimensions={0} | all-to-all | bytes 589824 | tf_op jit(solution)/shard_map/all_to_all | solution.py:459
  97.9 0.0 copy-done
  97.9 0.5 project.1
  98.4 6.0 %collective-permute-start.2 = (bf16[16,16,1152]{2,1,0:T(8,128)(2,1)S(1)}, bf16[16,16,1152]{2,1,0:T(8,128)(2,1)S(1)}, u32[]{:S(2)}, u32[]{:S(2)}) collective-permute-start(bf16[16,16,1152]{2,1,0:T(8,128)(2,1)S(1)} %get-tuple-element.42), channel_id=1, source_target_pairs={{0,16},{16,0},{32,48},{48,32},{64,80},{80,64},{96,112},{112,96},{1... | collective-permute-start | bytes 1769480 | tf_op jit(solution)/shard_map/ppermute | solution.py:518
  104.5 0.0 copy-done.1
  104.5 0.0 copy-done.2
  104.5 1.4 grad_x.1
  105.9 0.2 collective-permute-done.2
  106.1 0.1 add_convert_fusion
  106.2 13.4 %all_to_all.38 = bf16[4,4,16,1152]{3,2,1,0:T(8,128)(2,1)S(1)} all-to-all(bf16[4,4,16,1152]{3,2,1,0:T(8,128)(2,1)S(1)} %bitcast.33), channel_id=1, replica_groups={{0,128,256,384},{16,144,272,400},{32,160,288,416},{48,176,304,432},{64,..., dimensions={0} | all-to-all | bytes 1179648 | tf_op jit(solution)/shard_map/all_to_all | solution.py:459
  119.6 0.1 reduce_sum.25
  119.7 12.8 %all_to_all.39.parts_ref = bf16[4,16,2560]{2,1,0:T(8,128)(2,1)S(1)} all-to-all(bf16[4,16,2560]{2,1,0:T(8,128)(2,1)S(1)} %pad_maximum_fusion), channel_id=1, replica_groups={{0,32,64,96},{16,48,80,112},{128,160,192,224},{144,176,208,240},{256,28..., dimensions={0} | all-to-all | bytes 655360 | tf_op jit(solution)/shard_map/all_to_all | solution.py:459
  132.5 0.7 total.1
  133.2 10.1 %all_to_all.40.parts_ref = bf16[8,16,512]{2,1,0:T(8,128)(2,1)S(1)} all-to-all(bf16[8,16,512]{2,1,0:T(8,128)(2,1)S(1)} %get-tuple-element.50), channel_id=1, replica_groups={{0,16,128,144,256,272,384,400},{32,48,160,176,288,304,416,432},{64,80,1..., dimensions={0} | all-to-all | bytes 262144 | tf_op jit(solution)/shard_map/all_to_all | solution.py:459
  143.2 0.7 spread.1
  (7 shorter events, 0.0 us)
Async XLA Ops:
  50.2 20.9 %collective-permute-start = (bf16[16,16,1024]{2,1,0:T(8,128)(2,1)S(1)}, bf16[16,16,1024]{2,1,0:T(8,128)(2,1)S(1)}, u32[]{:S(2)}, u32[]{:S(2)}) collective-permute-start(bf16[16,16,1024]{2,1,0:T(8,128)(2,1)S(1)} %get-tuple-element.37), channel_id=1, source_target_pairs={{0,16},{16,0},{32,48},{48,32},{64,80},{80,64},{96,112},{112,96},{1... | collective-permute-start | bytes 1572872 | tf_op jit(solution)/shard_map/ppermute | solution.py:518
  72.0 13.4 %copy-start.3 = (f32[512]{0:T(512)S(1)}, f32[512]{0:T(512)}, u32[]{:S(2)}) copy-start(f32[512]{0:T(512)} %param.22) | copy-start | bytes 6148
  72.0 13.4 %copy-start.4 = (f32[32]{0:T(128)S(1)}, f32[32]{0:T(128)}, u32[]{:S(2)}) copy-start(f32[32]{0:T(128)} %param.23) | copy-start | bytes 388
  72.0 12.2 %all-to-all-start.2 = ((bf16[4,4,16,1024]{3,2,1,0:T(8,128)(2,1)}), bf16[4,4,16,1024]{3,2,1,0:T(8,128)(2,1)S(1)}, u32[]{:S(2)}, u32[]{:S(2)}) async-start(bf16[4,4,16,1024]{3,2,1,0:T(8,128)(2,1)} %bitcast.11), calls=%async_computation.2 | async-start | bytes 1048576 | tf_op jit(solution)/shard_map/all_to_all | solution.py:459
  76.2 21.7 %copy-start = (bf16[1,256,1024]{2,1,0:T(8,128)(2,1)S(1)}, bf16[1,256,1024]{2,1,0:T(8,128)(2,1)}, u32[]{:S(2)}) copy-start(bf16[1,256,1024]{2,1,0:T(8,128)(2,1)} %param.12) | copy-start | bytes 1572868
  76.2 9.2 %collective-permute-start.1 = (f32[144,128]{1,0:T(8,128)S(1)}, f32[144,128]{1,0:T(8,128)S(1)}, u32[]{:S(2)}, u32[]{:S(2)}) collective-permute-start(f32[144,128]{1,0:T(8,128)S(1)} %get-tuple-element.38.mine_ref), channel_id=1, source_target_pairs={{0,8},{1,9},{2,10},{3,11},{4,12},{5,13},{6,14},{7,15},{8,0},{9,1},... | collective-permute-start | bytes 221192 | tf_op jit(solution)/shard_map/ppermute | solution.py:569
  84.3 20.1 %copy-start.1 = (bf16[512,1024]{1,0:T(8,128)(2,1)S(1)}, bf16[512,1024]{1,0:T(8,128)(2,1)}, u32[]{:S(2)}) copy-start(bf16[512,1024]{1,0:T(8,128)(2,1)} %w_xdt_ref.1) | copy-start | bytes 3145732
  84.3 20.1 %copy-start.2 = (bf16[32,1024]{1,0:T(8,128)(2,1)S(1)}, bf16[32,1024]{1,0:T(8,128)(2,1)}, u32[]{:S(2)}) copy-start(bf16[32,1024]{1,0:T(8,128)(2,1)} %w_xbc_ref.1) | copy-start | bytes 196612
  98.4 7.6 %collective-permute-start.2 = (bf16[16,16,1152]{2,1,0:T(8,128)(2,1)S(1)}, bf16[16,16,1152]{2,1,0:T(8,128)(2,1)S(1)}, u32[]{:S(2)}, u32[]{:S(2)}) collective-permute-start(bf16[16,16,1152]{2,1,0:T(8,128)(2,1)S(1)} %get-tuple-element.42), channel_id=1, source_target_pairs={{0,16},{16,0},{32,48},{48,32},{64,80},{80,64},{96,112},{112,96},{1... | collective-permute-start | bytes 1769480 | tf_op jit(solution)/shard_map/ppermute | solution.py:518

commit v12 on v11

--- a/solution.py
+++ b/solution.py
@@ -60,7 +60,6 @@
 
 
 def scan_kernel(
-    core_ref,
     proj_ref,
     dt_gain_in,
     bc_gain_in,
@@ -71,8 +70,7 @@
     alog_in,
     skip_in,
     normed_ref,
-    w_keep_ref,
-    w_send_ref,
+    w_part_ref,
     xg_ref,
     misc_ref,
     dt_s,
@@ -235,10 +233,10 @@
     dt_normed = lax.dot_general(
         pre_grad, w_ref[...], contract_cols, preferred_element_type=f32
     ).astype(bf16)
-    w_part = scale * lax.dot_general(
-        low_s[...], pre_grad, contract_rows, preferred_element_type=f32
-    )
-    split_cores(core_ref, w_part, w_keep_ref, w_send_ref)
+    w_part_ref[...] = (
+        scale
+        * lax.dot_general(low_s[...], pre_grad, contract_rows, preferred_element_type=f32)
+    ).astype(bf16)
     source_sum = jnp.sum(src_s[...] * gy_s[...], axis=1, keepdims=True)
     b_grad = jnp.sum(b_acc[...], axis=2)
     c_grad = jnp.sum(c_acc[...], axis=2) + b_rows * source_sum
@@ -264,8 +262,7 @@
             normed_ref[y, last:, start + state : start + bc_width] = c_grad[rows]
 
 
-def join_kernel(parts_ref, kept_ref, other_ref, out_ref, both_ref):
-    both_ref[...] = (kept_ref[...].astype(f32) + other_ref[...].astype(f32)).astype(bf16)
+def join_kernel(parts_ref, out_ref):
     total = parts_ref[0].astype(f32)
     for peer in range(1, parts_ref.shape[0]):
         total = total + parts_ref[peer].astype(f32)
@@ -357,6 +354,7 @@
     core_ref,
     low_ref,
     x_ref,
+    w_part_ref,
     misc_ref,
     keep_ref,
     send_ref,
@@ -378,6 +376,7 @@
     out_s[:, :width] = scale * lax.dot_general(
         dt_low, x_ref[...], contract_rows, preferred_element_type=f32
     )
+    out_s[:, width : 2 * width] = w_part_ref[...].astype(f32)
     state = bc_width // 2
     all_s[...] = jnp.zeros_like(all_s)
     all_s[: state + 2, :] = misc_ref[: state + 2, :]
@@ -398,7 +397,7 @@
     piece = rank // free
     all_s[gain_row : gain_row + 1, rank : rank + bc_width] = gains[piece : piece + 1, :bc_width]
     for piece in range(width // lane):
-        out_s[piece * 64 : (piece + 1) * 64, width:] = all_s[
+        out_s[piece * 64 : (piece + 1) * 64, 2 * width :] = all_s[
             :, piece * lane : (piece + 1) * lane
         ]
     split_cores(core_ref, out_s, keep_ref, send_ref)
@@ -525,13 +524,12 @@
     packed_rows = z_pair * own * (rank // lane) + own
     by_y = (y_size, packed_rows, lane)
     half = (x_size * z_size, per_device)
-    normed_part, w_kept, w_sent, xg, misc = call(
+    normed_part, w_part, xg, misc = call(
         functools.partial(scan_kernel, scale=scale, z_pair=z_pair),
         "scan",
         [
             (by_y, bf16, local),
-            (half + (width,), bf16, local),
-            (half + (width,), bf16, local),
+            ((rank, width), bf16, local),
             ((tokens, width), f32, local),
             ((state + 8, width), f32, local),
         ],
@@ -550,26 +548,16 @@
             rows,
         ],
         42,
-        core,
         full_proj,
         far=(dt_gain_row, bc_gain_row, w_dt, bias_row, x_rows, gy_rows, a_log, skip_row),
     )
     normed_parts = send_to_all(normed_part, "tensor", along_y)
-    mine, w_both = call(
-        join_kernel,
-        "join",
-        [((packed_rows, lane), f32, local), (half + (width,), bf16)],
-        [],
-        16,
-        normed_parts,
-        w_kept,
-        swap_cores(w_sent),
-    )
-    w_by_x = sum_over_x(w_both)
+    (mine,) = call(
+        join_kernel, "join", [((packed_rows, lane), f32, local)], [], 4, normed_parts
+    )
     other = lax.ppermute(
         mine, "tensor", [(index, (index + y_size) % tensor) for index in range(tensor)]
     )
-    other, w_by_x = lax.optimization_barrier((other, w_by_x))
     (own_low,) = call(
         functools.partial(norm_kernel, state=state),
         "norm",
@@ -584,7 +572,7 @@
         bc_gain_row,
     )
     low = send_to_all(own_low, "tensor", along_y)
-    half_row = (half + (width + lane,), bf16)
+    half_row = (half + (2 * width + lane,), bf16)
     kept, sent = call(
         functools.partial(
             project_kernel, rank=rank, bc_width=bc_width, z_pair=z_pair, scale=scale
@@ -592,7 +580,7 @@
         "project",
         [(half_row[0], f32, local), half_row + (local,)],
         [
-            ((rank, width + lane), f32),
+            ((rank, 2 * width + lane), f32),
             ((64, width), f32),
             ((tokens, columns), bf16),
         ],
@@ -600,6 +588,7 @@
         core,
         low,
         x_rows,
+        w_part,
         misc,
     )
     (grad_x,) = call(
@@ -615,9 +604,9 @@
     )
     swapped, grad_x = lax.optimization_barrier((swap_cores(sent), grad_x))
     by_x = sum_over_x((kept + swapped.astype(f32)).astype(bf16))
-    by_z = by_x[:, :, width:].transpose(1, 0, 2).reshape(1, per_device, z_size * lane)
+    by_z = by_x[:, :, 2 * width :].transpose(1, 0, 2).reshape(1, per_device, z_size * lane)
     by_z = jnp.broadcast_to(by_z, (z_size, per_device, z_size * lane))
-    by_z = jnp.concatenate([by_x[:, :, :width], w_by_x, by_z], axis=2)
+    by_z = jnp.concatenate([by_x[:, :, : 2 * width], by_z], axis=2)
     all_parts = send_to_all(by_z, "dp", along_z)
     shared = x_size * cores
     grad_w_xdt, grad_w_dt, own_total = call(

time: 144 us -> 141 us (0.979)
  starting transfers between devices: 16.8 us -> 12.1 us
  blocking collectives: 94.8 us -> 98 us
    all_to_all x1 -> x0, waiting for transfers between devices: 5.76 us -> none  [send_to_all(): return lax.all_to_all(block, axis, 0, 0, axis_index_groups=groups)]
    all_to_all x1 -> x0, starting transfers between devices: 4.15 us -> none  [send_to_all(): return lax.all_to_all(block, axis, 0, 0, axis_index_groups=groups)]
    ppermute x1, waiting for transfers between devices: 1.03 us -> 5.03 us  [body(): lax.ppermute(mine, 'tensor', [(index, (index + y_size) % tensor) for inde...]
    all_to_all x6, blocking collectives: 94.8 us -> 98 us  [send_to_all(): return lax.all_to_all(block, axis, 0, 0, axis_index_groups=groups)]
    ppermute x2 -> x1, starting transfers between devices: 10.3 us -> 8.05 us  [swap_cores(): return lax.ppermute(sent, 'dp', other_core)]
    ppermute x1, starting transfers between devices: 2.31 us -> 4.05 us  [body(): lax.ppermute(mine, 'tensor', [(index, (index + y_size) % tensor) for inde...]
  transfers between devices with their start and end apart: 4 -> 2, of which waited for: 3 -> 2; matrix products, arithmetic and copies ran while one was open for 0% -> 0% of each run, Pallas kernels for 1% -> 1%
where the time goes in v12:
time: 141 us
  blocking collectives  98 us (70%)
  Pallas kernels  23.5 us (17%)
  starting transfers between devices  12.1 us (9%)
  waiting for transfers between devices  5.99 us (4%)
    all_to_all x6, blocking collectives, send_to_all(): return lax.all_to_all(block, axis, 0, 0, axis_index_groups=groups)  98 us
    pallas_call x8, Pallas kernels, call(): pl.pallas_call(kernel, out_shape=tuple((pltpu.VMEM(out[0], out[1]) if len...  23.5 us
    ppermute x1, starting transfers between devices, swap_cores(): return lax.ppermute(sent, 'dp', other_core)  8.05 us
    ppermute x1, waiting for transfers between devices, body(): lax.ppermute(mine, 'tensor', [(index, (index + y_size) % tensor) for inde...  5.03 us
    ppermute x1, starting transfers between devices, body(): lax.ppermute(mine, 'tensor', [(index, (index + y_size) % tensor) for inde...  4.05 us
  transfers between devices with their start and end apart: 2, of which 2 were waited for; matrix products, arithmetic and copies ran while one was open for 0% of the time, Pallas kernels for 1%

profile of v12, /device:TPU:1, one launch (start us, length us, event | category | flops | bytes accessed | tf_op | source)
XLA Modules:
  0.0 140.8 jit_solution(1729166378943639863)
XLA Ops:
  0.7 0.8 pack.1
  1.4 30.1 %all_to_all.30 = bf16[16,16,640]{2,1,0:T(8,128)(2,1)S(1)} all-to-all(bf16[16,16,640]{2,1,0:T(8,128)(2,1)S(1)} %pack.1), channel_id=1, replica_groups=mesh['dp'=32,'tensor'=16] {'tensor'}, dimensions={0} | all-to-all | bytes 655360 | tf_op jit(solution)/shard_map/all_to_all | solution.py:458
  31.5 0.0 copy-start.3
  31.5 0.0 copy-start.4
  31.5 18.7 %scan.1 = (bf16[8,144,128]{2,1,0:T(8,128)(2,1)S(1)}, bf16[512,1024]{1,0:T(8,128)(2,1)S(1)}, f32[256,1024]{1,0:T(8,128)S(1)}, f32[24,1024]{1,0:T(8,128)S(1)}) custom-call(bf16[256,640]{1,0:T(8,128)(2,1)S(1)} %bitcast.24, f32[1,512]{1,0:T(1,128)} %bitcast.28, f32[1,32]{1,0:T(1,128)} %bitcast.30, bf16[512,1024]{1,0:T(8,128)(2,1)} %w_in.1, f32[1,1024]{1,0:T(1,128)} %bitcast.37, ...), custom_call_target="tpu_custom_call" | custom-call | tf_op jit(solution)/shard_map/scan/pallas_call | solution.py:440
  50.2 0.0 copy-start
  50.2 14.0 %all_to_all.31.parts_ref = bf16[8,144,128]{2,1,0:T(8,128)(2,1)S(1)} all-to-all(bf16[8,144,128]{2,1,0:T(8,128)(2,1)S(1)} %get-tuple-element.30), channel_id=1, replica_groups={{0,1,2,3,4,5,6,7},{8,9,10,11,12,13,14,15},{16,17,18,19,20,21,22,23},{24..., dimensions={0} | all-to-all | bytes 589824 | tf_op jit(solution)/shard_map/all_to_all | solution.py:458
  64.3 4.1 %collective-permute-start = (f32[144,128]{1,0:T(8,128)S(1)}, f32[144,128]{1,0:T(8,128)S(1)}, u32[]{:S(2)}, u32[]{:S(2)}) collective-permute-start(f32[144,128]{1,0:T(8,128)S(1)} %join.1.mine_ref), channel_id=1, source_target_pairs={{0,8},{1,9},{2,10},{3,11},{4,12},{5,13},{6,14},{7,15},{8,0},{9,1},... | collective-permute-start | bytes 221192 | tf_op jit(solution)/shard_map/ppermute | solution.py:558
  68.3 5.0 %collective-permute-done.other_ref = f32[144,128]{1,0:T(8,128)S(1)} collective-permute-done((f32[144,128]{1,0:T(8,128)S(1)}, f32[144,128]{1,0:T(8,128)S(1)}, u32[]{:S(2)}, u32[]{:S(2)}) %collective-permute-start) | collective-permute-done | bytes 73760 | tf_op jit(solution)/shard_map/ppermute | solution.py:558
  73.4 0.0 copy-done.3
  73.4 0.0 copy-done.4
  73.4 0.4 norm.1
  73.8 12.2 %all_to_all.32.low_ref = bf16[8,144,128]{2,1,0:T(8,128)(2,1)S(1)} all-to-all(bf16[8,144,128]{2,1,0:T(8,128)(2,1)S(1)} %norm.1), channel_id=1, replica_groups={{0,1,2,3,4,5,6,7},{8,9,10,11,12,13,14,15},{16,17,18,19,20,21,22,23},{24..., dimensions={0} | all-to-all | bytes 589824 | tf_op jit(solution)/shard_map/all_to_all | solution.py:458
  86.0 0.0 copy-start.1
  86.0 0.0 copy-start.2
  86.0 0.0 copy-done
  86.0 0.8 project.1
  86.7 8.1 %collective-permute-start.1 = (bf16[16,16,2176]{2,1,0:T(8,128)(2,1)S(1)}, bf16[16,16,2176]{2,1,0:T(8,128)(2,1)S(1)}, u32[]{:S(2)}, u32[]{:S(2)}) collective-permute-start(bf16[16,16,2176]{2,1,0:T(8,128)(2,1)S(1)} %get-tuple-element.33), channel_id=1, source_target_pairs={{0,16},{16,0},{32,48},{48,32},{64,80},{80,64},{96,112},{112,96},{1... | collective-permute-start | bytes 3342344 | tf_op jit(solution)/shard_map/ppermute | solution.py:517
  94.8 0.0 copy-done.1
  94.8 0.0 copy-done.2
  94.8 1.4 grad_x.1
  96.2 1.0 collective-permute-done.1
  97.2 0.2 add_convert_fusion
  97.4 19.0 %all_to_all.33 = bf16[4,4,16,2176]{3,2,1,0:T(8,128)(2,1)S(1)} all-to-all(bf16[4,4,16,2176]{3,2,1,0:T(8,128)(2,1)S(1)} %bitcast.32), channel_id=1, replica_groups={{0,128,256,384},{16,144,272,400},{32,160,288,416},{48,176,304,432},{64,..., dimensions={0} | all-to-all | bytes 2228224 | tf_op jit(solution)/shard_map/all_to_all | solution.py:458
  116.4 0.2 reduce_sum.12
  116.7 12.7 %all_to_all.34.parts_ref = bf16[4,16,2560]{2,1,0:T(8,128)(2,1)S(1)} all-to-all(bf16[4,16,2560]{2,1,0:T(8,128)(2,1)S(1)} %pad_maximum_fusion), channel_id=1, replica_groups={{0,32,64,96},{16,48,80,112},{128,160,192,224},{144,176,208,240},{256,28..., dimensions={0} | all-to-all | bytes 655360 | tf_op jit(solution)/shard_map/all_to_all | solution.py:458
  129.4 0.7 total.1
  130.1 10.1 %all_to_all.35.parts_ref = bf16[8,16,512]{2,1,0:T(8,128)(2,1)S(1)} all-to-all(bf16[8,16,512]{2,1,0:T(8,128)(2,1)S(1)} %get-tuple-element.40), channel_id=1, replica_groups={{0,16,128,144,256,272,384,400},{32,48,160,176,288,304,416,432},{64,80,1..., dimensions={0} | all-to-all | bytes 262144 | tf_op jit(solution)/shard_map/all_to_all | solution.py:458
  140.1 0.7 spread.1
  (5 shorter events, 0.1 us)
Async XLA Ops:
  31.5 41.9 %copy-start.3 = (f32[512]{0:T(512)S(1)}, f32[512]{0:T(512)}, u32[]{:S(2)}) copy-start(f32[512]{0:T(512)} %param.22) | copy-start | bytes 6148
  31.5 41.9 %copy-start.4 = (f32[32]{0:T(128)S(1)}, f32[32]{0:T(128)}, u32[]{:S(2)}) copy-start(f32[32]{0:T(128)} %param.23) | copy-start | bytes 388
  50.2 35.8 %copy-start = (bf16[1,256,1024]{2,1,0:T(8,128)(2,1)S(1)}, bf16[1,256,1024]{2,1,0:T(8,128)(2,1)}, u32[]{:S(2)}) copy-start(bf16[1,256,1024]{2,1,0:T(8,128)(2,1)} %param.12) | copy-start | bytes 1572868
  64.3 9.1 %collective-permute-start = (f32[144,128]{1,0:T(8,128)S(1)}, f32[144,128]{1,0:T(8,128)S(1)}, u32[]{:S(2)}, u32[]{:S(2)}) collective-permute-start(f32[144,128]{1,0:T(8,128)S(1)} %join.1.mine_ref), channel_id=1, source_target_pairs={{0,8},{1,9},{2,10},{3,11},{4,12},{5,13},{6,14},{7,15},{8,0},{9,1},... | collective-permute-start | bytes 221192 | tf_op jit(solution)/shard_map/ppermute | solution.py:558
  86.0 8.8 %copy-start.1 = (bf16[512,1024]{1,0:T(8,128)(2,1)S(1)}, bf16[512,1024]{1,0:T(8,128)(2,1)}, u32[]{:S(2)}) copy-start(bf16[512,1024]{1,0:T(8,128)(2,1)} %w_xdt_ref.1) | copy-start | bytes 3145732
  86.0 8.8 %copy-start.2 = (bf16[32,1024]{1,0:T(8,128)(2,1)S(1)}, bf16[32,1024]{1,0:T(8,128)(2,1)}, u32[]{:S(2)}) copy-start(bf16[32,1024]{1,0:T(8,128)(2,1)} %w_xbc_ref.1) | copy-start | bytes 196612
  86.7 10.4 %collective-permute-start.1 = (bf16[16,16,2176]{2,1,0:T(8,128)(2,1)S(1)}, bf16[16,16,2176]{2,1,0:T(8,128)(2,1)S(1)}, u32[]{:S(2)}, u32[]{:S(2)}) collective-permute-start(bf16[16,16,2176]{2,1,0:T(8,128)(2,1)S(1)} %get-tuple-element.33), channel_id=1, source_target_pairs={{0,16},{16,0},{32,48},{48,32},{64,80},{80,64},{96,112},{112,96},{1... | collective-permute-start | bytes 3342344 | tf_op jit(solution)/shard_map/ppermute | solution.py:517
